TPU v7x, 128 devices: a whole 4x4x4 slice. The times are simulated.
128 devices in a mesh: east: 8 (over x, core), north: 16 (over z, y).
Axes of the slice: x: 4, y: 4, z: 4, core: 2. Of those that a mesh axis runs over, the one named last changes fastest.
Arguments:
- heights: bfloat16 [524288, 128], P(('east', 'north')), may hold values from -6 to 6
- segment_ids: int32 [524288], P(('east', 'north')), may hold values from 0 to 1023
- tile_owner: int32 [524288, 1], P(('east', 'north')), may hold values from 0 to 127; in each aligned block of 4096 rows (0 to 4095, 4096 to 8191, ...) at most 64 rows name the same one
- gap_mask: int32 [2048, 8192], P('east', 'north'), may hold values from 0 to 1
- extinction: float32 [8], replicated, may hold values from 0.5 to 300
- sun_side: int32 [8], replicated, may hold values from 0 to 1
Outputs:
- filled_surface: float32 [2048, 8192], P('east', 'north')
- transmittance: float32 [8, 2048, 8192], P(None, 'east', 'north')
Inputs may be any that keep to these rules, and one draw needn't show every extreme that they name: `tile_owner`: the rows of one device name one tile at most 64 times, a bound that some block reaches.
All inputs are finite; a program needn't handle non-finite values.
Results may differ from a plain program's by a relative error of at most 0.0003.
Values may be sent and summed in bfloat16 or wider, within the bound.
No kernel may reach another device: no remote copies, remote signals or barrier semaphores. Data moves between devices by JAX's collectives and lax.ppermute only.
A program may use at most 64 MiB of HBM per device.

v0:
```python
import jax
import jax.numpy as jnp
from jax import lax
from jax.sharding import PartitionSpec as P

NS = 8
STEPS = 20


def padded_2(cells, sides, width):
    for axis, dim in sides:
        count = lax.axis_size(axis)
        ends = count - 1
        head = lax.slice_in_dim(cells, 0, width, axis=dim)
        tail = lax.slice_in_dim(cells, cells.shape[dim] - width, cells.shape[dim], axis=dim)
        cells = jnp.concatenate(
            [
                lax.ppermute(tail, axis, [(i, (i + 1) % count) for i in range(ends)]),
                cells,
                lax.ppermute(head, axis, [((i + 1) % count, i) for i in range(ends)]),
            ],
            axis=dim,
        )
    return cells


def entering(part, axis, combine, identity, reverse):
    count = lax.axis_size(axis)
    place = lax.axis_index(axis)
    ahead = count - 1 - place if reverse else place
    gathered = lax.all_gather(part, axis)
    state = jnp.zeros_like(part) + jnp.asarray(identity, part.dtype)

    def one(hop, state):
        source = count - 1 - hop if reverse else hop
        return combine(state, lax.dynamic_index_in_dim(gathered, source, 0, False))

    return lax.fori_loop(0, ahead, one, state)


def relax_once(padded, unknown):
    centre = padded[1:-1, 1:-1]
    beside_all = 0.25 * (
        padded[2:, 1:-1] + padded[:-2, 1:-1] + padded[1:-1, 2:] + padded[1:-1, :-2]
    )
    return centre + unknown * 0.9 * (beside_all - centre)


def side_triangle(north_side, length):
    lower = lax.broadcasted_iota(jnp.int32, (length, length), 0)
    upper = lax.broadcasted_iota(jnp.int32, (length, length), 1)
    return jnp.where(
        north_side[:, None, None], (lower > upper)[None], (lower < upper)[None]
    ).astype(jnp.float32)


def body(heights, segment_ids, tile_owner, gap_mask, extinction, sun_side):
    rows_here = heights.shape[0]
    tile_rows, tile_cols = gap_mask.shape
    n_east = lax.axis_size("east")
    n_north = lax.axis_size("north")
    devices = n_east * n_north
    capacity = 2 * rows_here // devices
    segments_tile = tile_rows * tile_cols // 128
    target = tile_owner[:, 0]
    hits = (target[:, None] == lax.broadcasted_iota(jnp.int32, (rows_here, devices), 1)).astype(
        jnp.int32
    )
    rank = jnp.sum(jnp.cumsum(hits, axis=0) * hits, axis=1) - 1
    slot = target * capacity + rank
    send_heights = jnp.zeros((devices * capacity, 128), jnp.bfloat16).at[slot].set(heights)
    send_segments = jnp.full((devices * capacity,), -1, jnp.int32).at[slot].set(segment_ids)
    got_heights, got_segments = (
        lax.all_to_all(
            send_heights.reshape(devices, capacity, 128),
            ("east", "north"),
            split_axis=0,
            concat_axis=0,
            tiled=True,
        ),
        lax.all_to_all(
            send_segments.reshape(devices, capacity),
            ("east", "north"),
            split_axis=0,
            concat_axis=0,
            tiled=True,
        ),
    )
    got_heights = got_heights.reshape(devices * capacity, 128)
    got_segments = got_segments.reshape(devices * capacity)
    received = devices * capacity
    block = min(received, 2048)
    block_count = received // block

    def add_block(index, carry):
        summed, counted = carry
        part_heights = lax.dynamic_slice_in_dim(got_heights, index * block, block, 0)
        part_segments = lax.dynamic_slice_in_dim(got_segments, index * block, block, 0)
        onehot = part_segments[:, None] == lax.broadcasted_iota(
            jnp.int32, (block, segments_tile), 1
        )
        summed = summed + lax.dot_general(
            onehot.astype(jnp.bfloat16),
            part_heights,
            (((0,), (0,)), ((), ())),
            preferred_element_type=jnp.float32,
        )
        counted = counted + jnp.sum(onehot.astype(jnp.float32), axis=0)
        return (summed, counted)

    summed, counted = lax.fori_loop(
        0,
        block_count,
        add_block,
        (jnp.zeros((segments_tile, 128), jnp.float32), jnp.zeros((segments_tile,), jnp.float32)),
    )
    summed = summed.reshape(tile_rows, tile_cols)
    counted = jnp.broadcast_to(counted[:, None], (segments_tile, 128)).reshape(tile_rows, tile_cols)
    unknown = jnp.where((gap_mask == 1) | (counted == 0.0), 1.0, 0.0).astype(jnp.float32)
    surface = jnp.where(unknown > 0.0, 0.0, summed / jnp.maximum(counted, 1.0))
    for repeat_index in range(STEPS):
        padded = padded_2(surface, (("east", 0), ("north", 1)), 1)
        surface = relax_once(padded, unknown)
    total_cols = tile_cols * n_north
    col_blocks = tile_cols // 128
    north_side = sun_side == 1
    optical = (extinction / total_cols)[:, None, None] * jax.nn.softplus(surface)[None]
    optical_blocks = optical.reshape(NS, tile_rows, col_blocks, 128)
    inside = jnp.einsum(
        "sxbk,skj->sxbj",
        optical_blocks,
        side_triangle(north_side, 128),
        precision=lax.Precision.HIGHEST,
        preferred_element_type=jnp.float32,
    )
    block_sums = jnp.sum(optical_blocks, axis=3)
    carried = jnp.einsum(
        "sxk,skj->sxj",
        block_sums,
        side_triangle(north_side, col_blocks),
        precision=lax.Precision.HIGHEST,
        preferred_element_type=jnp.float32,
    )
    tile_totals = jnp.sum(block_sums, axis=2)

    def add_depths(earlier, later):
        return earlier + later

    before_south = entering(tile_totals, "north", add_depths, jnp.zeros_like(tile_totals), False)
    before_north = entering(tile_totals, "north", add_depths, jnp.zeros_like(tile_totals), True)
    before = jnp.where(north_side[:, None], before_north, before_south)
    exposure = inside + carried[:, :, :, None] + before[:, :, None, None]
    exposure = exposure.reshape(NS, tile_rows, tile_cols)
    return (surface, jnp.exp(-exposure))


def solution(mesh):
    return jax.shard_map(
        body,
        mesh=mesh,
        in_specs=(
            P(("east", "north"), None),
            P(("east", "north")),
            P(("east", "north"), None),
            P("east", "north"),
            P(),
            P(),
        ),
        out_specs=(P("east", "north"), P(None, "east", "north")),
        check_vma=False,
    )
```

profile of v0, /device:TPU:2, one launch (start us, length us, event | category | flops | bytes accessed | tf_op | source)
XLA Modules:
  0.0 510.3 jit_solution(5081610469889967008)
XLA Ops:
  5.1 15.7 %scatter_custom_fusion = s32[8192]{0:T(1024)S(1)} fusion(s32[4096]{0:T(1024)S(1)} %bitcast.57, s32[4096]{0:T(1024)} %param.13, s32[]{:T(128)} %constant.102.clone.1), kind=kCustom, calls=%fused_computation.406 | custom fusion | bytes 33280 | tf_op jit(solution)/shard_map/scatter | solution.py:72
  21.5 10.5 %all-to-all-start = ((s32[128,1,64]{2,1,0:T(1,128)}), s32[128,1,64]{2,1,0:T(1,128)S(1)}, u32[]{:S(2)}, u32[]{:S(2)}) async-start(s32[128,1,64]{2,1,0:T(1,128)} %bitcast.9), calls=%async_computation | async-start | bytes 131072 | tf_op jit(solution)/shard_map/all_to_all | solution.py:81
  32.1 12.8 %scatter_custom_fusion.1 = bf16[8192,128]{1,0:T(8,128)(2,1)} fusion(s32[4096]{0:T(1024)S(1)} %bitcast.58, bf16[4096,128]{1,0:T(8,128)(2,1)} %param.12, bf16[]{:T(256)} %constant.100.clone.1), kind=kCustom, calls=%fused_computation.26 | custom fusion | bytes 2097664 | tf_op jit(solution)/shard_map/scatter | solution.py:71
  44.8 9.8 %all-to-all-start.1 = ((bf16[128,64,128]{2,1,0:T(8,128)(2,1)}), bf16[128,64,128]{2,1,0:T(8,128)(2,1)S(1)}, u32[]{:S(2)}, u32[]{:S(2)}) async-start(bf16[128,64,128]{2,1,0:T(8,128)(2,1)} %bitcast.10), calls=%async_computation.1 | async-start | bytes 4194304 | tf_op jit(solution)/shard_map/all_to_all | solution.py:74
  56.0 28.3 %all-to-all-done.1 = bf16[128,64,128]{2,1,0:T(8,128)(2,1)S(1)} async-done(((bf16[128,64,128]{2,1,0:T(8,128)(2,1)}), bf16[128,64,128]{2,1,0:T(8,128)(2,1)S(1)}, u32[]{:S(2)}, u32[]{:S(2)}) %all-to-all-start.1) | async-done | bytes 2097184 | tf_op jit(solution)/shard_map/all_to_all | solution.py:74
  84.3 15.3 %while.40 = (s32[]{:T(128)}, f32[1024,128]{1,0:T(8,128)S(1)}, f32[1024]{0:T(1024)S(1)}, s32[8192]{0:T(1024)S(1)}, bf16[8192,128]{1,0:T(8,128)(2,1)S(1)}, /*index=5*/s32[]{:T(128)}, s32[]{:T(128)}, s32[]{:T(128)}, s32[]{:T(128)}) while((s32[]{:T(128)}, f32[1024,128]{1,0:T(8,128)S(1)}, f32[1024]{0:T(1024)S(1)}, s32[8192]{0:T(1024)S(1)}, ...), condition=%wide.region_7.8_spmd.clone, body=%wide.region_5.0_spmd.clone.sunk | while | flops 545522688 | bytes 1622182 | solution.py:111
  102.9 3.6 collective-permute-start
  109.2 4.6 collective-permute-start.3
  119.2 3.6 collective-permute-start.4
  125.5 5.0 collective-permute-start.7
  136.4 3.6 collective-permute-start.8
  142.8 5.0 collective-permute-start.11
  153.8 3.6 collective-permute-start.12
  160.1 5.0 collective-permute-start.15
  170.9 3.6 collective-permute-start.16
  177.2 5.0 collective-permute-start.19
  187.2 3.6 collective-permute-start.20
  193.6 7.0 %collective-permute-start.23 = (f32[258,1]{1,0:T(8,128)S(1)}, f32[258,1]{1,0:T(8,128)S(1)}, u32[]{:S(2)}, u32[]{:S(2)}) collective-permute-start(f32[258,1]{1,0:T(8,128)S(1)} %get-tuple-element.267), channel_id=1, source_target_pairs={{0,1},{1,2},{2,3},{3,4},{4,5},{5,6},{6,7},{7,8},{8,9},{9,10},{10,1... | collective-permute-start | bytes 3104 | tf_op jit(solution)/shard_map/ppermute | solution.py:18
  205.5 3.6 collective-permute-start.24
  211.9 7.1 %collective-permute-start.27 = (f32[258,1]{1,0:T(8,128)S(1)}, f32[258,1]{1,0:T(8,128)S(1)}, u32[]{:S(2)}, u32[]{:S(2)}) collective-permute-start(f32[258,1]{1,0:T(8,128)S(1)} %get-tuple-element.265), channel_id=1, source_target_pairs={{0,1},{1,2},{2,3},{3,4},{4,5},{5,6},{6,7},{7,8},{8,9},{9,10},{10,1... | collective-permute-start | bytes 3104 | tf_op jit(solution)/shard_map/ppermute | solution.py:18
  224.0 3.6 collective-permute-start.28
  230.3 7.1 %collective-permute-start.31 = (f32[258,1]{1,0:T(8,128)S(1)}, f32[258,1]{1,0:T(8,128)S(1)}, u32[]{:S(2)}, u32[]{:S(2)}) collective-permute-start(f32[258,1]{1,0:T(8,128)S(1)} %get-tuple-element.263), channel_id=1, source_target_pairs={{0,1},{1,2},{2,3},{3,4},{4,5},{5,6},{6,7},{7,8},{8,9},{9,10},{10,1... | collective-permute-start | bytes 3104 | tf_op jit(solution)/shard_map/ppermute | solution.py:18
  242.4 3.6 collective-permute-start.32
  248.8 7.1 %collective-permute-start.35 = (f32[258,1]{1,0:T(8,128)S(1)}, f32[258,1]{1,0:T(8,128)S(1)}, u32[]{:S(2)}, u32[]{:S(2)}) collective-permute-start(f32[258,1]{1,0:T(8,128)S(1)} %get-tuple-element.261), channel_id=1, source_target_pairs={{0,1},{1,2},{2,3},{3,4},{4,5},{5,6},{6,7},{7,8},{8,9},{9,10},{10,1... | collective-permute-start | bytes 3104 | tf_op jit(solution)/shard_map/ppermute | solution.py:18
  260.8 3.9 collective-permute-start.36
  267.2 7.1 %collective-permute-start.39 = (f32[258,1]{1,0:T(8,128)S(1)}, f32[258,1]{1,0:T(8,128)S(1)}, u32[]{:S(2)}, u32[]{:S(2)}) collective-permute-start(f32[258,1]{1,0:T(8,128)S(1)} %get-tuple-element.259), channel_id=1, source_target_pairs={{0,1},{1,2},{2,3},{3,4},{4,5},{5,6},{6,7},{7,8},{8,9},{9,10},{10,1... | collective-permute-start | bytes 3104 | tf_op jit(solution)/shard_map/ppermute | solution.py:18
  279.2 3.6 collective-permute-start.40
  285.6 7.1 %collective-permute-start.43 = (f32[258,1]{1,0:T(8,128)S(1)}, f32[258,1]{1,0:T(8,128)S(1)}, u32[]{:S(2)}, u32[]{:S(2)}) collective-permute-start(f32[258,1]{1,0:T(8,128)S(1)} %get-tuple-element.257), channel_id=1, source_target_pairs={{0,1},{1,2},{2,3},{3,4},{4,5},{5,6},{6,7},{7,8},{8,9},{9,10},{10,1... | collective-permute-start | bytes 3104 | tf_op jit(solution)/shard_map/ppermute | solution.py:18
  297.6 3.6 collective-permute-start.44
  304.0 7.1 %collective-permute-start.47 = (f32[258,1]{1,0:T(8,128)S(1)}, f32[258,1]{1,0:T(8,128)S(1)}, u32[]{:S(2)}, u32[]{:S(2)}) collective-permute-start(f32[258,1]{1,0:T(8,128)S(1)} %get-tuple-element.255), channel_id=1, source_target_pairs={{0,1},{1,2},{2,3},{3,4},{4,5},{5,6},{6,7},{7,8},{8,9},{9,10},{10,1... | collective-permute-start | bytes 3104 | tf_op jit(solution)/shard_map/ppermute | solution.py:18
  316.0 3.6 collective-permute-start.48
  322.4 7.1 %collective-permute-start.51 = (f32[258,1]{1,0:T(8,128)S(1)}, f32[258,1]{1,0:T(8,128)S(1)}, u32[]{:S(2)}, u32[]{:S(2)}) collective-permute-start(f32[258,1]{1,0:T(8,128)S(1)} %get-tuple-element.253), channel_id=1, source_target_pairs={{0,1},{1,2},{2,3},{3,4},{4,5},{5,6},{6,7},{7,8},{8,9},{9,10},{10,1... | collective-permute-start | bytes 3104 | tf_op jit(solution)/shard_map/ppermute | solution.py:18
  334.4 3.6 collective-permute-start.52
  340.8 7.1 %collective-permute-start.55 = (f32[258,1]{1,0:T(8,128)S(1)}, f32[258,1]{1,0:T(8,128)S(1)}, u32[]{:S(2)}, u32[]{:S(2)}) collective-permute-start(f32[258,1]{1,0:T(8,128)S(1)} %get-tuple-element.251), channel_id=1, source_target_pairs={{0,1},{1,2},{2,3},{3,4},{4,5},{5,6},{6,7},{7,8},{8,9},{9,10},{10,1... | collective-permute-start | bytes 3104 | tf_op jit(solution)/shard_map/ppermute | solution.py:18
  352.8 3.6 collective-permute-start.56
  359.2 7.1 %collective-permute-start.59 = (f32[258,1]{1,0:T(8,128)S(1)}, f32[258,1]{1,0:T(8,128)S(1)}, u32[]{:S(2)}, u32[]{:S(2)}) collective-permute-start(f32[258,1]{1,0:T(8,128)S(1)} %get-tuple-element.249), channel_id=1, source_target_pairs={{0,1},{1,2},{2,3},{3,4},{4,5},{5,6},{6,7},{7,8},{8,9},{9,10},{10,1... | collective-permute-start | bytes 3104 | tf_op jit(solution)/shard_map/ppermute | solution.py:18
  371.2 3.6 collective-permute-start.60
  377.6 7.1 %collective-permute-start.63 = (f32[258,1]{1,0:T(8,128)S(1)}, f32[258,1]{1,0:T(8,128)S(1)}, u32[]{:S(2)}, u32[]{:S(2)}) collective-permute-start(f32[258,1]{1,0:T(8,128)S(1)} %get-tuple-element.247), channel_id=1, source_target_pairs={{0,1},{1,2},{2,3},{3,4},{4,5},{5,6},{6,7},{7,8},{8,9},{9,10},{10,1... | collective-permute-start | bytes 3104 | tf_op jit(solution)/shard_map/ppermute | solution.py:18
  389.7 3.6 collective-permute-start.64
  396.0 7.1 %collective-permute-start.67 = (f32[258,1]{1,0:T(8,128)S(1)}, f32[258,1]{1,0:T(8,128)S(1)}, u32[]{:S(2)}, u32[]{:S(2)}) collective-permute-start(f32[258,1]{1,0:T(8,128)S(1)} %get-tuple-element.245), channel_id=1, source_target_pairs={{0,1},{1,2},{2,3},{3,4},{4,5},{5,6},{6,7},{7,8},{8,9},{9,10},{10,1... | collective-permute-start | bytes 3104 | tf_op jit(solution)/shard_map/ppermute | solution.py:18
  408.1 3.6 collective-permute-start.68
  414.4 7.1 %collective-permute-start.71 = (f32[258,1]{1,0:T(8,128)S(1)}, f32[258,1]{1,0:T(8,128)S(1)}, u32[]{:S(2)}, u32[]{:S(2)}) collective-permute-start(f32[258,1]{1,0:T(8,128)S(1)} %get-tuple-element.243), channel_id=1, source_target_pairs={{0,1},{1,2},{2,3},{3,4},{4,5},{5,6},{6,7},{7,8},{8,9},{9,10},{10,1... | collective-permute-start | bytes 3104 | tf_op jit(solution)/shard_map/ppermute | solution.py:18
  426.5 3.6 collective-permute-start.72
  432.8 7.1 %collective-permute-start.75 = (f32[258,1]{1,0:T(8,128)S(1)}, f32[258,1]{1,0:T(8,128)S(1)}, u32[]{:S(2)}, u32[]{:S(2)}) collective-permute-start(f32[258,1]{1,0:T(8,128)S(1)} %get-tuple-element.241), channel_id=1, source_target_pairs={{0,1},{1,2},{2,3},{3,4},{4,5},{5,6},{6,7},{7,8},{8,9},{9,10},{10,1... | collective-permute-start | bytes 3104 | tf_op jit(solution)/shard_map/ppermute | solution.py:18
  451.2 7.1 %collective-permute-start.79 = (f32[258,1]{1,0:T(8,128)S(1)}, f32[258,1]{1,0:T(8,128)S(1)}, u32[]{:S(2)}, u32[]{:S(2)}) collective-permute-start(f32[258,1]{1,0:T(8,128)S(1)} %get-tuple-element.239), channel_id=1, source_target_pairs={{0,1},{1,2},{2,3},{3,4},{4,5},{5,6},{6,7},{7,8},{8,9},{9,10},{10,1... | collective-permute-start | bytes 3104 | tf_op jit(solution)/shard_map/ppermute | solution.py:18
  463.9 34.7 %all-gather = f32[128,256]{1,0:T(8,128)S(1)} all-gather(f32[8,256]{1,0:T(8,128)S(1)} %get-tuple-element.207), channel_id=2, replica_groups=mesh['east'=8,'north'=16] {'north'}, dimensions={0}, use_global_device_ids=true | all-gather | bytes 139264 | tf_op jit(solution)/shard_map/all_gather | solution.py:31
  499.7 5.2 %negate_exponential_fusion = f32[8,256,4,128]{1,3,2,0:T(8,128)} fusion(f32[8,256]{1,0:T(8,128)S(1)} %broadcast_select_fusion, f32[8,256,4]{1,2,0:T(4,128)S(1)} %fusion.166, f32[256,4,128]{2,0,1:T(8,128)S(1)} %bitcast.49, f32[8]{0:T(128)S(1)} %broadcast_multiply_fusion, pred[128,128]{0,1:T(8,128)(4,1)S(1)} %get-tuple-element.320, ...), kind=kOutput, calls=%fused_computation.16 | convolution fusion | flops 1614938112 | bytes 4792360 | tf_op jit(solution)/shard_map/sxbk,skj->sxbj/dot_general | solution.py:129
  505.0 5.3 %copy.24 = f32[8,256,512]{2,1,0:T(8,128)} copy(f32[8,256,512]{1,2,0:T(8,128)} %bitcast.47) | data formatting | bytes 8388608
  (257 shorter events, 185.1 us)
Async XLA Ops:
  21.5 23.3 %all-to-all-start = ((s32[128,1,64]{2,1,0:T(1,128)}), s32[128,1,64]{2,1,0:T(1,128)S(1)}, u32[]{:S(2)}, u32[]{:S(2)}) async-start(s32[128,1,64]{2,1,0:T(1,128)} %bitcast.9), calls=%async_computation | async-start | bytes 131072 | tf_op jit(solution)/shard_map/all_to_all | solution.py:81
  44.8 39.4 %all-to-all-start.1 = ((bf16[128,64,128]{2,1,0:T(8,128)(2,1)}), bf16[128,64,128]{2,1,0:T(8,128)(2,1)S(1)}, u32[]{:S(2)}, u32[]{:S(2)}) async-start(bf16[128,64,128]{2,1,0:T(8,128)(2,1)} %bitcast.10), calls=%async_computation.1 | async-start | bytes 4194304 | tf_op jit(solution)/shard_map/all_to_all | solution.py:74
  101.0 5.6 %collective-permute-start.1 = (f32[1,512]{1,0:T(1,128)S(1)}, f32[1,512]{1,0:T(1,128)S(1)}, u32[]{:S(2)}, u32[]{:S(2)}) collective-permute-start(f32[1,512]{1,0:T(1,128)S(1)} %get-tuple-element.316), channel_id=1, source_target_pairs={{0,16},{16,32},{32,48},{48,64},{64,80},{80,96},{96,112},{1,17},{17... | collective-permute-start | bytes 6152 | tf_op jit(solution)/shard_map/ppermute | solution.py:18
  107.9 7.6 %collective-permute-start.2 = (f32[258,1]{1,0:T(8,128)S(1)}, f32[258,1]{1,0:T(8,128)S(1)}, u32[]{:S(2)}, u32[]{:S(2)}) collective-permute-start(f32[258,1]{1,0:T(8,128)S(1)} %get-tuple-element.276), channel_id=1, source_target_pairs={{1,0},{2,1},{3,2},{4,3},{5,4},{6,5},{7,6},{8,7},{9,8},{10,9},{11,1... | collective-permute-start | bytes 3104 | tf_op jit(solution)/shard_map/ppermute | solution.py:20
  109.2 7.5 %collective-permute-start.3 = (f32[258,1]{1,0:T(8,128)S(1)}, f32[258,1]{1,0:T(8,128)S(1)}, u32[]{:S(2)}, u32[]{:S(2)}) collective-permute-start(f32[258,1]{1,0:T(8,128)S(1)} %get-tuple-element.277), channel_id=1, source_target_pairs={{0,1},{1,2},{2,3},{3,4},{4,5},{5,6},{6,7},{7,8},{8,9},{9,10},{10,1... | collective-permute-start | bytes 3104 | tf_op jit(solution)/shard_map/ppermute | solution.py:18
  124.2 8.6 %collective-permute-start.6 = (f32[258,1]{1,0:T(8,128)S(1)}, f32[258,1]{1,0:T(8,128)S(1)}, u32[]{:S(2)}, u32[]{:S(2)}) collective-permute-start(f32[258,1]{1,0:T(8,128)S(1)} %get-tuple-element.274), channel_id=1, source_target_pairs={{1,0},{2,1},{3,2},{4,3},{5,4},{6,5},{7,6},{8,7},{9,8},{10,9},{11,1... | collective-permute-start | bytes 3104 | tf_op jit(solution)/shard_map/ppermute | solution.py:20
  125.5 8.5 %collective-permute-start.7 = (f32[258,1]{1,0:T(8,128)S(1)}, f32[258,1]{1,0:T(8,128)S(1)}, u32[]{:S(2)}, u32[]{:S(2)}) collective-permute-start(f32[258,1]{1,0:T(8,128)S(1)} %get-tuple-element.275), channel_id=1, source_target_pairs={{0,1},{1,2},{2,3},{3,4},{4,5},{5,6},{6,7},{7,8},{8,9},{9,10},{10,1... | collective-permute-start | bytes 3104 | tf_op jit(solution)/shard_map/ppermute | solution.py:18
  134.5 5.6 %collective-permute-start.9 = (f32[1,512]{1,0:T(1,128)S(1)}, f32[1,512]{1,0:T(1,128)S(1)}, u32[]{:S(2)}, u32[]{:S(2)}) collective-permute-start(f32[1,512]{1,0:T(1,128)S(1)} %get-tuple-element.312), channel_id=1, source_target_pairs={{0,16},{16,32},{32,48},{48,64},{64,80},{80,96},{96,112},{1,17},{17... | collective-permute-start | bytes 6152 | tf_op jit(solution)/shard_map/ppermute | solution.py:18
  141.5 8.7 %collective-permute-start.10 = (f32[258,1]{1,0:T(8,128)S(1)}, f32[258,1]{1,0:T(8,128)S(1)}, u32[]{:S(2)}, u32[]{:S(2)}) collective-permute-start(f32[258,1]{1,0:T(8,128)S(1)} %get-tuple-element.272), channel_id=1, source_target_pairs={{1,0},{2,1},{3,2},{4,3},{5,4},{6,5},{7,6},{8,7},{9,8},{10,9},{11,1... | collective-permute-start | bytes 3104 | tf_op jit(solution)/shard_map/ppermute | solution.py:20
  142.8 8.6 %collective-permute-start.11 = (f32[258,1]{1,0:T(8,128)S(1)}, f32[258,1]{1,0:T(8,128)S(1)}, u32[]{:S(2)}, u32[]{:S(2)}) collective-permute-start(f32[258,1]{1,0:T(8,128)S(1)} %get-tuple-element.273), channel_id=1, source_target_pairs={{0,1},{1,2},{2,3},{3,4},{4,5},{5,6},{6,7},{7,8},{8,9},{9,10},{10,1... | collective-permute-start | bytes 3104 | tf_op jit(solution)/shard_map/ppermute | solution.py:18
  158.8 8.4 %collective-permute-start.14 = (f32[258,1]{1,0:T(8,128)S(1)}, f32[258,1]{1,0:T(8,128)S(1)}, u32[]{:S(2)}, u32[]{:S(2)}) collective-permute-start(f32[258,1]{1,0:T(8,128)S(1)} %get-tuple-element.270), channel_id=1, source_target_pairs={{1,0},{2,1},{3,2},{4,3},{5,4},{6,5},{7,6},{8,7},{9,8},{10,9},{11,1... | collective-permute-start | bytes 3104 | tf_op jit(solution)/shard_map/ppermute | solution.py:20
  160.1 8.3 %collective-permute-start.15 = (f32[258,1]{1,0:T(8,128)S(1)}, f32[258,1]{1,0:T(8,128)S(1)}, u32[]{:S(2)}, u32[]{:S(2)}) collective-permute-start(f32[258,1]{1,0:T(8,128)S(1)} %get-tuple-element.271), channel_id=1, source_target_pairs={{0,1},{1,2},{2,3},{3,4},{4,5},{5,6},{6,7},{7,8},{8,9},{9,10},{10,1... | collective-permute-start | bytes 3104 | tf_op jit(solution)/shard_map/ppermute | solution.py:18
  175.9 7.7 %collective-permute-start.18 = (f32[258,1]{1,0:T(8,128)S(1)}, f32[258,1]{1,0:T(8,128)S(1)}, u32[]{:S(2)}, u32[]{:S(2)}) collective-permute-start(f32[258,1]{1,0:T(8,128)S(1)} %get-tuple-element.268), channel_id=1, source_target_pairs={{1,0},{2,1},{3,2},{4,3},{5,4},{6,5},{7,6},{8,7},{9,8},{10,9},{11,1... | collective-permute-start | bytes 3104 | tf_op jit(solution)/shard_map/ppermute | solution.py:20
  177.2 7.6 %collective-permute-start.19 = (f32[258,1]{1,0:T(8,128)S(1)}, f32[258,1]{1,0:T(8,128)S(1)}, u32[]{:S(2)}, u32[]{:S(2)}) collective-permute-start(f32[258,1]{1,0:T(8,128)S(1)} %get-tuple-element.269), channel_id=1, source_target_pairs={{0,1},{1,2},{2,3},{3,4},{4,5},{5,6},{6,7},{7,8},{8,9},{9,10},{10,1... | collective-permute-start | bytes 3104 | tf_op jit(solution)/shard_map/ppermute | solution.py:18
  192.3 9.7 %collective-permute-start.22 = (f32[258,1]{1,0:T(8,128)S(1)}, f32[258,1]{1,0:T(8,128)S(1)}, u32[]{:S(2)}, u32[]{:S(2)}) collective-permute-start(f32[258,1]{1,0:T(8,128)S(1)} %get-tuple-element.266), channel_id=1, source_target_pairs={{1,0},{2,1},{3,2},{4,3},{5,4},{6,5},{7,6},{8,7},{9,8},{10,9},{11,1... | collective-permute-start | bytes 3104 | tf_op jit(solution)/shard_map/ppermute | solution.py:20
  193.6 9.6 %collective-permute-start.23 = (f32[258,1]{1,0:T(8,128)S(1)}, f32[258,1]{1,0:T(8,128)S(1)}, u32[]{:S(2)}, u32[]{:S(2)}) collective-permute-start(f32[258,1]{1,0:T(8,128)S(1)} %get-tuple-element.267), channel_id=1, source_target_pairs={{0,1},{1,2},{2,3},{3,4},{4,5},{5,6},{6,7},{7,8},{8,9},{9,10},{10,1... | collective-permute-start | bytes 3104 | tf_op jit(solution)/shard_map/ppermute | solution.py:18
  210.6 9.8 %collective-permute-start.26 = (f32[258,1]{1,0:T(8,128)S(1)}, f32[258,1]{1,0:T(8,128)S(1)}, u32[]{:S(2)}, u32[]{:S(2)}) collective-permute-start(f32[258,1]{1,0:T(8,128)S(1)} %get-tuple-element.264), channel_id=1, source_target_pairs={{1,0},{2,1},{3,2},{4,3},{5,4},{6,5},{7,6},{8,7},{9,8},{10,9},{11,1... | collective-permute-start | bytes 3104 | tf_op jit(solution)/shard_map/ppermute | solution.py:20
  211.9 9.7 %collective-permute-start.27 = (f32[258,1]{1,0:T(8,128)S(1)}, f32[258,1]{1,0:T(8,128)S(1)}, u32[]{:S(2)}, u32[]{:S(2)}) collective-permute-start(f32[258,1]{1,0:T(8,128)S(1)} %get-tuple-element.265), channel_id=1, source_target_pairs={{0,1},{1,2},{2,3},{3,4},{4,5},{5,6},{6,7},{7,8},{8,9},{9,10},{10,1... | collective-permute-start | bytes 3104 | tf_op jit(solution)/shard_map/ppermute | solution.py:18
  229.0 9.8 %collective-permute-start.30 = (f32[258,1]{1,0:T(8,128)S(1)}, f32[258,1]{1,0:T(8,128)S(1)}, u32[]{:S(2)}, u32[]{:S(2)}) collective-permute-start(f32[258,1]{1,0:T(8,128)S(1)} %get-tuple-element.262), channel_id=1, source_target_pairs={{1,0},{2,1},{3,2},{4,3},{5,4},{6,5},{7,6},{8,7},{9,8},{10,9},{11,1... | collective-permute-start | bytes 3104 | tf_op jit(solution)/shard_map/ppermute | solution.py:20
  230.3 9.7 %collective-permute-start.31 = (f32[258,1]{1,0:T(8,128)S(1)}, f32[258,1]{1,0:T(8,128)S(1)}, u32[]{:S(2)}, u32[]{:S(2)}) collective-permute-start(f32[258,1]{1,0:T(8,128)S(1)} %get-tuple-element.263), channel_id=1, source_target_pairs={{0,1},{1,2},{2,3},{3,4},{4,5},{5,6},{6,7},{7,8},{8,9},{9,10},{10,1... | collective-permute-start | bytes 3104 | tf_op jit(solution)/shard_map/ppermute | solution.py:18
  247.5 9.7 %collective-permute-start.34 = (f32[258,1]{1,0:T(8,128)S(1)}, f32[258,1]{1,0:T(8,128)S(1)}, u32[]{:S(2)}, u32[]{:S(2)}) collective-permute-start(f32[258,1]{1,0:T(8,128)S(1)} %get-tuple-element.260), channel_id=1, source_target_pairs={{1,0},{2,1},{3,2},{4,3},{5,4},{6,5},{7,6},{8,7},{9,8},{10,9},{11,1... | collective-permute-start | bytes 3104 | tf_op jit(solution)/shard_map/ppermute | solution.py:20
  248.8 9.6 %collective-permute-start.35 = (f32[258,1]{1,0:T(8,128)S(1)}, f32[258,1]{1,0:T(8,128)S(1)}, u32[]{:S(2)}, u32[]{:S(2)}) collective-permute-start(f32[258,1]{1,0:T(8,128)S(1)} %get-tuple-element.261), channel_id=1, source_target_pairs={{0,1},{1,2},{2,3},{3,4},{4,5},{5,6},{6,7},{7,8},{8,9},{9,10},{10,1... | collective-permute-start | bytes 3104 | tf_op jit(solution)/shard_map/ppermute | solution.py:18
  258.9 5.8 %collective-permute-start.37 = (f32[1,512]{1,0:T(1,128)S(1)}, f32[1,512]{1,0:T(1,128)S(1)}, u32[]{:S(2)}, u32[]{:S(2)}) collective-permute-start(f32[1,512]{1,0:T(1,128)S(1)} %get-tuple-element.298), channel_id=1, source_target_pairs={{0,16},{16,32},{32,48},{48,64},{64,80},{80,96},{96,112},{1,17},{17... | collective-permute-start | bytes 6152 | tf_op jit(solution)/shard_map/ppermute | solution.py:18
  265.9 9.7 %collective-permute-start.38 = (f32[258,1]{1,0:T(8,128)S(1)}, f32[258,1]{1,0:T(8,128)S(1)}, u32[]{:S(2)}, u32[]{:S(2)}) collective-permute-start(f32[258,1]{1,0:T(8,128)S(1)} %get-tuple-element.258), channel_id=1, source_target_pairs={{1,0},{2,1},{3,2},{4,3},{5,4},{6,5},{7,6},{8,7},{9,8},{10,9},{11,1... | collective-permute-start | bytes 3104 | tf_op jit(solution)/shard_map/ppermute | solution.py:20
  267.2 9.6 %collective-permute-start.39 = (f32[258,1]{1,0:T(8,128)S(1)}, f32[258,1]{1,0:T(8,128)S(1)}, u32[]{:S(2)}, u32[]{:S(2)}) collective-permute-start(f32[258,1]{1,0:T(8,128)S(1)} %get-tuple-element.259), channel_id=1, source_target_pairs={{0,1},{1,2},{2,3},{3,4},{4,5},{5,6},{6,7},{7,8},{8,9},{9,10},{10,1... | collective-permute-start | bytes 3104 | tf_op jit(solution)/shard_map/ppermute | solution.py:18
  284.3 9.7 %collective-permute-start.42 = (f32[258,1]{1,0:T(8,128)S(1)}, f32[258,1]{1,0:T(8,128)S(1)}, u32[]{:S(2)}, u32[]{:S(2)}) collective-permute-start(f32[258,1]{1,0:T(8,128)S(1)} %get-tuple-element.256), channel_id=1, source_target_pairs={{1,0},{2,1},{3,2},{4,3},{5,4},{6,5},{7,6},{8,7},{9,8},{10,9},{11,1... | collective-permute-start | bytes 3104 | tf_op jit(solution)/shard_map/ppermute | solution.py:20
  285.6 9.6 %collective-permute-start.43 = (f32[258,1]{1,0:T(8,128)S(1)}, f32[258,1]{1,0:T(8,128)S(1)}, u32[]{:S(2)}, u32[]{:S(2)}) collective-permute-start(f32[258,1]{1,0:T(8,128)S(1)} %get-tuple-element.257), channel_id=1, source_target_pairs={{0,1},{1,2},{2,3},{3,4},{4,5},{5,6},{6,7},{7,8},{8,9},{9,10},{10,1... | collective-permute-start | bytes 3104 | tf_op jit(solution)/shard_map/ppermute | solution.py:18
  302.7 9.7 %collective-permute-start.46 = (f32[258,1]{1,0:T(8,128)S(1)}, f32[258,1]{1,0:T(8,128)S(1)}, u32[]{:S(2)}, u32[]{:S(2)}) collective-permute-start(f32[258,1]{1,0:T(8,128)S(1)} %get-tuple-element.254), channel_id=1, source_target_pairs={{1,0},{2,1},{3,2},{4,3},{5,4},{6,5},{7,6},{8,7},{9,8},{10,9},{11,1... | collective-permute-start | bytes 3104 | tf_op jit(solution)/shard_map/ppermute | solution.py:20
  304.0 9.6 %collective-permute-start.47 = (f32[258,1]{1,0:T(8,128)S(1)}, f32[258,1]{1,0:T(8,128)S(1)}, u32[]{:S(2)}, u32[]{:S(2)}) collective-permute-start(f32[258,1]{1,0:T(8,128)S(1)} %get-tuple-element.255), channel_id=1, source_target_pairs={{0,1},{1,2},{2,3},{3,4},{4,5},{5,6},{6,7},{7,8},{8,9},{9,10},{10,1... | collective-permute-start | bytes 3104 | tf_op jit(solution)/shard_map/ppermute | solution.py:18
  321.1 9.7 %collective-permute-start.50 = (f32[258,1]{1,0:T(8,128)S(1)}, f32[258,1]{1,0:T(8,128)S(1)}, u32[]{:S(2)}, u32[]{:S(2)}) collective-permute-start(f32[258,1]{1,0:T(8,128)S(1)} %get-tuple-element.252), channel_id=1, source_target_pairs={{1,0},{2,1},{3,2},{4,3},{5,4},{6,5},{7,6},{8,7},{9,8},{10,9},{11,1... | collective-permute-start | bytes 3104 | tf_op jit(solution)/shard_map/ppermute | solution.py:20
  322.4 9.6 %collective-permute-start.51 = (f32[258,1]{1,0:T(8,128)S(1)}, f32[258,1]{1,0:T(8,128)S(1)}, u32[]{:S(2)}, u32[]{:S(2)}) collective-permute-start(f32[258,1]{1,0:T(8,128)S(1)} %get-tuple-element.253), channel_id=1, source_target_pairs={{0,1},{1,2},{2,3},{3,4},{4,5},{5,6},{6,7},{7,8},{8,9},{9,10},{10,1... | collective-permute-start | bytes 3104 | tf_op jit(solution)/shard_map/ppermute | solution.py:18
  339.5 9.7 %collective-permute-start.54 = (f32[258,1]{1,0:T(8,128)S(1)}, f32[258,1]{1,0:T(8,128)S(1)}, u32[]{:S(2)}, u32[]{:S(2)}) collective-permute-start(f32[258,1]{1,0:T(8,128)S(1)} %get-tuple-element.250), channel_id=1, source_target_pairs={{1,0},{2,1},{3,2},{4,3},{5,4},{6,5},{7,6},{8,7},{9,8},{10,9},{11,1... | collective-permute-start | bytes 3104 | tf_op jit(solution)/shard_map/ppermute | solution.py:20
  340.8 9.6 %collective-permute-start.55 = (f32[258,1]{1,0:T(8,128)S(1)}, f32[258,1]{1,0:T(8,128)S(1)}, u32[]{:S(2)}, u32[]{:S(2)}) collective-permute-start(f32[258,1]{1,0:T(8,128)S(1)} %get-tuple-element.251), channel_id=1, source_target_pairs={{0,1},{1,2},{2,3},{3,4},{4,5},{5,6},{6,7},{7,8},{8,9},{9,10},{10,1... | collective-permute-start | bytes 3104 | tf_op jit(solution)/shard_map/ppermute | solution.py:18
  357.9 9.7 %collective-permute-start.58 = (f32[258,1]{1,0:T(8,128)S(1)}, f32[258,1]{1,0:T(8,128)S(1)}, u32[]{:S(2)}, u32[]{:S(2)}) collective-permute-start(f32[258,1]{1,0:T(8,128)S(1)} %get-tuple-element.248), channel_id=1, source_target_pairs={{1,0},{2,1},{3,2},{4,3},{5,4},{6,5},{7,6},{8,7},{9,8},{10,9},{11,1... | collective-permute-start | bytes 3104 | tf_op jit(solution)/shard_map/ppermute | solution.py:20
  359.2 9.6 %collective-permute-start.59 = (f32[258,1]{1,0:T(8,128)S(1)}, f32[258,1]{1,0:T(8,128)S(1)}, u32[]{:S(2)}, u32[]{:S(2)}) collective-permute-start(f32[258,1]{1,0:T(8,128)S(1)} %get-tuple-element.249), channel_id=1, source_target_pairs={{0,1},{1,2},{2,3},{3,4},{4,5},{5,6},{6,7},{7,8},{8,9},{9,10},{10,1... | collective-permute-start | bytes 3104 | tf_op jit(solution)/shard_map/ppermute | solution.py:18
  376.3 9.7 %collective-permute-start.62 = (f32[258,1]{1,0:T(8,128)S(1)}, f32[258,1]{1,0:T(8,128)S(1)}, u32[]{:S(2)}, u32[]{:S(2)}) collective-permute-start(f32[258,1]{1,0:T(8,128)S(1)} %get-tuple-element.246), channel_id=1, source_target_pairs={{1,0},{2,1},{3,2},{4,3},{5,4},{6,5},{7,6},{8,7},{9,8},{10,9},{11,1... | collective-permute-start | bytes 3104 | tf_op jit(solution)/shard_map/ppermute | solution.py:20
  377.6 9.6 %collective-permute-start.63 = (f32[258,1]{1,0:T(8,128)S(1)}, f32[258,1]{1,0:T(8,128)S(1)}, u32[]{:S(2)}, u32[]{:S(2)}) collective-permute-start(f32[258,1]{1,0:T(8,128)S(1)} %get-tuple-element.247), channel_id=1, source_target_pairs={{0,1},{1,2},{2,3},{3,4},{4,5},{5,6},{6,7},{7,8},{8,9},{9,10},{10,1... | collective-permute-start | bytes 3104 | tf_op jit(solution)/shard_map/ppermute | solution.py:18
  387.7 5.6 %collective-permute-start.65 = (f32[1,512]{1,0:T(1,128)S(1)}, f32[1,512]{1,0:T(1,128)S(1)}, u32[]{:S(2)}, u32[]{:S(2)}) collective-permute-start(f32[1,512]{1,0:T(1,128)S(1)} %get-tuple-element.284), channel_id=1, source_target_pairs={{0,16},{16,32},{32,48},{48,64},{64,80},{80,96},{96,112},{1,17},{17... | collective-permute-start | bytes 6152 | tf_op jit(solution)/shard_map/ppermute | solution.py:18
  394.7 9.7 %collective-permute-start.66 = (f32[258,1]{1,0:T(8,128)S(1)}, f32[258,1]{1,0:T(8,128)S(1)}, u32[]{:S(2)}, u32[]{:S(2)}) collective-permute-start(f32[258,1]{1,0:T(8,128)S(1)} %get-tuple-element.244), channel_id=1, source_target_pairs={{1,0},{2,1},{3,2},{4,3},{5,4},{6,5},{7,6},{8,7},{9,8},{10,9},{11,1... | collective-permute-start | bytes 3104 | tf_op jit(solution)/shard_map/ppermute | solution.py:20
  396.0 9.6 %collective-permute-start.67 = (f32[258,1]{1,0:T(8,128)S(1)}, f32[258,1]{1,0:T(8,128)S(1)}, u32[]{:S(2)}, u32[]{:S(2)}) collective-permute-start(f32[258,1]{1,0:T(8,128)S(1)} %get-tuple-element.245), channel_id=1, source_target_pairs={{0,1},{1,2},{2,3},{3,4},{4,5},{5,6},{6,7},{7,8},{8,9},{9,10},{10,1... | collective-permute-start | bytes 3104 | tf_op jit(solution)/shard_map/ppermute | solution.py:18
  413.1 9.7 %collective-permute-start.70 = (f32[258,1]{1,0:T(8,128)S(1)}, f32[258,1]{1,0:T(8,128)S(1)}, u32[]{:S(2)}, u32[]{:S(2)}) collective-permute-start(f32[258,1]{1,0:T(8,128)S(1)} %get-tuple-element.242), channel_id=1, source_target_pairs={{1,0},{2,1},{3,2},{4,3},{5,4},{6,5},{7,6},{8,7},{9,8},{10,9},{11,1... | collective-permute-start | bytes 3104 | tf_op jit(solution)/shard_map/ppermute | solution.py:20
  414.4 9.6 %collective-permute-start.71 = (f32[258,1]{1,0:T(8,128)S(1)}, f32[258,1]{1,0:T(8,128)S(1)}, u32[]{:S(2)}, u32[]{:S(2)}) collective-permute-start(f32[258,1]{1,0:T(8,128)S(1)} %get-tuple-element.243), channel_id=1, source_target_pairs={{0,1},{1,2},{2,3},{3,4},{4,5},{5,6},{6,7},{7,8},{8,9},{9,10},{10,1... | collective-permute-start | bytes 3104 | tf_op jit(solution)/shard_map/ppermute | solution.py:18
  424.5 5.6 %collective-permute-start.73 = (f32[1,512]{1,0:T(1,128)S(1)}, f32[1,512]{1,0:T(1,128)S(1)}, u32[]{:S(2)}, u32[]{:S(2)}) collective-permute-start(f32[1,512]{1,0:T(1,128)S(1)} %get-tuple-element.280), channel_id=1, source_target_pairs={{0,16},{16,32},{32,48},{48,64},{64,80},{80,96},{96,112},{1,17},{17... | collective-permute-start | bytes 6152 | tf_op jit(solution)/shard_map/ppermute | solution.py:18
  431.5 9.7 %collective-permute-start.74 = (f32[258,1]{1,0:T(8,128)S(1)}, f32[258,1]{1,0:T(8,128)S(1)}, u32[]{:S(2)}, u32[]{:S(2)}) collective-permute-start(f32[258,1]{1,0:T(8,128)S(1)} %get-tuple-element.240), channel_id=1, source_target_pairs={{1,0},{2,1},{3,2},{4,3},{5,4},{6,5},{7,6},{8,7},{9,8},{10,9},{11,1... | collective-permute-start | bytes 3104 | tf_op jit(solution)/shard_map/ppermute | solution.py:20
  432.8 9.6 %collective-permute-start.75 = (f32[258,1]{1,0:T(8,128)S(1)}, f32[258,1]{1,0:T(8,128)S(1)}, u32[]{:S(2)}, u32[]{:S(2)}) collective-permute-start(f32[258,1]{1,0:T(8,128)S(1)} %get-tuple-element.241), channel_id=1, source_target_pairs={{0,1},{1,2},{2,3},{3,4},{4,5},{5,6},{6,7},{7,8},{8,9},{9,10},{10,1... | collective-permute-start | bytes 3104 | tf_op jit(solution)/shard_map/ppermute | solution.py:18
  443.0 5.6 %collective-permute-start.77 = (f32[1,512]{1,0:T(1,128)S(1)}, f32[1,512]{1,0:T(1,128)S(1)}, u32[]{:S(2)}, u32[]{:S(2)}) collective-permute-start(f32[1,512]{1,0:T(1,128)S(1)} %get-tuple-element.278), channel_id=1, source_target_pairs={{0,16},{16,32},{32,48},{48,64},{64,80},{80,96},{96,112},{1,17},{17... | collective-permute-start | bytes 6152 | tf_op jit(solution)/shard_map/ppermute | solution.py:18
  449.9 9.7 %collective-permute-start.78 = (f32[258,1]{1,0:T(8,128)S(1)}, f32[258,1]{1,0:T(8,128)S(1)}, u32[]{:S(2)}, u32[]{:S(2)}) collective-permute-start(f32[258,1]{1,0:T(8,128)S(1)} %get-tuple-element.238), channel_id=1, source_target_pairs={{1,0},{2,1},{3,2},{4,3},{5,4},{6,5},{7,6},{8,7},{9,8},{10,9},{11,1... | collective-permute-start | bytes 3104 | tf_op jit(solution)/shard_map/ppermute | solution.py:20
  451.2 9.6 %collective-permute-start.79 = (f32[258,1]{1,0:T(8,128)S(1)}, f32[258,1]{1,0:T(8,128)S(1)}, u32[]{:S(2)}, u32[]{:S(2)}) collective-permute-start(f32[258,1]{1,0:T(8,128)S(1)} %get-tuple-element.239), channel_id=1, source_target_pairs={{0,1},{1,2},{2,3},{3,4},{4,5},{5,6},{6,7},{7,8},{8,9},{9,10},{10,1... | collective-permute-start | bytes 3104 | tf_op jit(solution)/shard_map/ppermute | solution.py:18
  (38 other events, 263.6 us)
where the time goes:
time: 513 us; the launch traced here: 510 us
  starting transfers between devices  289 us (56%)
  waiting for transfers between devices  107 us (21%)
  local copies, waits for them, and re-layouts  38.4 us (7%)
  blocking collectives  34.7 us (7%)
  other arithmetic  21.3 us (4%)
  matrix products  16.6 us (3%)
    ppermute x40, starting transfers between devices, padded_2(): lax.ppermute(tail, axis, [(i, (i + 1) % count) for i in range(ends)])  170 us
    ppermute x40, starting transfers between devices, padded_2(): lax.ppermute(head, axis, [((i + 1) % count, i) for i in range(ends)])  98.9 us
    ppermute x40, waiting for transfers between devices, padded_2(): lax.ppermute(head, axis, [((i + 1) % count, i) for i in range(ends)])  55 us
    all_gather x1, blocking collectives, entering(): gathered = lax.all_gather(part, axis)  34.7 us
    all_to_all x1, waiting for transfers between devices, body(): lax.all_to_all(send_heights.reshape(devices, capacity, 128), ('east', 'no...  28.3 us
    ppermute x40, waiting for transfers between devices, padded_2(): lax.ppermute(tail, axis, [(i, (i + 1) % count) for i in range(ends)])  24.1 us
    scatter x1, local copies, waits for them, and re-layouts, body(): jnp.full((devices * capacity,), -1, jnp.int32).at[slot].set(segment_ids)  15.7 us
    scatter x1, local copies, waits for them, and re-layouts, body(): jnp.zeros((devices * capacity, 128), jnp.bfloat16).at[slot].set(heights)  12.8 us
  transfers between devices with their start and end apart: 82, of which 61 were waited for; matrix products, arithmetic and copies ran while one was open for 3% of the time, Pallas kernels for 0%

commit v1 on v0

v1 whole, which is shorter than its diff:
```python
import jax
import jax.numpy as jnp
from jax import lax
from jax.experimental import pallas as pl
from jax.experimental.pallas import tpu as pltpu
from jax.sharding import PartitionSpec as P

NS = 8
STEPS = 20
CAP = 64
BLOCK = 72
HALO = 24
GAP = 1000.0

F32 = jnp.float32
BF16 = jnp.bfloat16
I32 = jnp.int32


def vmem():
    return pl.BlockSpec(memory_space=pltpu.VMEM)


def smem():
    return pl.BlockSpec(memory_space=pltpu.SMEM)


def iota(shape, dim):
    return lax.broadcasted_iota(I32, shape, dim)


def deal_kernel(heights, owner, segment, out, wide, dealt, slots, ids, slots_s, sem):
    devices = out.shape[0]
    rows = heights.shape[0]
    chunks = rows // 128
    zeros = jnp.zeros((BLOCK, 128), F32)

    @pl.loop(0, devices)
    def _(t):
        dealt[pl.ds(pl.multiple_of(t * BLOCK, 8), BLOCK), :] = zeros

    @pl.loop(0, rows // 64)
    def _(c):
        at = pl.ds(pl.multiple_of(c * 64, 64), 64)
        wide[at, :] = heights[at, :].astype(F32)

    tile = iota((devices, 128), 0)
    before = (iota((128, 256), 0) < iota((128, 256), 1)).astype(F32).astype(BF16)
    place = iota((128, 128), 0) & (CAP - 1)

    def chunk(c, carry):
        seen, named = carry
        own = owner[pl.ds(c, 1), :]
        hit = tile == own
        counts = jnp.dot(hit.astype(F32).astype(BF16), before, preferred_element_type=F32)
        rank = jnp.sum(jnp.where(hit, counts[:, :128] + seen, 0.0), axis=0, keepdims=True)
        rank = rank.astype(I32)
        slots[pl.ds(c, 1), :] = own * BLOCK + rank
        seg = segment[pl.ds(c, 1), :]
        code = (((seg & 127) + 128) << (seg >> 7)).astype(F32)
        coded = jnp.where(hit, jnp.broadcast_to(code, hit.shape), 0.0).astype(BF16)
        ranked = (place == rank).astype(F32).astype(BF16)
        named = named + lax.dot_general(
            coded, ranked, (((1,), (1,)), ((), ())), preferred_element_type=F32
        )
        return seen + counts[:, 128:], named

    start = jnp.zeros((devices, 128), F32)
    _, named = lax.fori_loop(0, chunks, chunk, (start, start), unroll=2)
    ids[...] = named
    copy = pltpu.make_async_copy(slots, slots_s, sem)
    copy.start()
    copy.wait()

    @pl.loop(0, devices)
    def _(t):
        dealt[pl.ds(t * BLOCK + CAP, 1), :] = ids[pl.ds(t, 1), :]

    @pl.loop(0, chunks)
    def _(c):
        for i in range(128):
            dealt[pl.ds(slots_s[c, i], 1), :] = wide[pl.ds(c * 128 + i, 1), :]

    @pl.loop(0, devices)
    def _(t):
        out[t] = dealt[pl.ds(pl.multiple_of(t * BLOCK, 8), BLOCK), :].astype(BF16)


def bin_kernel(got, gap_mask, out, first, last, acc, codes, lines):
    devices = got.shape[0]
    tile_rows, tile_cols = gap_mask.shape
    quarters = tile_cols // 128
    pairs = devices // 2
    low = iota((1, 128), 1) < CAP
    for p in range(pairs):
        a = got[2 * p][CAP:CAP + 1, :].astype(F32)
        b = got[2 * p + 1][CAP:CAP + 1, :].astype(F32)
        codes[p:p + 1, :] = jnp.where(low, a, b)
    code = codes[...]
    shift = jnp.zeros(code.shape, I32)
    for j in range(1, 8):
        shift = shift + (code >= 128.0 * 2**j).astype(I32)
    seg = (shift << 7) + (code.astype(I32) >> shift) - 128
    for q in range(quarters):
        lines[q] = jnp.where((code > 0.0) & ((seg & (quarters - 1)) == q), seg // quarters, -1)
    acc[...] = jnp.zeros(acc.shape, F32)
    line = iota((tile_rows, 128), 0)
    ones = jnp.ones((256, 128), BF16)

    @pl.loop(0, devices // 4)
    def _(i):
        cells = jnp.concatenate([got[4 * i + j][:CAP, :] for j in range(4)], axis=0)
        cells = jnp.concatenate([cells, ones], axis=1)
        for q in range(quarters):
            hot = jnp.concatenate(
                [
                    (line == lines[q, pl.ds(2 * i + j, 1), :]).astype(F32).astype(BF16)
                    for j in range(2)
                ],
                axis=1,
            )
            acc[q] += jnp.dot(hot, cells, preferred_element_type=F32)

    for q in range(quarters):
        cols = slice(q * 128, (q + 1) * 128)
        total = acc[q]
        summed, counted = total[:, :128], total[:, 128:]
        unknown = (gap_mask[:, cols] == 1) | (counted == 0.0)
        out[:, cols] = jnp.where(unknown, GAP, summed / jnp.maximum(counted, 1.0))
    first[...] = out[:HALO, :]
    last[...] = out[tile_rows - HALO:, :]


def sides_kernel(tile, above, below, west, east, slab):
    rows, cols = tile.shape
    slab[...] = jnp.zeros(slab.shape, F32)
    for out, at, keep in ((west, 0, 0), (east, cols - 128, 128 - HALO)):
        slab[:rows, :] = tile[:, at:at + 128]
        slab[rows:rows + HALO, :] = above[:, at:at + 128]
        slab[rows + HALO:rows + 2 * HALO, :] = below[:, at:at + 128]
        out[...] = slab[...].T[keep:keep + HALO, :]


def fill_kernel(tile, above, below, right, left, surface, depths, totals, cells, rate):
    rows, cols = tile.shape
    wide = cols + 128
    tall = rows + 2 * HALO

    def put(at, width, values):
        unknown = values > 0.5 * GAP
        cells[at, width] = jnp.where(unknown, 0.0, values)
        rate[at, width] = jnp.where(unknown, 0.9, 0.0)

    put(slice(0, rows), slice(0, cols), tile[...])
    put(slice(rows, rows + HALO), slice(0, cols), above[...])
    put(slice(rows + HALO, tall), slice(0, cols), below[...])
    beside = jnp.concatenate(
        [right[...], jnp.zeros((128 - 2 * HALO, right.shape[1]), F32), left[...]], axis=0
    ).T
    put(slice(0, tall), slice(cols, wide), beside[:tall, :])

    blocks = tall // 8
    top = iota((8, wide), 0) == 0
    bottom = iota((8, wide), 0) == 7

    def step(_, carry):
        def block(b):
            return cells[b * 8:b * 8 + 8, :]

        opening = block(0)
        lower_0 = pltpu.roll(opening, 7, axis=0)
        before = pltpu.roll(block(blocks - 1), 1, axis=0)
        here, here_up = opening, lower_0
        for b in range(blocks):
            if b + 1 < blocks:
                after = block(b + 1)
                after_up = pltpu.roll(after, 7, axis=0)
            else:
                after, after_up = opening, lower_0
            here_down = pltpu.roll(here, 1, axis=0)
            total = jnp.where(top, before, here_down) + jnp.where(bottom, after_up, here_up)
            total = total + (pltpu.roll(here, 1, axis=1) + pltpu.roll(here, wide - 1, axis=1))
            cells[b * 8:b * 8 + 8, :] = here + rate[b * 8:b * 8 + 8, :] * (0.25 * total - here)
            before, here, here_up = here_down, after, after_up
        return carry

    lax.fori_loop(0, STEPS, step, 0)
    final = cells[:rows, :cols]
    surface[...] = final
    soft = jnp.maximum(final, 0.0) + jnp.log1p(jnp.exp(-jnp.abs(final)))
    ahead = (iota((cols, cols), 0) < iota((cols, cols), 1)).astype(F32)
    south = jnp.dot(soft, ahead, precision=lax.Precision.HIGHEST, preferred_element_type=F32)
    whole = jnp.sum(soft, axis=1, keepdims=True)
    depths[0] = south
    depths[1] = (whole - south) - soft
    ones = jnp.ones((8, cols), F32)
    along = lax.dot_general(
        ones, soft, (((1,), (1,)), ((), ())), precision=lax.Precision.HIGHEST,
        preferred_element_type=F32,
    )
    packed = jnp.where(iota((8, 128), 0) == 0, along[:, :128], along[:, 128:])
    for n in range(totals.shape[0]):
        totals[n] = packed


def light_kernel(place, extinction, side, depths, totals, out, carried):
    s = pl.program_id(0)
    _, rows, cols = depths.shape
    count = totals.shape[0]

    @pl.when(s == 0)
    def _():
        here = place[0]
        zero = jnp.zeros((8, 128), F32)
        for k in range(2):
            total = zero
            for n in range(count):
                counts = here < n if k else here > n
                total = total + jnp.where(counts, totals[n], zero)
            turned = jnp.concatenate([total, jnp.zeros((120, 128), F32)], axis=0).T
            for half in range(rows // 128):
                carried[k, half * 128:(half + 1) * 128, :] = jnp.broadcast_to(
                    turned[:, half:half + 1], (128, 128)
                )

    pick = side[s]
    rate = -(extinction[s] / (cols * count))
    for q in range(cols // 128):
        at = slice(q * 128, (q + 1) * 128)
        out[0, :, at] = jnp.exp(rate * (depths[pick, :, at] + carried[pick]))


def moved(values, axis, hop):
    count = lax.axis_size(axis)
    return lax.ppermute(
        values, axis, [(i, i + hop) for i in range(count) if 0 <= i + hop < count]
    )


def body(heights, segment_ids, tile_owner, gap_mask, extinction, sun_side):
    rows_here = heights.shape[0]
    tile_rows, tile_cols = gap_mask.shape
    n_north = lax.axis_size("north")
    devices = lax.axis_size("east") * n_north
    chunks = rows_here // 128
    tall = tile_rows + 128
    mib = 1 << 20

    dealt = pl.pallas_call(
        deal_kernel,
        out_shape=jax.ShapeDtypeStruct((devices, BLOCK, 128), BF16),
        in_specs=[vmem()] * 3,
        out_specs=vmem(),
        scratch_shapes=[
            pltpu.VMEM((rows_here, 128), F32),
            pltpu.VMEM((devices * BLOCK, 128), F32),
            pltpu.VMEM((chunks, 128), I32),
            pltpu.VMEM((devices, 128), F32),
            pltpu.SMEM((chunks, 128), I32),
            pltpu.SemaphoreType.DMA,
        ],
        compiler_params=pltpu.CompilerParams(vmem_limit_bytes=24 * mib),
        name="deal",
    )(heights, tile_owner.reshape(chunks, 128), segment_ids.reshape(chunks, 128))

    got = lax.all_to_all(dealt, ("east", "north"), split_axis=0, concat_axis=0, tiled=True)

    strip = jax.ShapeDtypeStruct((HALO, tile_cols), F32)
    tile, first, last = pl.pallas_call(
        bin_kernel,
        out_shape=(jax.ShapeDtypeStruct((tile_rows, tile_cols), F32), strip, strip),
        in_specs=[vmem()] * 2,
        out_specs=(vmem(),) * 3,
        scratch_shapes=[
            pltpu.VMEM((tile_cols // 128, tile_rows, 256), F32),
            pltpu.VMEM((devices // 2, 128), F32),
            pltpu.VMEM((tile_cols // 128, devices // 2, 128), I32),
        ],
        compiler_params=pltpu.CompilerParams(vmem_limit_bytes=24 * mib),
        name="bin",
    )(got, gap_mask)

    below = moved(last, "east", 1)
    above = moved(first, "east", -1)

    turned = jax.ShapeDtypeStruct((HALO, tall), F32)
    west, east = pl.pallas_call(
        sides_kernel,
        out_shape=(turned, turned),
        in_specs=[vmem()] * 3,
        out_specs=(vmem(),) * 2,
        scratch_shapes=[pltpu.VMEM((tall, 128), F32)],
        compiler_params=pltpu.CompilerParams(vmem_limit_bytes=16 * mib),
        name="sides",
    )(tile, above, below)

    left = moved(east, "north", 1)
    right = moved(west, "north", -1)

    surface, depths, totals = pl.pallas_call(
        fill_kernel,
        out_shape=(
            jax.ShapeDtypeStruct((tile_rows, tile_cols), F32),
            jax.ShapeDtypeStruct((2, tile_rows, tile_cols), F32),
            jax.ShapeDtypeStruct((n_north, 8, 128), F32),
        ),
        in_specs=[vmem()] * 5,
        out_specs=(vmem(),) * 3,
        scratch_shapes=[pltpu.VMEM((tile_rows + 2 * HALO, tile_cols + 128), F32)] * 2,
        compiler_params=pltpu.CompilerParams(vmem_limit_bytes=32 * mib),
        name="fill",
    )(tile, above, below, right, left)

    totals = lax.all_to_all(totals, "north", split_axis=0, concat_axis=0, tiled=True)
    place = lax.axis_index("north").astype(I32).reshape(1)

    light = pl.pallas_call(
        light_kernel,
        grid=(NS,),
        out_shape=jax.ShapeDtypeStruct((NS, tile_rows, tile_cols), F32),
        in_specs=[smem()] * 3 + [vmem()] * 2,
        out_specs=pl.BlockSpec((1, tile_rows, tile_cols), lambda s: (s, 0, 0)),
        scratch_shapes=[pltpu.VMEM((2, tile_rows, 128), F32)],
        compiler_params=pltpu.CompilerParams(vmem_limit_bytes=24 * mib),
        name="light",
    )(place, extinction, sun_side, depths, totals)
    return surface, light


def solution(mesh):
    return jax.shard_map(
        body,
        mesh=mesh,
        in_specs=(
            P(("east", "north"), None),
            P(("east", "north")),
            P(("east", "north"), None),
            P("east", "north"),
            P(),
            P(),
        ),
        out_specs=(P("east", "north"), P(None, "east", "north")),
        check_vma=False,
    )
```

time: 513 us -> 117 us (0.23)
  starting transfers between devices: 289 us -> 18.5 us
  waiting for transfers between devices: 107 us -> 12.3 us
  Pallas kernels: 0 us -> 39.3 us
  local copies, waits for them, and re-layouts: 38.4 us -> 2.67 us
  other arithmetic: 21.3 us -> 0 us
  matrix products: 16.6 us -> 0 us
  blocking collectives: 34.7 us -> 42.7 us
    ppermute x80 -> x4, starting transfers between devices: 268 us -> 10.2 us  [moved(): lax.ppermute(values, axis, [(i, i + hop) for i in range(count) if 0 <= i...]
    ppermute x80 -> x4, waiting for transfers between devices: 79.1 us -> 4.6 us  [moved(): lax.ppermute(values, axis, [(i, i + hop) for i in range(count) if 0 <= i...]
    all_to_all x0 -> x1, blocking collectives: none -> 42.7 us  [body(): lax.all_to_all(dealt, ('east', 'north'), split_axis=0, concat_axis=0, til...]
    pallas_call x0 -> x5, Pallas kernels: none -> 39.3 us  [the longest x1 12.8 us: body(): pl.pallas_call(deal_kernel, out_shape=jax.ShapeDtypeStruct((devices, BLOC...]
    all_gather x1 -> x0, blocking collectives: 34.7 us -> none  [entering(): gathered = lax.all_gather(part, axis)]
    scatter x2 -> x0, local copies, waits for them, and re-layouts: 28.5 us -> none  [the longest x1 15.7 us: body(): jnp.full((devices * capacity,), -1, jnp.int32).at[slot].set(segment_ids)]
    all_to_all x2 -> x1, waiting for transfers between devices: 28.3 us -> 7.66 us  [body(): lax.all_to_all(totals, 'north', split_axis=0, concat_axis=0, tiled=True)]
    dot_general x6 -> x0, matrix products: 16.6 us -> none  [the longest x4 11.2 us: add_block(): lax.dot_general(onehot.astype(jnp.bfloat16), part_heights, (((0,), (0,)),...]
  transfers between devices with their start and end apart: 82 -> 5, of which waited for: 61 -> 3; matrix products, arithmetic and copies ran while one was open for 3% -> 0% of each run, Pallas kernels for 0% -> 0%
where the time goes in v1:
time: 117 us; the launch traced here: 116 us
  blocking collectives  42.7 us (36%)
  Pallas kernels  39.3 us (34%)
  starting transfers between devices  18.5 us (16%)
  waiting for transfers between devices  12.3 us (11%)
  local copies, waits for them, and re-layouts  2.67 us (2%)
    all_to_all x1, blocking collectives, body(): lax.all_to_all(dealt, ('east', 'north'), split_axis=0, concat_axis=0, til...  42.7 us
    pallas_call x1, Pallas kernels, body(): pl.pallas_call(deal_kernel, out_shape=jax.ShapeDtypeStruct((devices, BLOC...  12.8 us
    pallas_call x1, Pallas kernels, body(): pl.pallas_call(fill_kernel, out_shape=(jax.ShapeDtypeStruct((tile_rows, t...  11.8 us
    ppermute x4, starting transfers between devices, moved(): lax.ppermute(values, axis, [(i, i + hop) for i in range(count) if 0 <= i...  10.2 us
    pallas_call x1, Pallas kernels, body(): pl.pallas_call(bin_kernel, out_shape=(jax.ShapeDtypeStruct((tile_rows, ti...  9.99 us
    all_to_all x1, starting transfers between devices, body(): lax.all_to_all(totals, 'north', split_axis=0, concat_axis=0, tiled=True)  8.32 us
    all_to_all x1, waiting for transfers between devices, body(): lax.all_to_all(totals, 'north', split_axis=0, concat_axis=0, tiled=True)  7.66 us
    ppermute x4, waiting for transfers between devices, moved(): lax.ppermute(values, axis, [(i, i + hop) for i in range(count) if 0 <= i...  4.6 us
  transfers between devices with their start and end apart: 5, of which 3 were waited for; matrix products, arithmetic and copies ran while one was open for 0% of the time, Pallas kernels for 0%

profile of v1, /device:TPU:2, one launch (start us, length us, event | category | flops | bytes accessed | tf_op | source)
XLA Modules:
  0.0 116.1 jit_solution(17099839876264290030)
XLA Ops:
  0.6 0.0 copy-start
  0.6 1.2 %copy-done = bf16[4096,128]{1,0:T(8,128)(2,1)S(1)} copy-done((bf16[4096,128]{1,0:T(8,128)(2,1)S(1)}, bf16[4096,128]{1,0:T(8,128)(2,1)}, u32[]{:S(2)}) %copy-start) | copy-done | bytes 1048600
  1.9 0.0 copy-start.2
  1.9 0.7 copy-done.2
  2.6 0.0 copy-start.3
  2.6 0.7 copy-done.3
  3.3 12.8 %deal.1 = bf16[128,72,128]{2,1,0:T(8,128)(2,1)S(1)} custom-call(bf16[4096,128]{1,0:T(8,128)(2,1)S(1)} %copy-done, s32[32,128]{1,0:T(8,128)S(1)} %bitcast.3, s32[32,128]{1,0:T(8,128)S(1)} %bitcast.4), custom_call_target="tpu_custom_call" | custom-call | tf_op jit(solution)/shard_map/deal/pallas_call | solution.py:249
  16.1 0.0 copy-start.1
  16.1 42.7 %all_to_all.10.got = bf16[128,72,128]{2,1,0:T(8,128)(2,1)S(1)} all-to-all(bf16[128,72,128]{2,1,0:T(8,128)(2,1)S(1)} %deal.1), channel_id=1, replica_groups=mesh['east'=8,'north'=16] {'east','north'}, dimensions={0} | all-to-all | bytes 4718592 | tf_op jit(solution)/shard_map/all_to_all | solution.py:266
  58.8 0.0 copy-done.1
  58.8 0.0 copy-start.4
  58.8 0.0 copy-start.5
  58.8 10.0 %bin.1 = (f32[256,512]{1,0:T(8,128)S(1)}, f32[24,512]{1,0:T(8,128)S(1)}, f32[24,512]{1,0:T(8,128)S(1)}) custom-call(bf16[128,72,128]{2,1,0:T(8,128)(2,1)S(1)} %all_to_all.10.got, s32[256,512]{1,0:T(8,128)S(1)} %copy-done.1), custom_call_target="tpu_custom_call" | custom-call | tf_op jit(solution)/shard_map/bin/pallas_call | solution.py:269
  68.8 1.9 %collective-permute-start = (f32[24,512]{1,0:T(8,128)S(1)}, f32[24,512]{1,0:T(8,128)S(1)}, u32[]{:S(2)}, u32[]{:S(2)}) collective-permute-start(f32[24,512]{1,0:T(8,128)S(1)} %get-tuple-element.11), channel_id=1, source_target_pairs={{16,0},{32,16},{48,32},{64,48},{80,64},{96,80},{112,96},{17,1},{33... | collective-permute-start | bytes 147464 | tf_op jit(solution)/shard_map/ppermute | solution.py:235
  70.7 2.4 %collective-permute-start.1 = (f32[24,512]{1,0:T(8,128)S(1)}, f32[24,512]{1,0:T(8,128)S(1)}, u32[]{:S(2)}, u32[]{:S(2)}) collective-permute-start(f32[24,512]{1,0:T(8,128)S(1)} %get-tuple-element.12), channel_id=1, source_target_pairs={{0,16},{16,32},{32,48},{48,64},{64,80},{80,96},{96,112},{1,17},{17... | collective-permute-start | bytes 147464 | tf_op jit(solution)/shard_map/ppermute | solution.py:235
  73.1 0.0 collective-permute-done.above
  73.1 3.0 %collective-permute-done.1.below = f32[24,512]{1,0:T(8,128)S(1)} collective-permute-done((f32[24,512]{1,0:T(8,128)S(1)}, f32[24,512]{1,0:T(8,128)S(1)}, u32[]{:S(2)}, u32[]{:S(2)}) %collective-permute-start.1) | collective-permute-done | bytes 49184 | tf_op jit(solution)/shard_map/ppermute | solution.py:235
  76.1 0.2 sides.1
  76.3 1.3 %collective-permute-start.2 = (f32[24,384]{1,0:T(8,128)S(1)}, f32[24,384]{1,0:T(8,128)S(1)}, u32[]{:S(2)}, u32[]{:S(2)}) collective-permute-start(f32[24,384]{1,0:T(8,128)S(1)} %get-tuple-element.13), channel_id=1, source_target_pairs={{1,0},{2,1},{3,2},{4,3},{5,4},{6,5},{7,6},{8,7},{9,8},{10,9},{11,1... | collective-permute-start | bytes 110600 | tf_op jit(solution)/shard_map/ppermute | solution.py:235
  77.6 4.5 %collective-permute-start.3 = (f32[24,384]{1,0:T(8,128)S(1)}, f32[24,384]{1,0:T(8,128)S(1)}, u32[]{:S(2)}, u32[]{:S(2)}) collective-permute-start(f32[24,384]{1,0:T(8,128)S(1)} %get-tuple-element.14), channel_id=1, source_target_pairs={{0,1},{1,2},{2,3},{3,4},{4,5},{5,6},{6,7},{7,8},{8,9},{9,10},{10,1... | collective-permute-start | bytes 110600 | tf_op jit(solution)/shard_map/ppermute | solution.py:235
  82.1 0.0 collective-permute-done.2.right
  82.2 1.6 %collective-permute-done.3.left = f32[24,384]{1,0:T(8,128)S(1)} collective-permute-done((f32[24,384]{1,0:T(8,128)S(1)}, f32[24,384]{1,0:T(8,128)S(1)}, u32[]{:S(2)}, u32[]{:S(2)}) %collective-permute-start.3) | collective-permute-done | bytes 36896 | tf_op jit(solution)/shard_map/ppermute | solution.py:235
  83.8 11.8 %fill.1 = (f32[256,512]{1,0:T(8,128)}, f32[2,256,512]{2,1,0:T(8,128)S(1)}, f32[16,8,128]{2,1,0:T(8,128)}) custom-call(f32[256,512]{1,0:T(8,128)S(1)} %get-tuple-element.10.tile, f32[24,512]{1,0:T(8,128)S(1)} %collective-permute-done.above, f32[24,512]{1,0:T(8,128)S(1)} %collective-permute-done.1.below, f32[24,384]{1,0:T(8,128)S(1)} %collective-permute-done.2.right, ...), custom_call_target="tpu_custom_call" | custom-call | tf_op jit(solution)/shard_map/fill/pallas_call | solution.py:300
  95.6 8.3 %all-to-all-start.1 = ((f32[16,8,128]{2,1,0:T(8,128)}), f32[16,8,128]{2,1,0:T(8,128)S(1)}, u32[]{:S(2)}, u32[]{:S(2)}) async-start(f32[16,8,128]{2,1,0:T(8,128)} %get-tuple-element.17), calls=%async_computation.1 | async-start | bytes 131072 | tf_op jit(solution)/shard_map/all_to_all | solution.py:314
  103.9 7.7 %all-to-all-done.1.totals = f32[16,8,128]{2,1,0:T(8,128)S(1)} async-done(((f32[16,8,128]{2,1,0:T(8,128)}), f32[16,8,128]{2,1,0:T(8,128)S(1)}, u32[]{:S(2)}, u32[]{:S(2)}) %all-to-all-start.1) | async-done | bytes 65568 | tf_op jit(solution)/shard_map/all_to_all | solution.py:314
  111.6 0.0 copy-done.4
  111.6 0.0 copy-done.5
  111.6 4.5 %light.1 = f32[8,256,512]{2,1,0:T(8,128)} custom-call(s32[1]{0:T(128)} %bitcast.2.place, f32[8]{0:T(128)S(1)} %copy-done.4, s32[8]{0:T(128)S(1)} %copy-done.5, f32[2,256,512]{2,1,0:T(8,128)S(1)} %get-tuple-element.16.depths, f32[16,8,128]{2,1,0:T(8,128)S(1)} %all-to-all-done.1.totals), custom_call_target="tpu_custom_call" | custom-call | tf_op jit(solution)/shard_map/light/pallas_call | solution.py:317
Async XLA Ops:
  0.6 1.2 %copy-start = (bf16[4096,128]{1,0:T(8,128)(2,1)S(1)}, bf16[4096,128]{1,0:T(8,128)(2,1)}, u32[]{:S(2)}) copy-start(bf16[4096,128]{1,0:T(8,128)(2,1)} %heights.1) | copy-start | bytes 3145732
  1.9 0.7 copy-start.2
  2.6 0.7 copy-start.3
  16.1 42.7 %copy-start.1 = (s32[256,512]{1,0:T(8,128)S(1)}, s32[256,512]{1,0:T(8,128)}, u32[]{:S(2)}) copy-start(s32[256,512]{1,0:T(8,128)} %gap_mask.1) | copy-start | bytes 1572868
  58.8 52.8 %copy-start.4 = (f32[8]{0:T(128)S(1)}, f32[8]{0:T(128)}, u32[]{:S(2)}) copy-start(f32[8]{0:T(128)} %extinction.1) | copy-start | bytes 100
  58.8 52.8 %copy-start.5 = (s32[8]{0:T(128)S(1)}, s32[8]{0:T(128)}, u32[]{:S(2)}) copy-start(s32[8]{0:T(128)} %side.1) | copy-start | bytes 100
  68.8 4.3 %collective-permute-start = (f32[24,512]{1,0:T(8,128)S(1)}, f32[24,512]{1,0:T(8,128)S(1)}, u32[]{:S(2)}, u32[]{:S(2)}) collective-permute-start(f32[24,512]{1,0:T(8,128)S(1)} %get-tuple-element.11), channel_id=1, source_target_pairs={{16,0},{32,16},{48,32},{64,48},{80,64},{96,80},{112,96},{17,1},{33... | collective-permute-start | bytes 147464 | tf_op jit(solution)/shard_map/ppermute | solution.py:235
  70.7 5.4 %collective-permute-start.1 = (f32[24,512]{1,0:T(8,128)S(1)}, f32[24,512]{1,0:T(8,128)S(1)}, u32[]{:S(2)}, u32[]{:S(2)}) collective-permute-start(f32[24,512]{1,0:T(8,128)S(1)} %get-tuple-element.12), channel_id=1, source_target_pairs={{0,16},{16,32},{32,48},{48,64},{64,80},{80,96},{96,112},{1,17},{17... | collective-permute-start | bytes 147464 | tf_op jit(solution)/shard_map/ppermute | solution.py:235
  76.3 5.9 %collective-permute-start.2 = (f32[24,384]{1,0:T(8,128)S(1)}, f32[24,384]{1,0:T(8,128)S(1)}, u32[]{:S(2)}, u32[]{:S(2)}) collective-permute-start(f32[24,384]{1,0:T(8,128)S(1)} %get-tuple-element.13), channel_id=1, source_target_pairs={{1,0},{2,1},{3,2},{4,3},{5,4},{6,5},{7,6},{8,7},{9,8},{10,9},{11,1... | collective-permute-start | bytes 110600 | tf_op jit(solution)/shard_map/ppermute | solution.py:235
  77.6 6.2 %collective-permute-start.3 = (f32[24,384]{1,0:T(8,128)S(1)}, f32[24,384]{1,0:T(8,128)S(1)}, u32[]{:S(2)}, u32[]{:S(2)}) collective-permute-start(f32[24,384]{1,0:T(8,128)S(1)} %get-tuple-element.14), channel_id=1, source_target_pairs={{0,1},{1,2},{2,3},{3,4},{4,5},{5,6},{6,7},{7,8},{8,9},{9,10},{10,1... | collective-permute-start | bytes 110600 | tf_op jit(solution)/shard_map/ppermute | solution.py:235
  95.6 16.0 %all-to-all-start.1 = ((f32[16,8,128]{2,1,0:T(8,128)}), f32[16,8,128]{2,1,0:T(8,128)S(1)}, u32[]{:S(2)}, u32[]{:S(2)}) async-start(f32[16,8,128]{2,1,0:T(8,128)} %get-tuple-element.17), calls=%async_computation.1 | async-start | bytes 131072 | tf_op jit(solution)/shard_map/all_to_all | solution.py:314

commit v2 on v1

--- a/solution.py
+++ b/solution.py
@@ -11,6 +11,9 @@
 BLOCK = 72
 HALO = 24
 GAP = 1000.0
+GROUP = 64
+UNROLL = 16
+PARTS = 4
 
 F32 = jnp.float32
 BF16 = jnp.bfloat16
@@ -21,6 +24,10 @@
     return pl.BlockSpec(memory_space=pltpu.VMEM)
 
 
+def hbm():
+    return pl.BlockSpec(memory_space=pltpu.HBM)
+
+
 def smem():
     return pl.BlockSpec(memory_space=pltpu.SMEM)
 
@@ -29,24 +36,54 @@
     return lax.broadcasted_iota(I32, shape, dim)
 
 
-def deal_kernel(heights, owner, segment, out, wide, dealt, slots, ids, slots_s, sem):
+def split(values):
+    terms = []
+    for _ in range(3):
+        term = values.astype(BF16)
+        terms.append(term)
+        values = values - term.astype(F32)
+    return terms
+
+
+def deal_kernel(
+    heights_in,
+    owner_in,
+    segment_in,
+    out,
+    heights,
+    owner,
+    segment,
+    wide,
+    dealt,
+    packed,
+    slots,
+    ids,
+    slots_s,
+    sems,
+):
     devices = out.shape[0]
     rows = heights.shape[0]
     chunks = rows // 128
+    half = chunks // 2
+    loads = [
+        pltpu.make_async_copy(src, dst, sems.at[i])
+        for i, (src, dst) in enumerate(
+            ((owner_in, owner), (segment_in, segment), (heights_in, heights))
+        )
+    ]
+    for load in loads:
+        load.start()
     zeros = jnp.zeros((BLOCK, 128), F32)
 
-    @pl.loop(0, devices)
+    @pl.loop(0, devices, unroll=4)
     def _(t):
         dealt[pl.ds(pl.multiple_of(t * BLOCK, 8), BLOCK), :] = zeros
-
-    @pl.loop(0, rows // 64)
-    def _(c):
-        at = pl.ds(pl.multiple_of(c * 64, 64), 64)
-        wide[at, :] = heights[at, :].astype(F32)
 
     tile = iota((devices, 128), 0)
     before = (iota((128, 256), 0) < iota((128, 256), 1)).astype(F32).astype(BF16)
     place = iota((128, 128), 0) & (CAP - 1)
+    loads[0].wait()
+    loads[1].wait()
 
     def chunk(c, carry):
         seen, named = carry
@@ -66,24 +103,49 @@
         return seen + counts[:, 128:], named
 
     start = jnp.zeros((devices, 128), F32)
-    _, named = lax.fori_loop(0, chunks, chunk, (start, start), unroll=2)
+    carry = lax.fori_loop(0, half, chunk, (start, start), unroll=UNROLL)
+    copies = [
+        pltpu.make_async_copy(
+            slots.at[pl.ds(i * half, half)], slots_s.at[pl.ds(i * half, half)], sems.at[3 + i]
+        )
+        for i in range(2)
+    ]
+    copies[0].start()
+    _, named = lax.fori_loop(half, chunks, chunk, carry, unroll=UNROLL)
     ids[...] = named
-    copy = pltpu.make_async_copy(slots, slots_s, sem)
-    copy.start()
-    copy.wait()
-
-    @pl.loop(0, devices)
+    copies[1].start()
+    loads[2].wait()
+
+    @pl.loop(0, rows // 64, unroll=4)
+    def _(c):
+        at = pl.ds(pl.multiple_of(c * 64, 64), 64)
+        wide[at, :] = heights[at, :].astype(F32)
+
+    @pl.loop(0, devices, unroll=8)
     def _(t):
         dealt[pl.ds(t * BLOCK + CAP, 1), :] = ids[pl.ds(t, 1), :]
 
-    @pl.loop(0, chunks)
-    def _(c):
-        for i in range(128):
-            dealt[pl.ds(slots_s[c, i], 1), :] = wide[pl.ds(c * 128 + i, 1), :]
-
-    @pl.loop(0, devices)
-    def _(t):
-        out[t] = dealt[pl.ds(pl.multiple_of(t * BLOCK, 8), BLOCK), :].astype(BF16)
+    for i in range(2):
+        copies[i].wait()
+
+        @pl.loop(i * half, (i + 1) * half)
+        def _(c):
+            for i in range(128):
+                dealt[pl.ds(slots_s[c, i], 1), :] = wide[pl.ds(c * 128 + i, 1), :]
+
+    part = devices // PARTS
+    stores = []
+    for i in range(PARTS):
+
+        @pl.loop(i * part, (i + 1) * part, unroll=4)
+        def _(t):
+            packed[t] = dealt[pl.ds(pl.multiple_of(t * BLOCK, 8), BLOCK), :].astype(BF16)
+
+        at = pl.ds(i * part, part)
+        stores.append(pltpu.make_async_copy(packed.at[at], out.at[at], sems.at[5 + i]))
+        stores[-1].start()
+    for store in stores:
+        store.wait()
 
 
 def bin_kernel(got, gap_mask, out, first, last, acc, codes, lines):
@@ -103,23 +165,28 @@
     seg = (shift << 7) + (code.astype(I32) >> shift) - 128
     for q in range(quarters):
         lines[q] = jnp.where((code > 0.0) & ((seg & (quarters - 1)) == q), seg // quarters, -1)
-    acc[...] = jnp.zeros(acc.shape, F32)
     line = iota((tile_rows, 128), 0)
-    ones = jnp.ones((256, 128), BF16)
-
-    @pl.loop(0, devices // 4)
-    def _(i):
-        cells = jnp.concatenate([got[4 * i + j][:CAP, :] for j in range(4)], axis=0)
+    ones = jnp.ones((GROUP * CAP, 128), BF16)
+
+    def group(i, fresh):
+        cells = jnp.concatenate([got[GROUP * i + j][:CAP, :] for j in range(GROUP)], axis=0)
         cells = jnp.concatenate([cells, ones], axis=1)
         for q in range(quarters):
             hot = jnp.concatenate(
                 [
-                    (line == lines[q, pl.ds(2 * i + j, 1), :]).astype(F32).astype(BF16)
-                    for j in range(2)
+                    (line == lines[q, pl.ds(GROUP // 2 * i + j, 1), :]).astype(F32).astype(BF16)
+                    for j in range(GROUP // 2)
                 ],
                 axis=1,
             )
-            acc[q] += jnp.dot(hot, cells, preferred_element_type=F32)
+            part = jnp.dot(hot, cells, preferred_element_type=F32)
+            acc[q] = part if fresh else acc[q] + part
+
+    group(0, True)
+
+    @pl.loop(1, devices // GROUP)
+    def _(i):
+        group(i, False)
 
     for q in range(quarters):
         cols = slice(q * 128, (q + 1) * 128)
@@ -131,73 +198,89 @@
     last[...] = out[tile_rows - HALO:, :]
 
 
+def lay_rows(slab, tile, above, below, cols):
+    rows = tile.shape[0]
+    tall = slab.shape[0]
+    slab[:rows, :] = tile[:, cols]
+    slab[rows:rows + HALO, :] = above[:, cols]
+    slab[rows + HALO:tall - HALO, :] = jnp.zeros((tall - rows - 2 * HALO, 128), F32)
+    slab[tall - HALO:, :] = below[:, cols]
+
+
 def sides_kernel(tile, above, below, west, east, slab):
+    cols = tile.shape[1]
+    lanes = slab.shape[0] // 128
+    for out, at, keep in ((west, 0, 0), (east, cols - 128, 128 - HALO)):
+        lay_rows(slab, tile, above, below, slice(at, at + 128))
+        for k in range(lanes):
+            out[k] = slab[pl.ds(k, 128, stride=lanes), :].T[keep:keep + HALO, :]
+
+
+def fill_kernel(
+    tile, above, below, right, left, surface, depths, totals, slabs, turned, cells, keep, rate
+):
     rows, cols = tile.shape
-    slab[...] = jnp.zeros(slab.shape, F32)
-    for out, at, keep in ((west, 0, 0), (east, cols - 128, 128 - HALO)):
-        slab[:rows, :] = tile[:, at:at + 128]
-        slab[rows:rows + HALO, :] = above[:, at:at + 128]
-        slab[rows + HALO:rows + 2 * HALO, :] = below[:, at:at + 128]
-        out[...] = slab[...].T[keep:keep + HALO, :]
-
-
-def fill_kernel(tile, above, below, right, left, surface, depths, totals, cells, rate):
-    rows, cols = tile.shape
-    wide = cols + 128
-    tall = rows + 2 * HALO
-
-    def put(at, width, values):
-        unknown = values > 0.5 * GAP
-        cells[at, width] = jnp.where(unknown, 0.0, values)
-        rate[at, width] = jnp.where(unknown, 0.9, 0.0)
-
-    put(slice(0, rows), slice(0, cols), tile[...])
-    put(slice(rows, rows + HALO), slice(0, cols), above[...])
-    put(slice(rows + HALO, tall), slice(0, cols), below[...])
-    beside = jnp.concatenate(
-        [right[...], jnp.zeros((128 - 2 * HALO, right.shape[1]), F32), left[...]], axis=0
-    ).T
-    put(slice(0, tall), slice(cols, wide), beside[:tall, :])
-
-    blocks = tall // 8
-    top = iota((8, wide), 0) == 0
-    bottom = iota((8, wide), 0) == 7
+    quarters = cols // 128
+    lanes, long, _ = turned.shape
+    deep = long // 8
+
+    for q in range(quarters):
+        at = slice(q * 128, (q + 1) * 128)
+        lay_rows(slabs.at[q], tile, above, below, at)
+        for k in range(lanes):
+            turned[k, at, :] = slabs[q, pl.ds(k, 128, stride=lanes), :].T
+    for k in range(lanes):
+        turned[k, cols:cols + HALO, :] = right[k]
+        turned[k, cols + HALO:, :] = left[k]
+    for v in range(deep):
+        for k in range(lanes):
+            values = turned[k, pl.ds(v, 8, stride=deep), :]
+            unknown = values > 0.5 * GAP
+            cells[v, k] = jnp.where(unknown, 0.0, values)
+            keep[v, k] = jnp.where(unknown, 1.0 - 0.9, 1.0)
+            rate[v, k] = jnp.where(unknown, 0.9 * 0.25, 0.0)
 
     def step(_, carry):
-        def block(b):
-            return cells[b * 8:b * 8 + 8, :]
-
-        opening = block(0)
-        lower_0 = pltpu.roll(opening, 7, axis=0)
-        before = pltpu.roll(block(blocks - 1), 1, axis=0)
-        here, here_up = opening, lower_0
-        for b in range(blocks):
-            if b + 1 < blocks:
-                after = block(b + 1)
-                after_up = pltpu.roll(after, 7, axis=0)
+        opening = [cells[0, k] for k in range(lanes)]
+        before = [pltpu.roll(cells[deep - 1, k], 1, axis=0) for k in range(lanes)]
+        here = opening
+        for v in range(deep):
+            if v + 1 < deep:
+                after = [cells[v + 1, k] for k in range(lanes)]
             else:
-                after, after_up = opening, lower_0
-            here_down = pltpu.roll(here, 1, axis=0)
-            total = jnp.where(top, before, here_down) + jnp.where(bottom, after_up, here_up)
-            total = total + (pltpu.roll(here, 1, axis=1) + pltpu.roll(here, wide - 1, axis=1))
-            cells[b * 8:b * 8 + 8, :] = here + rate[b * 8:b * 8 + 8, :] * (0.25 * total - here)
-            before, here, here_up = here_down, after, after_up
+                after = [pltpu.roll(values, 7, axis=0) for values in opening]
+            lower = [pltpu.roll(here[-1], 1, axis=1)] + here[:-1]
+            upper = here[1:] + [pltpu.roll(here[0], 127, axis=1)]
+            for k in range(lanes):
+                total = (before[k] + after[k]) + (lower[k] + upper[k])
+                cells[v, k] = keep[v, k] * here[k] + rate[v, k] * total
+            before, here = here, after
         return carry
 
     lax.fori_loop(0, STEPS, step, 0)
-    final = cells[:rows, :cols]
-    surface[...] = final
+
+    for v in range(deep):
+        for k in range(lanes):
+            turned[k, pl.ds(v, 8, stride=deep), :] = cells[v, k]
+    for q in range(quarters):
+        at = slice(q * 128, (q + 1) * 128)
+        for k in range(lanes):
+            slabs[q, pl.ds(k, 128, stride=lanes), :] = turned[k, at, :].T
+        surface[:, at] = slabs[q, :rows, :]
+    final = surface[...]
     soft = jnp.maximum(final, 0.0) + jnp.log1p(jnp.exp(-jnp.abs(final)))
-    ahead = (iota((cols, cols), 0) < iota((cols, cols), 1)).astype(F32)
-    south = jnp.dot(soft, ahead, precision=lax.Precision.HIGHEST, preferred_element_type=F32)
-    whole = jnp.sum(soft, axis=1, keepdims=True)
+    ahead = (iota((cols, cols), 0) < iota((cols, cols), 1)).astype(F32).astype(BF16)
+    ones = jnp.ones((8, cols), BF16)
+    south = jnp.zeros((rows, cols), F32)
+    along = jnp.zeros((8, rows), F32)
+    for term in reversed(split(soft)):
+        south = south + jnp.dot(term, ahead, preferred_element_type=F32)
+        along = along + lax.dot_general(
+            ones, term, (((1,), (1,)), ((), ())), preferred_element_type=F32
+        )
+    whole = south[:, cols - 1:] + soft[:, cols - 1:]
     depths[0] = south
     depths[1] = (whole - south) - soft
-    ones = jnp.ones((8, cols), F32)
-    along = lax.dot_general(
-        ones, soft, (((1,), (1,)), ((), ())), precision=lax.Precision.HIGHEST,
-        preferred_element_type=F32,
-    )
     packed = jnp.where(iota((8, 128), 0) == 0, along[:, :128], along[:, 128:])
     for n in range(totals.shape[0]):
         totals[n] = packed
@@ -224,10 +307,10 @@
                 )
 
     pick = side[s]
-    rate = -(extinction[s] / (cols * count))
+    rate = extinction[s] * (-1.4426950408889634 / (cols * count))
     for q in range(cols // 128):
         at = slice(q * 128, (q + 1) * 128)
-        out[0, :, at] = jnp.exp(rate * (depths[pick, :, at] + carried[pick]))
+        out[0, :, at] = jnp.exp2(rate * (depths[pick, :, at] + carried[pick]))
 
 
 def moved(values, axis, hop):
@@ -243,23 +326,28 @@
     n_north = lax.axis_size("north")
     devices = lax.axis_size("east") * n_north
     chunks = rows_here // 128
-    tall = tile_rows + 128
+    lanes = -(-(tile_rows + 2 * HALO) // 128)
+    long = tile_cols + 2 * HALO
     mib = 1 << 20
 
     dealt = pl.pallas_call(
         deal_kernel,
         out_shape=jax.ShapeDtypeStruct((devices, BLOCK, 128), BF16),
-        in_specs=[vmem()] * 3,
-        out_specs=vmem(),
+        in_specs=[hbm()] * 3,
+        out_specs=hbm(),
         scratch_shapes=[
+            pltpu.VMEM((rows_here, 128), BF16),
+            pltpu.VMEM((chunks, 128), I32),
+            pltpu.VMEM((chunks, 128), I32),
             pltpu.VMEM((rows_here, 128), F32),
             pltpu.VMEM((devices * BLOCK, 128), F32),
+            pltpu.VMEM((devices, BLOCK, 128), BF16),
             pltpu.VMEM((chunks, 128), I32),
             pltpu.VMEM((devices, 128), F32),
             pltpu.SMEM((chunks, 128), I32),
-            pltpu.SemaphoreType.DMA,
+            pltpu.SemaphoreType.DMA((5 + PARTS,)),
         ],
-        compiler_params=pltpu.CompilerParams(vmem_limit_bytes=24 * mib),
+        compiler_params=pltpu.CompilerParams(vmem_limit_bytes=60 * mib),
         name="deal",
     )(heights, tile_owner.reshape(chunks, 128), segment_ids.reshape(chunks, 128))
 
@@ -283,13 +371,13 @@
     below = moved(last, "east", 1)
     above = moved(first, "east", -1)
 
-    turned = jax.ShapeDtypeStruct((HALO, tall), F32)
+    turned = jax.ShapeDtypeStruct((lanes, HALO, 128), F32)
     west, east = pl.pallas_call(
         sides_kernel,
         out_shape=(turned, turned),
         in_specs=[vmem()] * 3,
         out_specs=(vmem(),) * 2,
-        scratch_shapes=[pltpu.VMEM((tall, 128), F32)],
+        scratch_shapes=[pltpu.VMEM((lanes * 128, 128), F32)],
         compiler_params=pltpu.CompilerParams(vmem_limit_bytes=16 * mib),
         name="sides",
     )(tile, above, below)
@@ -306,7 +394,11 @@
         ),
         in_specs=[vmem()] * 5,
         out_specs=(vmem(),) * 3,
-        scratch_shapes=[pltpu.VMEM((tile_rows + 2 * HALO, tile_cols + 128), F32)] * 2,
+        scratch_shapes=[
+            pltpu.VMEM((tile_cols // 128, lanes * 128, 128), F32),
+            pltpu.VMEM((lanes, long, 128), F32),
+        ]
+        + [pltpu.VMEM((long // 8, lanes, 8, 128), F32)] * 3,
         compiler_params=pltpu.CompilerParams(vmem_limit_bytes=32 * mib),
         name="fill",
     )(tile, above, below, right, left)

time: 117 us -> 98.8 us (0.84)
  Pallas kernels: 39.3 us -> 24 us
  local copies, waits for them, and re-layouts: 2.67 us -> 0.01 us
    pallas_call x1, Pallas kernels: 9.99 us -> 4.53 us  [body(): pl.pallas_call(bin_kernel, out_shape=(jax.ShapeDtypeStruct((tile_rows, ti...]
    pallas_call x1, Pallas kernels: 12.8 us -> 7.71 us  [body(): pl.pallas_call(deal_kernel, out_shape=jax.ShapeDtypeStruct((devices, BLOC...]
    pallas_call x1, Pallas kernels: 11.8 us -> 7.03 us  [body(): pl.pallas_call(fill_kernel, out_shape=(jax.ShapeDtypeStruct((tile_rows, t...]
    unnamed x12 -> x6, local copies, waits for them, and re-layouts: 2.67 us -> 0.01 us
where the time goes in v2:
time: 98.8 us; the launch traced here: 98.4 us
  blocking collectives  42.9 us (43%)
  Pallas kernels  24 us (24%)
  starting transfers between devices  18.5 us (19%)
  waiting for transfers between devices  12.3 us (12%)
    all_to_all x1, blocking collectives, body(): lax.all_to_all(dealt, ('east', 'north'), split_axis=0, concat_axis=0, til...  42.9 us
    ppermute x4, starting transfers between devices, moved(): lax.ppermute(values, axis, [(i, i + hop) for i in range(count) if 0 <= i...  10.2 us
    all_to_all x1, starting transfers between devices, body(): lax.all_to_all(totals, 'north', split_axis=0, concat_axis=0, tiled=True)  8.32 us
    pallas_call x1, Pallas kernels, body(): pl.pallas_call(deal_kernel, out_shape=jax.ShapeDtypeStruct((devices, BLOC...  7.71 us
    all_to_all x1, waiting for transfers between devices, body(): lax.all_to_all(totals, 'north', split_axis=0, concat_axis=0, tiled=True)  7.66 us
    pallas_call x1, Pallas kernels, body(): pl.pallas_call(fill_kernel, out_shape=(jax.ShapeDtypeStruct((tile_rows, t...  7.03 us
    ppermute x4, waiting for transfers between devices, moved(): lax.ppermute(values, axis, [(i, i + hop) for i in range(count) if 0 <= i...  4.6 us
    pallas_call x1, Pallas kernels, body(): pl.pallas_call(light_kernel, grid=(NS,), out_shape=jax.ShapeDtypeStruct((...  4.57 us
  transfers between devices with their start and end apart: 5, of which 3 were waited for; matrix products, arithmetic and copies ran while one was open for 0% of the time, Pallas kernels for 0%

profile of v2, /device:TPU:2, one launch (start us, length us, event | category | flops | bytes accessed | tf_op | source)
XLA Modules:
  0.0 98.4 jit_solution(4795088694053069066)
XLA Ops:
  0.6 7.7 %deal.1 = bf16[128,72,128]{2,1,0:T(8,128)(2,1)} custom-call(bf16[4096,128]{1,0:T(8,128)(2,1)} %heights_in.1, s32[32,128]{1,0:T(8,128)} %bitcast.3, s32[32,128]{1,0:T(8,128)} %bitcast.4), custom_call_target="tpu_custom_call" | custom-call | tf_op jit(solution)/shard_map/deal/pallas_call | solution.py:333
  8.3 0.0 copy-start
  8.4 42.9 %all_to_all.10.got = bf16[128,72,128]{2,1,0:T(8,128)(2,1)S(1)} all-to-all(bf16[128,72,128]{2,1,0:T(8,128)(2,1)} %deal.1), channel_id=1, replica_groups=mesh['east'=8,'north'=16] {'east','north'}, dimensions={0} | all-to-all | bytes 4718592 | tf_op jit(solution)/shard_map/all_to_all | solution.py:354
  51.3 0.0 copy-done
  51.3 0.0 copy-start.1
  51.3 0.0 copy-start.2
  51.3 4.5 %bin.1 = (f32[256,512]{1,0:T(8,128)S(1)}, f32[24,512]{1,0:T(8,128)S(1)}, f32[24,512]{1,0:T(8,128)S(1)}) custom-call(bf16[128,72,128]{2,1,0:T(8,128)(2,1)S(1)} %all_to_all.10.got, s32[256,512]{1,0:T(8,128)S(1)} %copy-done), custom_call_target="tpu_custom_call" | custom-call | tf_op jit(solution)/shard_map/bin/pallas_call | solution.py:357
  55.8 1.9 %collective-permute-start = (f32[24,512]{1,0:T(8,128)S(1)}, f32[24,512]{1,0:T(8,128)S(1)}, u32[]{:S(2)}, u32[]{:S(2)}) collective-permute-start(f32[24,512]{1,0:T(8,128)S(1)} %get-tuple-element.11), channel_id=1, source_target_pairs={{16,0},{32,16},{48,32},{64,48},{80,64},{96,80},{112,96},{17,1},{33... | collective-permute-start | bytes 147464 | tf_op jit(solution)/shard_map/ppermute | solution.py:318
  57.7 2.4 %collective-permute-start.1 = (f32[24,512]{1,0:T(8,128)S(1)}, f32[24,512]{1,0:T(8,128)S(1)}, u32[]{:S(2)}, u32[]{:S(2)}) collective-permute-start(f32[24,512]{1,0:T(8,128)S(1)} %get-tuple-element.12), channel_id=1, source_target_pairs={{0,16},{16,32},{32,48},{48,64},{64,80},{80,96},{96,112},{1,17},{17... | collective-permute-start | bytes 147464 | tf_op jit(solution)/shard_map/ppermute | solution.py:318
  60.2 0.0 collective-permute-done.above
  60.2 3.0 %collective-permute-done.1.below = f32[24,512]{1,0:T(8,128)S(1)} collective-permute-done((f32[24,512]{1,0:T(8,128)S(1)}, f32[24,512]{1,0:T(8,128)S(1)}, u32[]{:S(2)}, u32[]{:S(2)}) %collective-permute-start.1) | collective-permute-done | bytes 49184 | tf_op jit(solution)/shard_map/ppermute | solution.py:318
  63.1 0.2 sides.1
  63.3 1.3 %collective-permute-start.2 = (f32[3,24,128]{2,1,0:T(8,128)S(1)}, f32[3,24,128]{2,1,0:T(8,128)S(1)}, u32[]{:S(2)}, u32[]{:S(2)}) collective-permute-start(f32[3,24,128]{2,1,0:T(8,128)S(1)} %get-tuple-element.13), channel_id=1, source_target_pairs={{1,0},{2,1},{3,2},{4,3},{5,4},{6,5},{7,6},{8,7},{9,8},{10,9},{11,1... | collective-permute-start | bytes 110600 | tf_op jit(solution)/shard_map/ppermute | solution.py:318
  64.6 4.5 %collective-permute-start.3 = (f32[3,24,128]{2,1,0:T(8,128)S(1)}, f32[3,24,128]{2,1,0:T(8,128)S(1)}, u32[]{:S(2)}, u32[]{:S(2)}) collective-permute-start(f32[3,24,128]{2,1,0:T(8,128)S(1)} %get-tuple-element.14), channel_id=1, source_target_pairs={{0,1},{1,2},{2,3},{3,4},{4,5},{5,6},{6,7},{7,8},{8,9},{9,10},{10,1... | collective-permute-start | bytes 110600 | tf_op jit(solution)/shard_map/ppermute | solution.py:318
  69.2 0.0 collective-permute-done.2.right
  69.2 1.6 %collective-permute-done.3.left = f32[3,24,128]{2,1,0:T(8,128)S(1)} collective-permute-done((f32[3,24,128]{2,1,0:T(8,128)S(1)}, f32[3,24,128]{2,1,0:T(8,128)S(1)}, u32[]{:S(2)}, u32[]{:S(2)}) %collective-permute-start.3) | collective-permute-done | bytes 36896 | tf_op jit(solution)/shard_map/ppermute | solution.py:318
  70.8 7.0 %fill.1 = (f32[256,512]{1,0:T(8,128)}, f32[2,256,512]{2,1,0:T(8,128)S(1)}, f32[16,8,128]{2,1,0:T(8,128)}) custom-call(f32[256,512]{1,0:T(8,128)S(1)} %get-tuple-element.10.tile, f32[24,512]{1,0:T(8,128)S(1)} %collective-permute-done.above, f32[24,512]{1,0:T(8,128)S(1)} %collective-permute-done.1.below, f32[3,24,128]{2,1,0:T(8,128)S(1)} %collective-permute-done.2.right, ...), custom_call_target="tpu_custom_call" | custom-call | tf_op jit(solution)/shard_map/fill/pallas_call | solution.py:388
  77.8 8.3 %all-to-all-start.1 = ((f32[16,8,128]{2,1,0:T(8,128)}), f32[16,8,128]{2,1,0:T(8,128)S(1)}, u32[]{:S(2)}, u32[]{:S(2)}) async-start(f32[16,8,128]{2,1,0:T(8,128)} %get-tuple-element.17), calls=%async_computation.1 | async-start | bytes 131072 | tf_op jit(solution)/shard_map/all_to_all | solution.py:406
  86.2 7.7 %all-to-all-done.1.totals = f32[16,8,128]{2,1,0:T(8,128)S(1)} async-done(((f32[16,8,128]{2,1,0:T(8,128)}), f32[16,8,128]{2,1,0:T(8,128)S(1)}, u32[]{:S(2)}, u32[]{:S(2)}) %all-to-all-start.1) | async-done | bytes 65568 | tf_op jit(solution)/shard_map/all_to_all | solution.py:406
  93.8 0.0 copy-done.1
  93.8 0.0 copy-done.2
  93.8 4.6 %light.1 = f32[8,256,512]{2,1,0:T(8,128)} custom-call(s32[1]{0:T(128)} %bitcast.2.place, f32[8]{0:T(128)S(1)} %copy-done.1, s32[8]{0:T(128)S(1)} %copy-done.2, f32[2,256,512]{2,1,0:T(8,128)S(1)} %get-tuple-element.16.depths, f32[16,8,128]{2,1,0:T(8,128)S(1)} %all-to-all-done.1.totals), custom_call_target="tpu_custom_call" | custom-call | tf_op jit(solution)/shard_map/light/pallas_call | solution.py:409
Async XLA Ops:
  8.3 42.9 %copy-start = (s32[256,512]{1,0:T(8,128)S(1)}, s32[256,512]{1,0:T(8,128)}, u32[]{:S(2)}) copy-start(s32[256,512]{1,0:T(8,128)} %gap_mask.1) | copy-start | bytes 1572868
  51.3 42.6 %copy-start.1 = (f32[8]{0:T(128)S(1)}, f32[8]{0:T(128)}, u32[]{:S(2)}) copy-start(f32[8]{0:T(128)} %extinction.1) | copy-start | bytes 100
  51.3 42.6 %copy-start.2 = (s32[8]{0:T(128)S(1)}, s32[8]{0:T(128)}, u32[]{:S(2)}) copy-start(s32[8]{0:T(128)} %side.1) | copy-start | bytes 100
  55.8 4.3 %collective-permute-start = (f32[24,512]{1,0:T(8,128)S(1)}, f32[24,512]{1,0:T(8,128)S(1)}, u32[]{:S(2)}, u32[]{:S(2)}) collective-permute-start(f32[24,512]{1,0:T(8,128)S(1)} %get-tuple-element.11), channel_id=1, source_target_pairs={{16,0},{32,16},{48,32},{64,48},{80,64},{96,80},{112,96},{17,1},{33... | collective-permute-start | bytes 147464 | tf_op jit(solution)/shard_map/ppermute | solution.py:318
  57.7 5.4 %collective-permute-start.1 = (f32[24,512]{1,0:T(8,128)S(1)}, f32[24,512]{1,0:T(8,128)S(1)}, u32[]{:S(2)}, u32[]{:S(2)}) collective-permute-start(f32[24,512]{1,0:T(8,128)S(1)} %get-tuple-element.12), channel_id=1, source_target_pairs={{0,16},{16,32},{32,48},{48,64},{64,80},{80,96},{96,112},{1,17},{17... | collective-permute-start | bytes 147464 | tf_op jit(solution)/shard_map/ppermute | solution.py:318
  63.3 5.9 %collective-permute-start.2 = (f32[3,24,128]{2,1,0:T(8,128)S(1)}, f32[3,24,128]{2,1,0:T(8,128)S(1)}, u32[]{:S(2)}, u32[]{:S(2)}) collective-permute-start(f32[3,24,128]{2,1,0:T(8,128)S(1)} %get-tuple-element.13), channel_id=1, source_target_pairs={{1,0},{2,1},{3,2},{4,3},{5,4},{6,5},{7,6},{8,7},{9,8},{10,9},{11,1... | collective-permute-start | bytes 110600 | tf_op jit(solution)/shard_map/ppermute | solution.py:318
  64.6 6.2 %collective-permute-start.3 = (f32[3,24,128]{2,1,0:T(8,128)S(1)}, f32[3,24,128]{2,1,0:T(8,128)S(1)}, u32[]{:S(2)}, u32[]{:S(2)}) collective-permute-start(f32[3,24,128]{2,1,0:T(8,128)S(1)} %get-tuple-element.14), channel_id=1, source_target_pairs={{0,1},{1,2},{2,3},{3,4},{4,5},{5,6},{6,7},{7,8},{8,9},{9,10},{10,1... | collective-permute-start | bytes 110600 | tf_op jit(solution)/shard_map/ppermute | solution.py:318
  77.8 16.0 %all-to-all-start.1 = ((f32[16,8,128]{2,1,0:T(8,128)}), f32[16,8,128]{2,1,0:T(8,128)S(1)}, u32[]{:S(2)}, u32[]{:S(2)}) async-start(f32[16,8,128]{2,1,0:T(8,128)} %get-tuple-element.17), calls=%async_computation.1 | async-start | bytes 131072 | tf_op jit(solution)/shard_map/all_to_all | solution.py:406

commit v3 on v2

--- a/solution.py
+++ b/solution.py
@@ -12,8 +12,10 @@
 HALO = 24
 GAP = 1000.0
 GROUP = 64
-UNROLL = 16
+TEAM = 8
+DELAY = 2
 PARTS = 4
+PIECES = 1
 
 F32 = jnp.float32
 BF16 = jnp.bfloat16
@@ -64,7 +66,7 @@
     devices = out.shape[0]
     rows = heights.shape[0]
     chunks = rows // 128
-    half = chunks // 2
+    groups = chunks // TEAM
     loads = [
         pltpu.make_async_copy(src, dst, sems.at[i])
         for i, (src, dst) in enumerate(
@@ -85,35 +87,40 @@
     loads[0].wait()
     loads[1].wait()
 
-    def chunk(c, carry):
+    def rank_team(g, carry):
         seen, named = carry
-        own = owner[pl.ds(c, 1), :]
-        hit = tile == own
-        counts = jnp.dot(hit.astype(F32).astype(BF16), before, preferred_element_type=F32)
-        rank = jnp.sum(jnp.where(hit, counts[:, :128] + seen, 0.0), axis=0, keepdims=True)
-        rank = rank.astype(I32)
-        slots[pl.ds(c, 1), :] = own * BLOCK + rank
-        seg = segment[pl.ds(c, 1), :]
-        code = (((seg & 127) + 128) << (seg >> 7)).astype(F32)
-        coded = jnp.where(hit, jnp.broadcast_to(code, hit.shape), 0.0).astype(BF16)
-        ranked = (place == rank).astype(F32).astype(BF16)
-        named = named + lax.dot_general(
-            coded, ranked, (((1,), (1,)), ((), ())), preferred_element_type=F32
-        )
-        return seen + counts[:, 128:], named
+        for i in range(TEAM):
+            c = g * TEAM + i
+            own = owner[pl.ds(c, 1), :]
+            hit = tile == own
+            counts = jnp.dot(hit.astype(F32).astype(BF16), before, preferred_element_type=F32)
+            rank = jnp.sum(jnp.where(hit, counts[:, :128] + seen, 0.0), axis=0, keepdims=True)
+            rank = rank.astype(I32)
+            slots[g, i:i + 1, :] = own * BLOCK + rank
+            seg = segment[pl.ds(c, 1), :]
+            code = (((seg & 127) + 128) << (seg >> 7)).astype(F32)
+            coded = jnp.where(hit, jnp.broadcast_to(code, hit.shape), 0.0).astype(BF16)
+            ranked = (place == rank).astype(F32).astype(BF16)
+            named = named + lax.dot_general(
+                coded, ranked, (((1,), (1,)), ((), ())), preferred_element_type=F32
+            )
+            seen = seen + counts[:, 128:]
+        return seen, named
+
+    def copy_slots(g):
+        return pltpu.make_async_copy(slots.at[g], slots_s.at[g], sems.at[3 + lax.rem(g, DELAY)])
+
+    def place_team(g):
+        for i in range(TEAM):
+            for j in range(128):
+                row = g * (TEAM * 128) + (i * 128 + j)
+                dealt[pl.ds(slots_s[g, i, j], 1), :] = wide[pl.ds(row, 1), :]
 
     start = jnp.zeros((devices, 128), F32)
-    carry = lax.fori_loop(0, half, chunk, (start, start), unroll=UNROLL)
-    copies = [
-        pltpu.make_async_copy(
-            slots.at[pl.ds(i * half, half)], slots_s.at[pl.ds(i * half, half)], sems.at[3 + i]
-        )
-        for i in range(2)
-    ]
-    copies[0].start()
-    _, named = lax.fori_loop(half, chunks, chunk, carry, unroll=UNROLL)
-    ids[...] = named
-    copies[1].start()
+    carry = start, start
+    for g in range(DELAY):
+        carry = rank_team(g, carry)
+        copy_slots(g).start()
     loads[2].wait()
 
     @pl.loop(0, rows // 64, unroll=4)
@@ -121,17 +128,23 @@
         at = pl.ds(pl.multiple_of(c * 64, 64), 64)
         wide[at, :] = heights[at, :].astype(F32)
 
+    def overlap(g, carry):
+        copy_slots(g - DELAY).wait()
+        place_team(g - DELAY)
+        carry = rank_team(g, carry)
+        copy_slots(g).start()
+        return carry
+
+    _, named = lax.fori_loop(DELAY, groups, overlap, carry)
+    ids[...] = named
+
     @pl.loop(0, devices, unroll=8)
     def _(t):
         dealt[pl.ds(t * BLOCK + CAP, 1), :] = ids[pl.ds(t, 1), :]
 
-    for i in range(2):
-        copies[i].wait()
-
-        @pl.loop(i * half, (i + 1) * half)
-        def _(c):
-            for i in range(128):
-                dealt[pl.ds(slots_s[c, i], 1), :] = wide[pl.ds(c * 128 + i, 1), :]
+    for g in range(groups - DELAY, groups):
+        copy_slots(g).wait()
+        place_team(g)
 
     part = devices // PARTS
     stores = []
@@ -142,13 +155,13 @@
             packed[t] = dealt[pl.ds(pl.multiple_of(t * BLOCK, 8), BLOCK), :].astype(BF16)
 
         at = pl.ds(i * part, part)
-        stores.append(pltpu.make_async_copy(packed.at[at], out.at[at], sems.at[5 + i]))
+        stores.append(pltpu.make_async_copy(packed.at[at], out.at[at], sems.at[3 + DELAY + i]))
         stores[-1].start()
     for store in stores:
         store.wait()
 
 
-def bin_kernel(got, gap_mask, out, first, last, acc, codes, lines):
+def bin_kernel(got, gap_mask, out, one, two, acc, codes, lines):
     devices = got.shape[0]
     tile_rows, tile_cols = gap_mask.shape
     quarters = tile_cols // 128
@@ -194,8 +207,10 @@
         summed, counted = total[:, :128], total[:, 128:]
         unknown = (gap_mask[:, cols] == 1) | (counted == 0.0)
         out[:, cols] = jnp.where(unknown, GAP, summed / jnp.maximum(counted, 1.0))
-    first[...] = out[:HALO, :]
-    last[...] = out[tile_rows - HALO:, :]
+    odd = lax.axis_index("east") % 2 == 1
+    first, last = out[:HALO, :], out[tile_rows - HALO:, :]
+    one[...] = jnp.where(odd, last, first)
+    two[...] = jnp.where(odd, first, last)
 
 
 def lay_rows(slab, tile, above, below, cols):
@@ -207,19 +222,51 @@
     slab[tall - HALO:, :] = below[:, cols]
 
 
-def sides_kernel(tile, above, below, west, east, slab):
+def upper_lower(axis, one, two):
+    odd = lax.axis_index(axis) % 2 == 1
+    return jnp.where(odd, one, two), jnp.where(odd, two, one)
+
+
+def sides_kernel(tile, got_one, got_two, one, two, slab):
     cols = tile.shape[1]
     lanes = slab.shape[0] // 128
-    for out, at, keep in ((west, 0, 0), (east, cols - 128, 128 - HALO)):
+    above, below = upper_lower("east", got_one[...], got_two[...])
+    odd = lax.axis_index("north") % 2 == 1
+    strips = []
+    for at, keep in ((0, 0), (cols - 128, 128 - HALO)):
         lay_rows(slab, tile, above, below, slice(at, at + 128))
-        for k in range(lanes):
-            out[k] = slab[pl.ds(k, 128, stride=lanes), :].T[keep:keep + HALO, :]
+        strips.append(
+            [
+                slab[pl.ds(k, 128, stride=lanes), :].T[keep:keep + HALO, :]
+                for k in range(lanes)
+            ]
+        )
+    for k in range(lanes):
+        west, east = strips[0][k], strips[1][k]
+        one[k] = jnp.where(odd, east, west)
+        two[k] = jnp.where(odd, west, east)
 
 
 def fill_kernel(
-    tile, above, below, right, left, surface, depths, totals, slabs, turned, cells, keep, rate
+    tile,
+    east_one,
+    east_two,
+    north_one,
+    north_two,
+    surface_out,
+    depths,
+    totals,
+    surface,
+    slabs,
+    turned,
+    cells,
+    keep,
+    rate,
+    sem,
 ):
     rows, cols = tile.shape
+    above, below = upper_lower("east", east_one[...], east_two[...])
+    right, left = upper_lower("north", north_one[...], north_two[...])
     quarters = cols // 128
     lanes, long, _ = turned.shape
     deep = long // 8
@@ -267,6 +314,8 @@
         for k in range(lanes):
             slabs[q, pl.ds(k, 128, stride=lanes), :] = turned[k, at, :].T
         surface[:, at] = slabs[q, :rows, :]
+    store = pltpu.make_async_copy(surface, surface_out, sem)
+    store.start()
     final = surface[...]
     soft = jnp.maximum(final, 0.0) + jnp.log1p(jnp.exp(-jnp.abs(final)))
     ahead = (iota((cols, cols), 0) < iota((cols, cols), 1)).astype(F32).astype(BF16)
@@ -284,40 +333,52 @@
     packed = jnp.where(iota((8, 128), 0) == 0, along[:, :128], along[:, 128:])
     for n in range(totals.shape[0]):
         totals[n] = packed
-
-
-def light_kernel(place, extinction, side, depths, totals, out, carried):
-    s = pl.program_id(0)
-    _, rows, cols = depths.shape
-    count = totals.shape[0]
-
-    @pl.when(s == 0)
-    def _():
-        here = place[0]
-        zero = jnp.zeros((8, 128), F32)
-        for k in range(2):
-            total = zero
-            for n in range(count):
-                counts = here < n if k else here > n
-                total = total + jnp.where(counts, totals[n], zero)
-            turned = jnp.concatenate([total, jnp.zeros((120, 128), F32)], axis=0).T
-            for half in range(rows // 128):
-                carried[k, half * 128:(half + 1) * 128, :] = jnp.broadcast_to(
-                    turned[:, half:half + 1], (128, 128)
+    store.wait()
+
+
+def light_kernel(extinction, side, depths, totals, out, light, carried, sems):
+    count, rows, cols = light.shape
+    n_north = totals.shape[0]
+    here = lax.axis_index("north")
+    zero = jnp.zeros((8, 128), F32)
+    for k in range(2):
+        total = zero
+        for n in range(n_north):
+            counts = here < n if k else here > n
+            total = total + jnp.where(counts, totals[n], zero)
+        turned = jnp.concatenate([total, jnp.zeros((120, 128), F32)], axis=0).T
+        for half in range(rows // 128):
+            carried[k, half * 128:(half + 1) * 128, :] = jnp.broadcast_to(
+                turned[:, half:half + 1], (128, 128)
+            )
+
+    def store(s, i):
+        at = pl.ds(i * (rows // PIECES), rows // PIECES)
+        return pltpu.make_async_copy(light.at[s, at], out.at[s, at], sems.at[s, i])
+
+    @pl.loop(0, count)
+    def _(s):
+        pick = side[s]
+        rate = extinction[s] * (-1.4426950408889634 / (cols * n_north))
+        for i in range(PIECES):
+            tall = slice(i * (rows // PIECES), (i + 1) * (rows // PIECES))
+            for q in range(cols // 128):
+                at = slice(q * 128, (q + 1) * 128)
+                light[s, tall, at] = jnp.exp2(
+                    rate * (depths[pick, tall, at] + carried[pick, tall, :])
                 )
-
-    pick = side[s]
-    rate = extinction[s] * (-1.4426950408889634 / (cols * count))
-    for q in range(cols // 128):
-        at = slice(q * 128, (q + 1) * 128)
-        out[0, :, at] = jnp.exp2(rate * (depths[pick, :, at] + carried[pick]))
-
-
-def moved(values, axis, hop):
+            store(s, i).start()
+
+    @pl.loop(0, count)
+    def _(s):
+        for i in range(PIECES):
+            store(s, i).wait()
+
+
+def swapped(values, axis, start):
     count = lax.axis_size(axis)
-    return lax.ppermute(
-        values, axis, [(i, i + hop) for i in range(count) if 0 <= i + hop < count]
-    )
+    edges = [(i, i + 1) for i in range(start, count - 1, 2)]
+    return lax.ppermute(values, axis, edges + [(j, i) for i, j in edges])
 
 
 def body(heights, segment_ids, tile_owner, gap_mask, extinction, sun_side):
@@ -342,10 +403,10 @@
             pltpu.VMEM((rows_here, 128), F32),
             pltpu.VMEM((devices * BLOCK, 128), F32),
             pltpu.VMEM((devices, BLOCK, 128), BF16),
-            pltpu.VMEM((chunks, 128), I32),
+            pltpu.VMEM((chunks // TEAM, 8, 128), I32),
             pltpu.VMEM((devices, 128), F32),
-            pltpu.SMEM((chunks, 128), I32),
-            pltpu.SemaphoreType.DMA((5 + PARTS,)),
+            pltpu.SMEM((chunks // TEAM, 8, 128), I32),
+            pltpu.SemaphoreType.DMA((3 + DELAY + PARTS,)),
         ],
         compiler_params=pltpu.CompilerParams(vmem_limit_bytes=60 * mib),
         name="deal",
@@ -354,7 +415,7 @@
     got = lax.all_to_all(dealt, ("east", "north"), split_axis=0, concat_axis=0, tiled=True)
 
     strip = jax.ShapeDtypeStruct((HALO, tile_cols), F32)
-    tile, first, last = pl.pallas_call(
+    tile, one, two = pl.pallas_call(
         bin_kernel,
         out_shape=(jax.ShapeDtypeStruct((tile_rows, tile_cols), F32), strip, strip),
         in_specs=[vmem()] * 2,
@@ -368,11 +429,10 @@
         name="bin",
     )(got, gap_mask)
 
-    below = moved(last, "east", 1)
-    above = moved(first, "east", -1)
+    east = swapped(one, "east", 1), swapped(two, "east", 0)
 
     turned = jax.ShapeDtypeStruct((lanes, HALO, 128), F32)
-    west, east = pl.pallas_call(
+    one, two = pl.pallas_call(
         sides_kernel,
         out_shape=(turned, turned),
         in_specs=[vmem()] * 3,
@@ -380,10 +440,9 @@
         scratch_shapes=[pltpu.VMEM((lanes * 128, 128), F32)],
         compiler_params=pltpu.CompilerParams(vmem_limit_bytes=16 * mib),
         name="sides",
-    )(tile, above, below)
-
-    left = moved(east, "north", 1)
-    right = moved(west, "north", -1)
+    )(tile, *east)
+
+    north = swapped(one, "north", 1), swapped(two, "north", 0)
 
     surface, depths, totals = pl.pallas_call(
         fill_kernel,
@@ -393,29 +452,32 @@
             jax.ShapeDtypeStruct((n_north, 8, 128), F32),
         ),
         in_specs=[vmem()] * 5,
-        out_specs=(vmem(),) * 3,
+        out_specs=(hbm(), vmem(), vmem()),
         scratch_shapes=[
+            pltpu.VMEM((tile_rows, tile_cols), F32),
             pltpu.VMEM((tile_cols // 128, lanes * 128, 128), F32),
             pltpu.VMEM((lanes, long, 128), F32),
         ]
-        + [pltpu.VMEM((long // 8, lanes, 8, 128), F32)] * 3,
+        + [pltpu.VMEM((long // 8, lanes, 8, 128), F32)] * 3
+        + [pltpu.SemaphoreType.DMA],
         compiler_params=pltpu.CompilerParams(vmem_limit_bytes=32 * mib),
         name="fill",
-    )(tile, above, below, right, left)
+    )(tile, *east, *north)
 
     totals = lax.all_to_all(totals, "north", split_axis=0, concat_axis=0, tiled=True)
-    place = lax.axis_index("north").astype(I32).reshape(1)
-
     light = pl.pallas_call(
         light_kernel,
-        grid=(NS,),
         out_shape=jax.ShapeDtypeStruct((NS, tile_rows, tile_cols), F32),
-        in_specs=[smem()] * 3 + [vmem()] * 2,
-        out_specs=pl.BlockSpec((1, tile_rows, tile_cols), lambda s: (s, 0, 0)),
-        scratch_shapes=[pltpu.VMEM((2, tile_rows, 128), F32)],
+        in_specs=[smem()] * 2 + [vmem()] * 2,
+        out_specs=hbm(),
+        scratch_shapes=[
+            pltpu.VMEM((NS, tile_rows, tile_cols), F32),
+            pltpu.VMEM((2, tile_rows, 128), F32),
+            pltpu.SemaphoreType.DMA((NS, PIECES)),
+        ],
         compiler_params=pltpu.CompilerParams(vmem_limit_bytes=24 * mib),
         name="light",
-    )(place, extinction, sun_side, depths, totals)
+    )(extinction, sun_side, depths, totals)
     return surface, light
 
 

time: 98.8 us -> 88.5 us (0.90)
  blocking collectives: 42.9 us -> 56.6 us
  starting transfers between devices: 18.5 us -> 5.09 us
  waiting for transfers between devices: 12.3 us -> 5.17 us
  Pallas kernels: 24 us -> 20.6 us
    all_to_all x0 -> x1, blocking collectives: none -> 13.7 us  [body(): lax.all_to_all(totals, 'north', split_axis=0, concat_axis=0, tiled=True)]
    all_to_all x1 -> x0, starting transfers between devices: 8.32 us -> none  [body(): lax.all_to_all(totals, 'north', split_axis=0, concat_axis=0, tiled=True)]
    all_to_all x1 -> x0, waiting for transfers between devices: 7.66 us -> none  [body(): lax.all_to_all(totals, 'north', split_axis=0, concat_axis=0, tiled=True)]
    ppermute x4, starting transfers between devices: 10.2 us -> 5.09 us  [swapped(): return lax.ppermute(values, axis, edges + [(j, i) for i, j in edges])]
    pallas_call x1, Pallas kernels: 4.57 us -> 2.95 us  [body(): pl.pallas_call(light_kernel, out_shape=jax.ShapeDtypeStruct((NS, tile_row...]
    pallas_call x1, Pallas kernels: 7.71 us -> 6.51 us  [body(): pl.pallas_call(deal_kernel, out_shape=jax.ShapeDtypeStruct((devices, BLOC...]
  transfers between devices with their start and end apart: 5 -> 4, of which waited for: 3 -> 2; matrix products, arithmetic and copies ran while one was open for 0% -> 0% of each run, Pallas kernels for 0% -> 0%
where the time goes in v3:
time: 88.5 us; the launch traced here: 88.2 us
  blocking collectives  56.6 us (64%)
  Pallas kernels  20.6 us (23%)
  waiting for transfers between devices  5.17 us (6%)
  starting transfers between devices  5.09 us (6%)
    all_to_all x1, blocking collectives, body(): lax.all_to_all(dealt, ('east', 'north'), split_axis=0, concat_axis=0, til...  42.9 us
    all_to_all x1, blocking collectives, body(): lax.all_to_all(totals, 'north', split_axis=0, concat_axis=0, tiled=True)  13.7 us
    pallas_call x1, Pallas kernels, body(): pl.pallas_call(deal_kernel, out_shape=jax.ShapeDtypeStruct((devices, BLOC...  6.51 us
    pallas_call x1, Pallas kernels, body(): pl.pallas_call(fill_kernel, out_shape=(jax.ShapeDtypeStruct((tile_rows, t...  6.42 us
    ppermute x4, waiting for transfers between devices, swapped(): return lax.ppermute(values, axis, edges + [(j, i) for i, j in edges])  5.17 us
    ppermute x4, starting transfers between devices, swapped(): return lax.ppermute(values, axis, edges + [(j, i) for i, j in edges])  5.09 us
    pallas_call x1, Pallas kernels, body(): pl.pallas_call(bin_kernel, out_shape=(jax.ShapeDtypeStruct((tile_rows, ti...  4.53 us
    pallas_call x1, Pallas kernels, body(): pl.pallas_call(light_kernel, out_shape=jax.ShapeDtypeStruct((NS, tile_row...  2.95 us
  transfers between devices with their start and end apart: 4, of which 2 were waited for; matrix products, arithmetic and copies ran while one was open for 0% of the time, Pallas kernels for 0%

profile of v3, /device:TPU:2, one launch (start us, length us, event | category | flops | bytes accessed | tf_op | source)
XLA Modules:
  0.0 88.2 jit_solution(9487203121725845268)
XLA Ops:
  0.6 6.5 %deal.1 = bf16[128,72,128]{2,1,0:T(8,128)(2,1)} custom-call(bf16[4096,128]{1,0:T(8,128)(2,1)} %heights_in.1, s32[32,128]{1,0:T(8,128)} %bitcast.2, s32[32,128]{1,0:T(8,128)} %bitcast.3), custom_call_target="tpu_custom_call" | custom-call | tf_op jit(solution)/shard_map/deal/pallas_call | solution.py:394
  7.2 0.0 copy-start
  7.2 42.9 %all_to_all.10.got = bf16[128,72,128]{2,1,0:T(8,128)(2,1)S(1)} all-to-all(bf16[128,72,128]{2,1,0:T(8,128)(2,1)} %deal.1), channel_id=1, replica_groups=mesh['east'=8,'north'=16] {'east','north'}, dimensions={0} | all-to-all | bytes 4718592 | tf_op jit(solution)/shard_map/all_to_all | solution.py:415
  50.1 0.0 copy-done
  50.1 0.0 copy-start.1
  50.1 0.0 copy-start.2
  50.1 4.5 %bin.1 = (f32[256,512]{1,0:T(8,128)S(1)}, f32[24,512]{1,0:T(8,128)S(1)}, f32[24,512]{1,0:T(8,128)S(1)}) custom-call(bf16[128,72,128]{2,1,0:T(8,128)(2,1)S(1)} %all_to_all.10.got, s32[256,512]{1,0:T(8,128)S(1)} %copy-done), custom_call_target="tpu_custom_call" | custom-call | tf_op jit(solution)/shard_map/bin/pallas_call | solution.py:418
  54.6 1.9 %collective-permute-start = (f32[24,512]{1,0:T(8,128)S(1)}, f32[24,512]{1,0:T(8,128)S(1)}, u32[]{:S(2)}, u32[]{:S(2)}) collective-permute-start(f32[24,512]{1,0:T(8,128)S(1)} %get-tuple-element.11), channel_id=1, source_target_pairs={{16,32},{48,64},{80,96},{32,16},{64,48},{96,80},{17,33},{49,65},{8... | collective-permute-start | bytes 147464 | tf_op jit(solution)/shard_map/ppermute | solution.py:381
  56.5 0.4 collective-permute-start.1
  57.0 3.0 %collective-permute-done.got_one.east_one = f32[24,512]{1,0:T(8,128)S(1)} collective-permute-done((f32[24,512]{1,0:T(8,128)S(1)}, f32[24,512]{1,0:T(8,128)S(1)}, u32[]{:S(2)}, u32[]{:S(2)}) %collective-permute-start) | collective-permute-done | bytes 49184 | tf_op jit(solution)/shard_map/ppermute | solution.py:381
  60.0 0.0 collective-permute-done.1.got_two.east_two
  60.0 0.2 sides.1
  60.2 0.7 collective-permute-start.2
  60.9 2.1 %collective-permute-start.3 = (f32[3,24,128]{2,1,0:T(8,128)S(1)}, f32[3,24,128]{2,1,0:T(8,128)S(1)}, u32[]{:S(2)}, u32[]{:S(2)}) collective-permute-start(f32[3,24,128]{2,1,0:T(8,128)S(1)} %get-tuple-element.14), channel_id=1, source_target_pairs={{0,1},{2,3},{4,5},{6,7},{8,9},{10,11},{12,13},{14,15},{1,0},{3,2},... | collective-permute-start | bytes 110600 | tf_op jit(solution)/shard_map/ppermute | solution.py:381
  62.9 0.0 collective-permute-done.2.north_one
  62.9 2.1 %collective-permute-done.3.north_two = f32[3,24,128]{2,1,0:T(8,128)S(1)} collective-permute-done((f32[3,24,128]{2,1,0:T(8,128)S(1)}, f32[3,24,128]{2,1,0:T(8,128)S(1)}, u32[]{:S(2)}, u32[]{:S(2)}) %collective-permute-start.3) | collective-permute-done | bytes 36896 | tf_op jit(solution)/shard_map/ppermute | solution.py:381
  65.1 6.4 %fill.1 = (f32[256,512]{1,0:T(8,128)}, f32[2,256,512]{2,1,0:T(8,128)S(1)}, f32[16,8,128]{2,1,0:T(8,128)S(1)}) custom-call(f32[256,512]{1,0:T(8,128)S(1)} %get-tuple-element.10.tile, f32[24,512]{1,0:T(8,128)S(1)} %collective-permute-done.got_one.east_one, f32[24,512]{1,0:T(8,128)S(1)} %collective-permute-done.1.got_two.east_two, ...), custom_call_target="tpu_custom_call" | custom-call | tf_op jit(solution)/shard_map/fill/pallas_call | solution.py:447
  71.5 13.7 %all_to_all.11.totals = f32[16,8,128]{2,1,0:T(8,128)S(1)} all-to-all(f32[16,8,128]{2,1,0:T(8,128)S(1)} %get-tuple-element.17), channel_id=1, replica_groups=mesh['east'=8,'north'=16] {'north'}, dimensions={0} | all-to-all | bytes 131072 | tf_op jit(solution)/shard_map/all_to_all | solution.py:467
  85.2 0.0 copy-done.1
  85.3 0.0 copy-done.2
  85.3 3.0 %light.1 = f32[8,256,512]{2,1,0:T(8,128)} custom-call(f32[8]{0:T(128)S(1)} %copy-done.1, s32[8]{0:T(128)S(1)} %copy-done.2, f32[2,256,512]{2,1,0:T(8,128)S(1)} %get-tuple-element.16.depths, f32[16,8,128]{2,1,0:T(8,128)S(1)} %all_to_all.11.totals), custom_call_target="tpu_custom_call" | custom-call | tf_op jit(solution)/shard_map/light/pallas_call | solution.py:468
Async XLA Ops:
  7.2 42.9 %copy-start = (s32[256,512]{1,0:T(8,128)S(1)}, s32[256,512]{1,0:T(8,128)}, u32[]{:S(2)}) copy-start(s32[256,512]{1,0:T(8,128)} %gap_mask.1) | copy-start | bytes 1572868
  50.1 35.2 %copy-start.1 = (f32[8]{0:T(128)S(1)}, f32[8]{0:T(128)}, u32[]{:S(2)}) copy-start(f32[8]{0:T(128)} %extinction.1) | copy-start | bytes 100
  50.1 35.2 %copy-start.2 = (s32[8]{0:T(128)S(1)}, s32[8]{0:T(128)}, u32[]{:S(2)}) copy-start(s32[8]{0:T(128)} %side.1) | copy-start | bytes 100
  54.6 5.4 %collective-permute-start = (f32[24,512]{1,0:T(8,128)S(1)}, f32[24,512]{1,0:T(8,128)S(1)}, u32[]{:S(2)}, u32[]{:S(2)}) collective-permute-start(f32[24,512]{1,0:T(8,128)S(1)} %get-tuple-element.11), channel_id=1, source_target_pairs={{16,32},{48,64},{80,96},{32,16},{64,48},{96,80},{17,33},{49,65},{8... | collective-permute-start | bytes 147464 | tf_op jit(solution)/shard_map/ppermute | solution.py:381
  56.5 3.5 %collective-permute-start.1 = (f32[24,512]{1,0:T(8,128)S(1)}, f32[24,512]{1,0:T(8,128)S(1)}, u32[]{:S(2)}, u32[]{:S(2)}) collective-permute-start(f32[24,512]{1,0:T(8,128)S(1)} %get-tuple-element.12), channel_id=1, source_target_pairs={{0,16},{32,48},{64,80},{96,112},{16,0},{48,32},{80,64},{112,96},{1... | collective-permute-start | bytes 147464 | tf_op jit(solution)/shard_map/ppermute | solution.py:381
  60.2 2.7 %collective-permute-start.2 = (f32[3,24,128]{2,1,0:T(8,128)S(1)}, f32[3,24,128]{2,1,0:T(8,128)S(1)}, u32[]{:S(2)}, u32[]{:S(2)}) collective-permute-start(f32[3,24,128]{2,1,0:T(8,128)S(1)} %get-tuple-element.13), channel_id=1, source_target_pairs={{1,2},{3,4},{5,6},{7,8},{9,10},{11,12},{13,14},{2,1},{4,3},{6,5},{... | collective-permute-start | bytes 110600 | tf_op jit(solution)/shard_map/ppermute | solution.py:381
  60.9 4.2 %collective-permute-start.3 = (f32[3,24,128]{2,1,0:T(8,128)S(1)}, f32[3,24,128]{2,1,0:T(8,128)S(1)}, u32[]{:S(2)}, u32[]{:S(2)}) collective-permute-start(f32[3,24,128]{2,1,0:T(8,128)S(1)} %get-tuple-element.14), channel_id=1, source_target_pairs={{0,1},{2,3},{4,5},{6,7},{8,9},{10,11},{12,13},{14,15},{1,0},{3,2},... | collective-permute-start | bytes 110600 | tf_op jit(solution)/shard_map/ppermute | solution.py:381

commit v4 on v3

--- a/solution.py
+++ b/solution.py
@@ -45,6 +45,10 @@
         terms.append(term)
         values = values - term.astype(F32)
     return terms
+
+
+def softplus(values):
+    return jnp.maximum(values, 0.0) + jnp.log1p(jnp.exp(-jnp.abs(values)))
 
 
 def deal_kernel(
@@ -253,16 +257,12 @@
     east_two,
     north_one,
     north_two,
-    surface_out,
-    depths,
+    cells,
     totals,
-    surface,
     slabs,
     turned,
-    cells,
     keep,
     rate,
-    sem,
 ):
     rows, cols = tile.shape
     above, below = upper_lower("east", east_one[...], east_two[...])
@@ -306,6 +306,25 @@
 
     lax.fori_loop(0, STEPS, step, 0)
 
+    sums = [jnp.zeros((8, 128), F32) for _ in range(lanes)]
+    for v in range(deep):
+        inside = iota((8, 128), 0) * deep + v < cols
+        for k in range(lanes):
+            soft = softplus(cells[v, k])
+            sums[k] = sums[k] + (soft if 7 * deep + v < cols else jnp.where(inside, soft, 0.0))
+    packed = jnp.zeros((8, 128), F32)
+    for k in range(lanes):
+        total = jnp.sum(sums[k], axis=0, keepdims=True)
+        packed = packed + jnp.where(iota((8, 128), 0) == k, total, 0.0)
+    for n in range(totals.shape[0]):
+        totals[n] = packed
+
+
+def depth_kernel(cells, surface_out, depths, surface, slabs, turned, sem):
+    rows, cols = surface.shape
+    quarters = cols // 128
+    lanes = turned.shape[0]
+    deep = cells.shape[0]
     for v in range(deep):
         for k in range(lanes):
             turned[k, pl.ds(v, 8, stride=deep), :] = cells[v, k]
@@ -316,29 +335,21 @@
         surface[:, at] = slabs[q, :rows, :]
     store = pltpu.make_async_copy(surface, surface_out, sem)
     store.start()
-    final = surface[...]
-    soft = jnp.maximum(final, 0.0) + jnp.log1p(jnp.exp(-jnp.abs(final)))
+    soft = softplus(surface[...])
     ahead = (iota((cols, cols), 0) < iota((cols, cols), 1)).astype(F32).astype(BF16)
-    ones = jnp.ones((8, cols), BF16)
     south = jnp.zeros((rows, cols), F32)
-    along = jnp.zeros((8, rows), F32)
     for term in reversed(split(soft)):
         south = south + jnp.dot(term, ahead, preferred_element_type=F32)
-        along = along + lax.dot_general(
-            ones, term, (((1,), (1,)), ((), ())), preferred_element_type=F32
-        )
     whole = south[:, cols - 1:] + soft[:, cols - 1:]
     depths[0] = south
     depths[1] = (whole - south) - soft
-    packed = jnp.where(iota((8, 128), 0) == 0, along[:, :128], along[:, 128:])
-    for n in range(totals.shape[0]):
-        totals[n] = packed
     store.wait()
 
 
 def light_kernel(extinction, side, depths, totals, out, light, carried, sems):
     count, rows, cols = light.shape
     n_north = totals.shape[0]
+    lanes = carried.shape[1] // 128
     here = lax.axis_index("north")
     zero = jnp.zeros((8, 128), F32)
     for k in range(2):
@@ -347,9 +358,9 @@
             counts = here < n if k else here > n
             total = total + jnp.where(counts, totals[n], zero)
         turned = jnp.concatenate([total, jnp.zeros((120, 128), F32)], axis=0).T
-        for half in range(rows // 128):
-            carried[k, half * 128:(half + 1) * 128, :] = jnp.broadcast_to(
-                turned[:, half:half + 1], (128, 128)
+        for lane in range(lanes):
+            carried[k, pl.ds(lane, 128, stride=lanes), :] = jnp.broadcast_to(
+                turned[:, lane:lane + 1], (128, 128)
             )
 
     def store(s, i):
@@ -444,27 +455,46 @@
 
     north = swapped(one, "north", 1), swapped(two, "north", 0)
 
-    surface, depths, totals = pl.pallas_call(
+    shape = jax.ShapeDtypeStruct((long // 8, lanes, 8, 128), F32)
+    cells, totals = pl.pallas_call(
         fill_kernel,
+        out_shape=(shape, jax.ShapeDtypeStruct((n_north, 8, 128), F32)),
+        in_specs=[vmem()] * 5,
+        out_specs=(vmem(), vmem()),
+        scratch_shapes=[
+            pltpu.VMEM((tile_cols // 128, lanes * 128, 128), F32),
+            pltpu.VMEM((lanes, long, 128), F32),
+        ]
+        + [pltpu.VMEM(shape.shape, F32)] * 2,
+        compiler_params=pltpu.CompilerParams(vmem_limit_bytes=32 * mib),
+        name="fill",
+    )(tile, *east, *north)
+
+    totals = lax.all_to_all(totals, "north", split_axis=0, concat_axis=0, tiled=True)
+
+    surface, depths = pl.pallas_call(
+        depth_kernel,
         out_shape=(
             jax.ShapeDtypeStruct((tile_rows, tile_cols), F32),
             jax.ShapeDtypeStruct((2, tile_rows, tile_cols), F32),
-            jax.ShapeDtypeStruct((n_north, 8, 128), F32),
         ),
-        in_specs=[vmem()] * 5,
-        out_specs=(hbm(), vmem(), vmem()),
+        in_specs=[vmem()],
+        out_specs=(hbm(), vmem()),
         scratch_shapes=[
             pltpu.VMEM((tile_rows, tile_cols), F32),
             pltpu.VMEM((tile_cols // 128, lanes * 128, 128), F32),
             pltpu.VMEM((lanes, long, 128), F32),
-        ]
-        + [pltpu.VMEM((long // 8, lanes, 8, 128), F32)] * 3
-        + [pltpu.SemaphoreType.DMA],
-        compiler_params=pltpu.CompilerParams(vmem_limit_bytes=32 * mib),
-        name="fill",
-    )(tile, *east, *north)
-
-    totals = lax.all_to_all(totals, "north", split_axis=0, concat_axis=0, tiled=True)
+            pltpu.SemaphoreType.DMA,
+        ],
+        compiler_params=pltpu.CompilerParams(vmem_limit_bytes=16 * mib),
+        cost_estimate=pl.CostEstimate(
+            flops=6 * tile_rows * tile_cols * tile_cols,
+            bytes_accessed=16 * tile_rows * tile_cols,
+            transcendentals=2 * tile_rows * tile_cols,
+        ),
+        name="depth",
+    )(cells)
+
     light = pl.pallas_call(
         light_kernel,
         out_shape=jax.ShapeDtypeStruct((NS, tile_rows, tile_cols), F32),
@@ -472,7 +502,7 @@
         out_specs=hbm(),
         scratch_shapes=[
             pltpu.VMEM((NS, tile_rows, tile_cols), F32),
-            pltpu.VMEM((2, tile_rows, 128), F32),
+            pltpu.VMEM((2, lanes * 128, 128), F32),
             pltpu.SemaphoreType.DMA((NS, PIECES)),
         ],
         compiler_params=pltpu.CompilerParams(vmem_limit_bytes=24 * mib),

time: 88.5 us -> 89.6 us (1.012)
  blocking collectives: 56.6 us -> 42.9 us
  waiting for transfers between devices: 5.17 us -> 11.6 us
  starting transfers between devices: 5.09 us -> 11.4 us
  Pallas kernels: 20.6 us -> 22.6 us
    all_to_all x1 -> x0, blocking collectives: 13.7 us -> none  [body(): lax.all_to_all(totals, 'north', split_axis=0, concat_axis=0, tiled=True)]
    all_to_all x0 -> x1, waiting for transfers between devices: none -> 6.47 us  [body(): lax.all_to_all(totals, 'north', split_axis=0, concat_axis=0, tiled=True)]
    all_to_all x0 -> x1, starting transfers between devices: none -> 6.28 us  [body(): lax.all_to_all(totals, 'north', split_axis=0, concat_axis=0, tiled=True)]
    pallas_call x1 -> x2, Pallas kernels: 6.42 us -> 8.32 us  [the longest x1 7.13 us: body(): pl.pallas_call(fill_kernel, out_shape=(shape, jax.ShapeDtypeStruct((n_nor...]
  transfers between devices with their start and end apart: 4 -> 5, of which waited for: 2 -> 3; matrix products, arithmetic and copies ran while one was open for 0% -> 0% of each run, Pallas kernels for 0% -> 1%
where the time goes in v4:
time: 89.6 us; the launch traced here: 89.3 us
  blocking collectives  42.9 us (48%)
  Pallas kernels  22.6 us (25%)
  waiting for transfers between devices  11.6 us (13%)
  starting transfers between devices  11.4 us (13%)
    all_to_all x1, blocking collectives, body(): lax.all_to_all(dealt, ('east', 'north'), split_axis=0, concat_axis=0, til...  42.9 us
    pallas_call x1, Pallas kernels, body(): pl.pallas_call(fill_kernel, out_shape=(shape, jax.ShapeDtypeStruct((n_nor...  7.13 us
    pallas_call x1, Pallas kernels, body(): pl.pallas_call(deal_kernel, out_shape=jax.ShapeDtypeStruct((devices, BLOC...  6.51 us
    all_to_all x1, waiting for transfers between devices, body(): lax.all_to_all(totals, 'north', split_axis=0, concat_axis=0, tiled=True)  6.47 us
    all_to_all x1, starting transfers between devices, body(): lax.all_to_all(totals, 'north', split_axis=0, concat_axis=0, tiled=True)  6.28 us
    ppermute x4, waiting for transfers between devices, swapped(): return lax.ppermute(values, axis, edges + [(j, i) for i, j in edges])  5.17 us
    ppermute x4, starting transfers between devices, swapped(): return lax.ppermute(values, axis, edges + [(j, i) for i, j in edges])  5.09 us
    pallas_call x1, Pallas kernels, body(): pl.pallas_call(bin_kernel, out_shape=(jax.ShapeDtypeStruct((tile_rows, ti...  4.53 us
  transfers between devices with their start and end apart: 5, of which 3 were waited for; matrix products, arithmetic and copies ran while one was open for 0% of the time, Pallas kernels for 1%

profile of v4, /device:TPU:2, one launch (start us, length us, event | category | flops | bytes accessed | tf_op | source)
XLA Modules:
  0.0 89.3 jit_solution(11548645437623992824)
XLA Ops:
  0.6 6.5 %deal.1 = bf16[128,72,128]{2,1,0:T(8,128)(2,1)} custom-call(bf16[4096,128]{1,0:T(8,128)(2,1)} %heights_in.1, s32[32,128]{1,0:T(8,128)} %bitcast.2, s32[32,128]{1,0:T(8,128)} %bitcast.3), custom_call_target="tpu_custom_call" | custom-call | tf_op jit(solution)/shard_map/deal/pallas_call | solution.py:405
  7.2 0.0 copy-start
  7.2 42.9 %all_to_all.10.got = bf16[128,72,128]{2,1,0:T(8,128)(2,1)S(1)} all-to-all(bf16[128,72,128]{2,1,0:T(8,128)(2,1)} %deal.1), channel_id=1, replica_groups=mesh['east'=8,'north'=16] {'east','north'}, dimensions={0} | all-to-all | bytes 4718592 | tf_op jit(solution)/shard_map/all_to_all | solution.py:426
  50.1 0.0 copy-done
  50.1 0.0 copy-start.1
  50.1 0.0 copy-start.2
  50.1 4.5 %bin.1 = (f32[256,512]{1,0:T(8,128)S(1)}, f32[24,512]{1,0:T(8,128)S(1)}, f32[24,512]{1,0:T(8,128)S(1)}) custom-call(bf16[128,72,128]{2,1,0:T(8,128)(2,1)S(1)} %all_to_all.10.got, s32[256,512]{1,0:T(8,128)S(1)} %copy-done), custom_call_target="tpu_custom_call" | custom-call | tf_op jit(solution)/shard_map/bin/pallas_call | solution.py:429
  54.6 1.9 %collective-permute-start = (f32[24,512]{1,0:T(8,128)S(1)}, f32[24,512]{1,0:T(8,128)S(1)}, u32[]{:S(2)}, u32[]{:S(2)}) collective-permute-start(f32[24,512]{1,0:T(8,128)S(1)} %get-tuple-element.12), channel_id=1, source_target_pairs={{16,32},{48,64},{80,96},{32,16},{64,48},{96,80},{17,33},{49,65},{8... | collective-permute-start | bytes 147464 | tf_op jit(solution)/shard_map/ppermute | solution.py:392
  56.5 0.4 collective-permute-start.1
  57.0 3.0 %collective-permute-done.got_one.east_one = f32[24,512]{1,0:T(8,128)S(1)} collective-permute-done((f32[24,512]{1,0:T(8,128)S(1)}, f32[24,512]{1,0:T(8,128)S(1)}, u32[]{:S(2)}, u32[]{:S(2)}) %collective-permute-start) | collective-permute-done | bytes 49184 | tf_op jit(solution)/shard_map/ppermute | solution.py:392
  60.0 0.0 collective-permute-done.1.got_two.east_two
  60.0 0.2 sides.1
  60.2 0.7 collective-permute-start.2
  60.9 2.1 %collective-permute-start.3 = (f32[3,24,128]{2,1,0:T(8,128)S(1)}, f32[3,24,128]{2,1,0:T(8,128)S(1)}, u32[]{:S(2)}, u32[]{:S(2)}) collective-permute-start(f32[3,24,128]{2,1,0:T(8,128)S(1)} %get-tuple-element.15), channel_id=1, source_target_pairs={{0,1},{2,3},{4,5},{6,7},{8,9},{10,11},{12,13},{14,15},{1,0},{3,2},... | collective-permute-start | bytes 110600 | tf_op jit(solution)/shard_map/ppermute | solution.py:392
  62.9 0.0 collective-permute-done.2.north_one
  62.9 2.1 %collective-permute-done.3.north_two = f32[3,24,128]{2,1,0:T(8,128)S(1)} collective-permute-done((f32[3,24,128]{2,1,0:T(8,128)S(1)}, f32[3,24,128]{2,1,0:T(8,128)S(1)}, u32[]{:S(2)}, u32[]{:S(2)}) %collective-permute-start.3) | collective-permute-done | bytes 36896 | tf_op jit(solution)/shard_map/ppermute | solution.py:392
  65.1 7.1 %fill.1 = (f32[70,3,8,128]{3,2,1,0:T(8,128)S(1)}, f32[16,8,128]{2,1,0:T(8,128)}) custom-call(f32[256,512]{1,0:T(8,128)S(1)} %get-tuple-element.11.tile, f32[24,512]{1,0:T(8,128)S(1)} %collective-permute-done.got_one.east_one, f32[24,512]{1,0:T(8,128)S(1)} %collective-permute-done.1.got_two.east_two, f32[3,24,128]{2,1,0:T(8,128)S(1)} %collective-permute-done.2.north_one, ...), custom_call_target="tpu_custom_call" | custom-call | tf_op jit(solution)/shard_map/fill/pallas_call | solution.py:459
  72.2 6.3 %all-to-all-start.1 = ((f32[16,8,128]{2,1,0:T(8,128)}), f32[16,8,128]{2,1,0:T(8,128)S(1)}, u32[]{:S(2)}, u32[]{:S(2)}) async-start(f32[16,8,128]{2,1,0:T(8,128)} %get-tuple-element.19), calls=%async_computation.1 | async-start | bytes 131072 | tf_op jit(solution)/shard_map/all_to_all | solution.py:473
  78.5 1.2 %depth.1 = (f32[256,512]{1,0:T(8,128)}, f32[2,256,512]{2,1,0:T(8,128)S(1)}) custom-call(f32[70,3,8,128]{3,2,1,0:T(8,128)S(1)} %get-tuple-element.16.cells), custom_call_target="tpu_custom_call" | custom-call | flops 402653184 | bytes 2097152 | tf_op jit(solution)/shard_map/depth/pallas_call | solution.py:475
  79.7 6.5 %all-to-all-done.1.totals = f32[16,8,128]{2,1,0:T(8,128)S(1)} async-done(((f32[16,8,128]{2,1,0:T(8,128)}), f32[16,8,128]{2,1,0:T(8,128)S(1)}, u32[]{:S(2)}, u32[]{:S(2)}) %all-to-all-start.1) | async-done | bytes 65568 | tf_op jit(solution)/shard_map/all_to_all | solution.py:473
  86.2 0.0 copy-done.1
  86.2 0.0 copy-done.2
  86.2 3.1 %light.1 = f32[8,256,512]{2,1,0:T(8,128)} custom-call(f32[8]{0:T(128)S(1)} %copy-done.1, s32[8]{0:T(128)S(1)} %copy-done.2, f32[2,256,512]{2,1,0:T(8,128)S(1)} %get-tuple-element.18.depths, f32[16,8,128]{2,1,0:T(8,128)S(1)} %all-to-all-done.1.totals), custom_call_target="tpu_custom_call" | custom-call | tf_op jit(solution)/shard_map/light/pallas_call | solution.py:498
Async XLA Ops:
  7.2 42.9 %copy-start = (s32[256,512]{1,0:T(8,128)S(1)}, s32[256,512]{1,0:T(8,128)}, u32[]{:S(2)}) copy-start(s32[256,512]{1,0:T(8,128)} %gap_mask.1) | copy-start | bytes 1572868
  50.1 36.1 %copy-start.1 = (f32[8]{0:T(128)S(1)}, f32[8]{0:T(128)}, u32[]{:S(2)}) copy-start(f32[8]{0:T(128)} %extinction.1) | copy-start | bytes 100
  50.1 36.1 %copy-start.2 = (s32[8]{0:T(128)S(1)}, s32[8]{0:T(128)}, u32[]{:S(2)}) copy-start(s32[8]{0:T(128)} %side.1) | copy-start | bytes 100
  54.6 5.4 %collective-permute-start = (f32[24,512]{1,0:T(8,128)S(1)}, f32[24,512]{1,0:T(8,128)S(1)}, u32[]{:S(2)}, u32[]{:S(2)}) collective-permute-start(f32[24,512]{1,0:T(8,128)S(1)} %get-tuple-element.12), channel_id=1, source_target_pairs={{16,32},{48,64},{80,96},{32,16},{64,48},{96,80},{17,33},{49,65},{8... | collective-permute-start | bytes 147464 | tf_op jit(solution)/shard_map/ppermute | solution.py:392
  56.5 3.5 %collective-permute-start.1 = (f32[24,512]{1,0:T(8,128)S(1)}, f32[24,512]{1,0:T(8,128)S(1)}, u32[]{:S(2)}, u32[]{:S(2)}) collective-permute-start(f32[24,512]{1,0:T(8,128)S(1)} %get-tuple-element.13), channel_id=1, source_target_pairs={{0,16},{32,48},{64,80},{96,112},{16,0},{48,32},{80,64},{112,96},{1... | collective-permute-start | bytes 147464 | tf_op jit(solution)/shard_map/ppermute | solution.py:392
  60.2 2.7 %collective-permute-start.2 = (f32[3,24,128]{2,1,0:T(8,128)S(1)}, f32[3,24,128]{2,1,0:T(8,128)S(1)}, u32[]{:S(2)}, u32[]{:S(2)}) collective-permute-start(f32[3,24,128]{2,1,0:T(8,128)S(1)} %get-tuple-element.14), channel_id=1, source_target_pairs={{1,2},{3,4},{5,6},{7,8},{9,10},{11,12},{13,14},{2,1},{4,3},{6,5},{... | collective-permute-start | bytes 110600 | tf_op jit(solution)/shard_map/ppermute | solution.py:392
  60.9 4.2 %collective-permute-start.3 = (f32[3,24,128]{2,1,0:T(8,128)S(1)}, f32[3,24,128]{2,1,0:T(8,128)S(1)}, u32[]{:S(2)}, u32[]{:S(2)}) collective-permute-start(f32[3,24,128]{2,1,0:T(8,128)S(1)} %get-tuple-element.15), channel_id=1, source_target_pairs={{0,1},{2,3},{4,5},{6,7},{8,9},{10,11},{12,13},{14,15},{1,0},{3,2},... | collective-permute-start | bytes 110600 | tf_op jit(solution)/shard_map/ppermute | solution.py:392
  72.2 14.0 %all-to-all-start.1 = ((f32[16,8,128]{2,1,0:T(8,128)}), f32[16,8,128]{2,1,0:T(8,128)S(1)}, u32[]{:S(2)}, u32[]{:S(2)}) async-start(f32[16,8,128]{2,1,0:T(8,128)} %get-tuple-element.19), calls=%async_computation.1 | async-start | bytes 131072 | tf_op jit(solution)/shard_map/all_to_all | solution.py:473

commit v5 on v4

--- a/solution.py
+++ b/solution.py
@@ -48,7 +48,7 @@
 
 
 def softplus(values):
-    return jnp.maximum(values, 0.0) + jnp.log1p(jnp.exp(-jnp.abs(values)))
+    return jnp.log(1.0 + jnp.exp(values))
 
 
 def deal_kernel(
@@ -251,37 +251,37 @@
         two[k] = jnp.where(odd, west, east)
 
 
-def fill_kernel(
-    tile,
-    east_one,
-    east_two,
-    north_one,
-    north_two,
-    cells,
-    totals,
-    slabs,
-    turned,
-    keep,
-    rate,
-):
-    rows, cols = tile.shape
+def turn_kernel(tile, east_one, east_two, coded, slabs, turned):
+    cols = tile.shape[1]
+    deep, lanes, _, _ = coded.shape
     above, below = upper_lower("east", east_one[...], east_two[...])
-    right, left = upper_lower("north", north_one[...], north_two[...])
-    quarters = cols // 128
-    lanes, long, _ = turned.shape
-    deep = long // 8
-
-    for q in range(quarters):
+    for q in range(cols // 128):
         at = slice(q * 128, (q + 1) * 128)
         lay_rows(slabs.at[q], tile, above, below, at)
         for k in range(lanes):
             turned[k, at, :] = slabs[q, pl.ds(k, 128, stride=lanes), :].T
     for k in range(lanes):
-        turned[k, cols:cols + HALO, :] = right[k]
-        turned[k, cols + HALO:, :] = left[k]
+        turned[k, cols:, :] = jnp.zeros((2 * HALO, 128), F32)
     for v in range(deep):
         for k in range(lanes):
-            values = turned[k, pl.ds(v, 8, stride=deep), :]
+            coded[v, k] = turned[k, pl.ds(v, 8, stride=deep), :]
+
+
+def fill_kernel(coded, north_one, north_two, cells, totals, halo, keep, rate):
+    deep, lanes, _, _ = coded.shape
+    long = 8 * deep
+    cols = long - 2 * HALO
+    right, left = upper_lower("north", north_one[...], north_two[...])
+    for k in range(lanes):
+        halo[k, cols:cols + HALO, :] = right[k]
+        halo[k, cols + HALO:, :] = left[k]
+    for v in range(deep):
+        column = iota((8, 128), 0) * deep + v
+        for k in range(lanes):
+            values = coded[v, k]
+            if 7 * deep + v >= cols:
+                beyond = halo[k, pl.ds(v, 8, stride=deep), :]
+                values = jnp.where(column >= cols, beyond, values)
             unknown = values > 0.5 * GAP
             cells[v, k] = jnp.where(unknown, 0.0, values)
             keep[v, k] = jnp.where(unknown, 1.0 - 0.9, 1.0)
@@ -304,7 +304,7 @@
             before, here = here, after
         return carry
 
-    lax.fori_loop(0, STEPS, step, 0)
+    lax.fori_loop(0, STEPS, step, 0, unroll=2)
 
     sums = [jnp.zeros((8, 128), F32) for _ in range(lanes)]
     for v in range(deep):
@@ -456,19 +456,33 @@
     north = swapped(one, "north", 1), swapped(two, "north", 0)
 
     shape = jax.ShapeDtypeStruct((long // 8, lanes, 8, 128), F32)
+    coded = pl.pallas_call(
+        turn_kernel,
+        out_shape=shape,
+        in_specs=[vmem()] * 3,
+        out_specs=vmem(),
+        scratch_shapes=[
+            pltpu.VMEM((tile_cols // 128, lanes * 128, 128), F32),
+            pltpu.VMEM((lanes, long, 128), F32),
+        ],
+        compiler_params=pltpu.CompilerParams(vmem_limit_bytes=16 * mib),
+        cost_estimate=pl.CostEstimate(
+            flops=4 * tile_rows * tile_cols,
+            bytes_accessed=16 * tile_rows * tile_cols,
+            transcendentals=0,
+        ),
+        name="turn",
+    )(tile, *east)
+
     cells, totals = pl.pallas_call(
         fill_kernel,
         out_shape=(shape, jax.ShapeDtypeStruct((n_north, 8, 128), F32)),
-        in_specs=[vmem()] * 5,
+        in_specs=[vmem()] * 3,
         out_specs=(vmem(), vmem()),
-        scratch_shapes=[
-            pltpu.VMEM((tile_cols // 128, lanes * 128, 128), F32),
-            pltpu.VMEM((lanes, long, 128), F32),
-        ]
-        + [pltpu.VMEM(shape.shape, F32)] * 2,
+        scratch_shapes=[pltpu.VMEM((lanes, long, 128), F32)] + [pltpu.VMEM(shape.shape, F32)] * 2,
         compiler_params=pltpu.CompilerParams(vmem_limit_bytes=32 * mib),
         name="fill",
-    )(tile, *east, *north)
+    )(coded, *north)
 
     totals = lax.all_to_all(totals, "north", split_axis=0, concat_axis=0, tiled=True)
 

time: 89.6 us -> 89.6 us (level)
  transfers between devices with their start and end apart: 5 -> 5, of which waited for: 3 -> 3; matrix products, arithmetic and copies ran while one was open for 0% -> 0% of each run, Pallas kernels for 1% -> 2%
where the time goes in v5:
time: 89.6 us; the launch traced here: 89.3 us
  blocking collectives  42.9 us (48%)
  Pallas kernels  23 us (26%)
  starting transfers between devices  11.4 us (13%)
  waiting for transfers between devices  11.3 us (13%)
    all_to_all x1, blocking collectives, body(): lax.all_to_all(dealt, ('east', 'north'), split_axis=0, concat_axis=0, til...  42.9 us
    pallas_call x1, Pallas kernels, body(): pl.pallas_call(fill_kernel, out_shape=(shape, jax.ShapeDtypeStruct((n_nor...  7.18 us
    pallas_call x1, Pallas kernels, body(): pl.pallas_call(deal_kernel, out_shape=jax.ShapeDtypeStruct((devices, BLOC...  6.5 us
    all_to_all x1, waiting for transfers between devices, body(): lax.all_to_all(totals, 'north', split_axis=0, concat_axis=0, tiled=True)  6.46 us
    all_to_all x1, starting transfers between devices, body(): lax.all_to_all(totals, 'north', split_axis=0, concat_axis=0, tiled=True)  6.28 us
    ppermute x4, starting transfers between devices, swapped(): return lax.ppermute(values, axis, edges + [(j, i) for i, j in edges])  5.1 us
    ppermute x4, waiting for transfers between devices, swapped(): return lax.ppermute(values, axis, edges + [(j, i) for i, j in edges])  4.82 us
    pallas_call x1, Pallas kernels, body(): pl.pallas_call(bin_kernel, out_shape=(jax.ShapeDtypeStruct((tile_rows, ti...  4.53 us
  transfers between devices with their start and end apart: 5, of which 3 were waited for; matrix products, arithmetic and copies ran while one was open for 0% of the time, Pallas kernels for 2%

profile of v5, /device:TPU:2, one launch (start us, length us, event | category | flops | bytes accessed | tf_op | source)
XLA Modules:
  0.0 89.3 jit_solution(11568590294574809549)
XLA Ops:
  0.6 6.5 %deal.1 = bf16[128,72,128]{2,1,0:T(8,128)(2,1)} custom-call(bf16[4096,128]{1,0:T(8,128)(2,1)} %heights_in.1, s32[32,128]{1,0:T(8,128)} %bitcast.2, s32[32,128]{1,0:T(8,128)} %bitcast.3), custom_call_target="tpu_custom_call" | custom-call | tf_op jit(solution)/shard_map/deal/pallas_call | solution.py:405
  7.1 0.0 copy-start
  7.2 42.9 %all_to_all.10.got = bf16[128,72,128]{2,1,0:T(8,128)(2,1)S(1)} all-to-all(bf16[128,72,128]{2,1,0:T(8,128)(2,1)} %deal.1), channel_id=1, replica_groups=mesh['east'=8,'north'=16] {'east','north'}, dimensions={0} | all-to-all | bytes 4718592 | tf_op jit(solution)/shard_map/all_to_all | solution.py:426
  50.0 0.0 copy-done
  50.0 4.5 %bin.1 = (f32[256,512]{1,0:T(8,128)S(1)}, f32[24,512]{1,0:T(8,128)S(1)}, f32[24,512]{1,0:T(8,128)S(1)}) custom-call(bf16[128,72,128]{2,1,0:T(8,128)(2,1)S(1)} %all_to_all.10.got, s32[256,512]{1,0:T(8,128)S(1)} %copy-done), custom_call_target="tpu_custom_call" | custom-call | tf_op jit(solution)/shard_map/bin/pallas_call | solution.py:429
  54.6 0.0 copy-start.1
  54.6 0.0 copy-start.2
  54.6 1.9 %collective-permute-start = (f32[24,512]{1,0:T(8,128)S(1)}, f32[24,512]{1,0:T(8,128)S(1)}, u32[]{:S(2)}, u32[]{:S(2)}) collective-permute-start(f32[24,512]{1,0:T(8,128)S(1)} %get-tuple-element.12), channel_id=1, source_target_pairs={{16,32},{48,64},{80,96},{32,16},{64,48},{96,80},{17,33},{49,65},{8... | collective-permute-start | bytes 147464 | tf_op jit(solution)/shard_map/ppermute | solution.py:392
  56.5 0.4 collective-permute-start.1
  57.0 3.0 %collective-permute-done.east_one.got_one = f32[24,512]{1,0:T(8,128)S(1)} collective-permute-done((f32[24,512]{1,0:T(8,128)S(1)}, f32[24,512]{1,0:T(8,128)S(1)}, u32[]{:S(2)}, u32[]{:S(2)}) %collective-permute-start) | collective-permute-done | bytes 49184 | tf_op jit(solution)/shard_map/ppermute | solution.py:392
  60.0 0.0 collective-permute-done.1.east_two.got_two
  60.0 0.2 sides.1
  60.2 0.7 collective-permute-start.2
  60.9 2.1 %collective-permute-start.3 = (f32[3,24,128]{2,1,0:T(8,128)S(1)}, f32[3,24,128]{2,1,0:T(8,128)S(1)}, u32[]{:S(2)}, u32[]{:S(2)}) collective-permute-start(f32[3,24,128]{2,1,0:T(8,128)S(1)} %get-tuple-element.15), channel_id=1, source_target_pairs={{0,1},{2,3},{4,5},{6,7},{8,9},{10,11},{12,13},{14,15},{1,0},{3,2},... | collective-permute-start | bytes 110600 | tf_op jit(solution)/shard_map/ppermute | solution.py:392
  62.9 0.3 turn.1.coded
  63.3 0.0 collective-permute-done.2.north_one
  63.3 1.8 %collective-permute-done.3.north_two = f32[3,24,128]{2,1,0:T(8,128)S(1)} collective-permute-done((f32[3,24,128]{2,1,0:T(8,128)S(1)}, f32[3,24,128]{2,1,0:T(8,128)S(1)}, u32[]{:S(2)}, u32[]{:S(2)}) %collective-permute-start.3) | collective-permute-done | bytes 36896 | tf_op jit(solution)/shard_map/ppermute | solution.py:392
  65.1 7.2 %fill.1 = (f32[70,3,8,128]{3,2,1,0:T(8,128)S(1)}, f32[16,8,128]{2,1,0:T(8,128)}) custom-call(f32[70,3,8,128]{3,2,1,0:T(8,128)S(1)} %turn.1.coded, f32[3,24,128]{2,1,0:T(8,128)S(1)} %collective-permute-done.2.north_one, f32[3,24,128]{2,1,0:T(8,128)S(1)} %collective-permute-done.3.north_two), custom_call_target="tpu_custom_call" | custom-call | tf_op jit(solution)/shard_map/fill/pallas_call | solution.py:477
  72.3 6.3 %all-to-all-start.1 = ((f32[16,8,128]{2,1,0:T(8,128)}), f32[16,8,128]{2,1,0:T(8,128)S(1)}, u32[]{:S(2)}, u32[]{:S(2)}) async-start(f32[16,8,128]{2,1,0:T(8,128)} %get-tuple-element.19), calls=%async_computation.1 | async-start | bytes 131072 | tf_op jit(solution)/shard_map/all_to_all | solution.py:487
  78.5 1.2 %depth.1 = (f32[256,512]{1,0:T(8,128)}, f32[2,256,512]{2,1,0:T(8,128)S(1)}) custom-call(f32[70,3,8,128]{3,2,1,0:T(8,128)S(1)} %get-tuple-element.16.cells), custom_call_target="tpu_custom_call" | custom-call | flops 402653184 | bytes 2097152 | tf_op jit(solution)/shard_map/depth/pallas_call | solution.py:489
  79.7 6.5 %all-to-all-done.1.totals = f32[16,8,128]{2,1,0:T(8,128)S(1)} async-done(((f32[16,8,128]{2,1,0:T(8,128)}), f32[16,8,128]{2,1,0:T(8,128)S(1)}, u32[]{:S(2)}, u32[]{:S(2)}) %all-to-all-start.1) | async-done | bytes 65568 | tf_op jit(solution)/shard_map/all_to_all | solution.py:487
  86.2 0.0 copy-done.1
  86.2 0.0 copy-done.2
  86.2 3.1 %light.1 = f32[8,256,512]{2,1,0:T(8,128)} custom-call(f32[8]{0:T(128)S(1)} %copy-done.1, s32[8]{0:T(128)S(1)} %copy-done.2, f32[2,256,512]{2,1,0:T(8,128)S(1)} %get-tuple-element.18.depths, f32[16,8,128]{2,1,0:T(8,128)S(1)} %all-to-all-done.1.totals), custom_call_target="tpu_custom_call" | custom-call | tf_op jit(solution)/shard_map/light/pallas_call | solution.py:512
Async XLA Ops:
  7.1 42.9 %copy-start = (s32[256,512]{1,0:T(8,128)S(1)}, s32[256,512]{1,0:T(8,128)}, u32[]{:S(2)}) copy-start(s32[256,512]{1,0:T(8,128)} %gap_mask.1) | copy-start | bytes 1572868
  54.6 31.6 %copy-start.1 = (f32[8]{0:T(128)S(1)}, f32[8]{0:T(128)}, u32[]{:S(2)}) copy-start(f32[8]{0:T(128)} %extinction.1) | copy-start | bytes 100
  54.6 31.6 %copy-start.2 = (s32[8]{0:T(128)S(1)}, s32[8]{0:T(128)}, u32[]{:S(2)}) copy-start(s32[8]{0:T(128)} %side.1) | copy-start | bytes 100
  54.6 5.4 %collective-permute-start = (f32[24,512]{1,0:T(8,128)S(1)}, f32[24,512]{1,0:T(8,128)S(1)}, u32[]{:S(2)}, u32[]{:S(2)}) collective-permute-start(f32[24,512]{1,0:T(8,128)S(1)} %get-tuple-element.12), channel_id=1, source_target_pairs={{16,32},{48,64},{80,96},{32,16},{64,48},{96,80},{17,33},{49,65},{8... | collective-permute-start | bytes 147464 | tf_op jit(solution)/shard_map/ppermute | solution.py:392
  56.5 3.5 %collective-permute-start.1 = (f32[24,512]{1,0:T(8,128)S(1)}, f32[24,512]{1,0:T(8,128)S(1)}, u32[]{:S(2)}, u32[]{:S(2)}) collective-permute-start(f32[24,512]{1,0:T(8,128)S(1)} %get-tuple-element.13), channel_id=1, source_target_pairs={{0,16},{32,48},{64,80},{96,112},{16,0},{48,32},{80,64},{112,96},{1... | collective-permute-start | bytes 147464 | tf_op jit(solution)/shard_map/ppermute | solution.py:392
  60.2 3.1 %collective-permute-start.2 = (f32[3,24,128]{2,1,0:T(8,128)S(1)}, f32[3,24,128]{2,1,0:T(8,128)S(1)}, u32[]{:S(2)}, u32[]{:S(2)}) collective-permute-start(f32[3,24,128]{2,1,0:T(8,128)S(1)} %get-tuple-element.14), channel_id=1, source_target_pairs={{1,2},{3,4},{5,6},{7,8},{9,10},{11,12},{13,14},{2,1},{4,3},{6,5},{... | collective-permute-start | bytes 110600 | tf_op jit(solution)/shard_map/ppermute | solution.py:392
  60.9 4.2 %collective-permute-start.3 = (f32[3,24,128]{2,1,0:T(8,128)S(1)}, f32[3,24,128]{2,1,0:T(8,128)S(1)}, u32[]{:S(2)}, u32[]{:S(2)}) collective-permute-start(f32[3,24,128]{2,1,0:T(8,128)S(1)} %get-tuple-element.15), channel_id=1, source_target_pairs={{0,1},{2,3},{4,5},{6,7},{8,9},{10,11},{12,13},{14,15},{1,0},{3,2},... | collective-permute-start | bytes 110600 | tf_op jit(solution)/shard_map/ppermute | solution.py:392
  72.3 14.0 %all-to-all-start.1 = ((f32[16,8,128]{2,1,0:T(8,128)}), f32[16,8,128]{2,1,0:T(8,128)S(1)}, u32[]{:S(2)}, u32[]{:S(2)}) async-start(f32[16,8,128]{2,1,0:T(8,128)} %get-tuple-element.19), calls=%async_computation.1 | async-start | bytes 131072 | tf_op jit(solution)/shard_map/all_to_all | solution.py:487

commit v6 on v5

--- a/solution.py
+++ b/solution.py
@@ -267,7 +267,7 @@
             coded[v, k] = turned[k, pl.ds(v, 8, stride=deep), :]
 
 
-def fill_kernel(coded, north_one, north_two, cells, totals, halo, keep, rate):
+def fill_kernel(coded, north_one, north_two, filled, totals, halo, cells, rate):
     deep, lanes, _, _ = coded.shape
     long = 8 * deep
     cols = long - 2 * HALO
@@ -284,7 +284,6 @@
                 values = jnp.where(column >= cols, beyond, values)
             unknown = values > 0.5 * GAP
             cells[v, k] = jnp.where(unknown, 0.0, values)
-            keep[v, k] = jnp.where(unknown, 1.0 - 0.9, 1.0)
             rate[v, k] = jnp.where(unknown, 0.9 * 0.25, 0.0)
 
     def step(_, carry):
@@ -300,7 +299,7 @@
             upper = here[1:] + [pltpu.roll(here[0], 127, axis=1)]
             for k in range(lanes):
                 total = (before[k] + after[k]) + (lower[k] + upper[k])
-                cells[v, k] = keep[v, k] * here[k] + rate[v, k] * total
+                cells[v, k] = here[k] + rate[v, k] * (total - 4.0 * here[k])
             before, here = here, after
         return carry
 
@@ -310,6 +309,7 @@
     for v in range(deep):
         inside = iota((8, 128), 0) * deep + v < cols
         for k in range(lanes):
+            filled[v, k] = cells[v, k]
             soft = softplus(cells[v, k])
             sums[k] = sums[k] + (soft if 7 * deep + v < cols else jnp.where(inside, soft, 0.0))
     packed = jnp.zeros((8, 128), F32)

time: 89.6 us -> 88.1 us (0.983)
  Pallas kernels: 23 us -> 21.5 us
    pallas_call x1, Pallas kernels: 7.18 us -> 5.64 us  [body(): pl.pallas_call(fill_kernel, out_shape=(shape, jax.ShapeDtypeStruct((n_nor...]
where the time goes in v6:
time: 88.1 us; the launch traced here: 87.8 us
  blocking collectives  42.9 us (49%)
  Pallas kernels  21.5 us (24%)
  starting transfers between devices  11.4 us (13%)
  waiting for transfers between devices  11.3 us (13%)
    all_to_all x1, blocking collectives, body(): lax.all_to_all(dealt, ('east', 'north'), split_axis=0, concat_axis=0, til...  42.9 us
    pallas_call x1, Pallas kernels, body(): pl.pallas_call(deal_kernel, out_shape=jax.ShapeDtypeStruct((devices, BLOC...  6.5 us
    all_to_all x1, waiting for transfers between devices, body(): lax.all_to_all(totals, 'north', split_axis=0, concat_axis=0, tiled=True)  6.45 us
    all_to_all x1, starting transfers between devices, body(): lax.all_to_all(totals, 'north', split_axis=0, concat_axis=0, tiled=True)  6.28 us
    pallas_call x1, Pallas kernels, body(): pl.pallas_call(fill_kernel, out_shape=(shape, jax.ShapeDtypeStruct((n_nor...  5.64 us
    ppermute x4, starting transfers between devices, swapped(): return lax.ppermute(values, axis, edges + [(j, i) for i, j in edges])  5.1 us
    ppermute x4, waiting for transfers between devices, swapped(): return lax.ppermute(values, axis, edges + [(j, i) for i, j in edges])  4.82 us
    pallas_call x1, Pallas kernels, body(): pl.pallas_call(bin_kernel, out_shape=(jax.ShapeDtypeStruct((tile_rows, ti...  4.53 us
  transfers between devices with their start and end apart: 5, of which 3 were waited for; matrix products, arithmetic and copies ran while one was open for 0% of the time, Pallas kernels for 2%

profile of v6, /device:TPU:2, one launch (start us, length us, event | category | flops | bytes accessed | tf_op | source)
XLA Modules:
  0.0 87.8 jit_solution(17263390050538066997)
XLA Ops:
  0.6 6.5 %deal.1 = bf16[128,72,128]{2,1,0:T(8,128)(2,1)} custom-call(bf16[4096,128]{1,0:T(8,128)(2,1)} %heights_in.1, s32[32,128]{1,0:T(8,128)} %bitcast.2, s32[32,128]{1,0:T(8,128)} %bitcast.3), custom_call_target="tpu_custom_call" | custom-call | tf_op jit(solution)/shard_map/deal/pallas_call | solution.py:405
  7.1 0.0 copy-start
  7.2 42.9 %all_to_all.10.got = bf16[128,72,128]{2,1,0:T(8,128)(2,1)S(1)} all-to-all(bf16[128,72,128]{2,1,0:T(8,128)(2,1)} %deal.1), channel_id=1, replica_groups=mesh['east'=8,'north'=16] {'east','north'}, dimensions={0} | all-to-all | bytes 4718592 | tf_op jit(solution)/shard_map/all_to_all | solution.py:426
  50.0 0.0 copy-done
  50.0 4.5 %bin.1 = (f32[256,512]{1,0:T(8,128)S(1)}, f32[24,512]{1,0:T(8,128)S(1)}, f32[24,512]{1,0:T(8,128)S(1)}) custom-call(bf16[128,72,128]{2,1,0:T(8,128)(2,1)S(1)} %all_to_all.10.got, s32[256,512]{1,0:T(8,128)S(1)} %copy-done), custom_call_target="tpu_custom_call" | custom-call | tf_op jit(solution)/shard_map/bin/pallas_call | solution.py:429
  54.6 0.0 copy-start.1
  54.6 0.0 copy-start.2
  54.6 1.9 %collective-permute-start = (f32[24,512]{1,0:T(8,128)S(1)}, f32[24,512]{1,0:T(8,128)S(1)}, u32[]{:S(2)}, u32[]{:S(2)}) collective-permute-start(f32[24,512]{1,0:T(8,128)S(1)} %get-tuple-element.12), channel_id=1, source_target_pairs={{16,32},{48,64},{80,96},{32,16},{64,48},{96,80},{17,33},{49,65},{8... | collective-permute-start | bytes 147464 | tf_op jit(solution)/shard_map/ppermute | solution.py:392
  56.5 0.4 collective-permute-start.1
  57.0 3.0 %collective-permute-done.east_one.got_one = f32[24,512]{1,0:T(8,128)S(1)} collective-permute-done((f32[24,512]{1,0:T(8,128)S(1)}, f32[24,512]{1,0:T(8,128)S(1)}, u32[]{:S(2)}, u32[]{:S(2)}) %collective-permute-start) | collective-permute-done | bytes 49184 | tf_op jit(solution)/shard_map/ppermute | solution.py:392
  60.0 0.0 collective-permute-done.1.east_two.got_two
  60.0 0.2 sides.1
  60.2 0.7 collective-permute-start.2
  60.9 2.1 %collective-permute-start.3 = (f32[3,24,128]{2,1,0:T(8,128)S(1)}, f32[3,24,128]{2,1,0:T(8,128)S(1)}, u32[]{:S(2)}, u32[]{:S(2)}) collective-permute-start(f32[3,24,128]{2,1,0:T(8,128)S(1)} %get-tuple-element.15), channel_id=1, source_target_pairs={{0,1},{2,3},{4,5},{6,7},{8,9},{10,11},{12,13},{14,15},{1,0},{3,2},... | collective-permute-start | bytes 110600 | tf_op jit(solution)/shard_map/ppermute | solution.py:392
  62.9 0.3 turn.1.coded
  63.3 0.0 collective-permute-done.2.north_one
  63.3 1.8 %collective-permute-done.3.north_two = f32[3,24,128]{2,1,0:T(8,128)S(1)} collective-permute-done((f32[3,24,128]{2,1,0:T(8,128)S(1)}, f32[3,24,128]{2,1,0:T(8,128)S(1)}, u32[]{:S(2)}, u32[]{:S(2)}) %collective-permute-start.3) | collective-permute-done | bytes 36896 | tf_op jit(solution)/shard_map/ppermute | solution.py:392
  65.1 5.6 %fill.1 = (f32[70,3,8,128]{3,2,1,0:T(8,128)S(1)}, f32[16,8,128]{2,1,0:T(8,128)}) custom-call(f32[70,3,8,128]{3,2,1,0:T(8,128)S(1)} %turn.1.coded, f32[3,24,128]{2,1,0:T(8,128)S(1)} %collective-permute-done.2.north_one, f32[3,24,128]{2,1,0:T(8,128)S(1)} %collective-permute-done.3.north_two), custom_call_target="tpu_custom_call" | custom-call | tf_op jit(solution)/shard_map/fill/pallas_call | solution.py:477
  70.7 6.3 %all-to-all-start.1 = ((f32[16,8,128]{2,1,0:T(8,128)}), f32[16,8,128]{2,1,0:T(8,128)S(1)}, u32[]{:S(2)}, u32[]{:S(2)}) async-start(f32[16,8,128]{2,1,0:T(8,128)} %get-tuple-element.19), calls=%async_computation.1 | async-start | bytes 131072 | tf_op jit(solution)/shard_map/all_to_all | solution.py:487
  77.0 1.2 %depth.1 = (f32[256,512]{1,0:T(8,128)}, f32[2,256,512]{2,1,0:T(8,128)S(1)}) custom-call(f32[70,3,8,128]{3,2,1,0:T(8,128)S(1)} %get-tuple-element.16.cells), custom_call_target="tpu_custom_call" | custom-call | flops 402653184 | bytes 2097152 | tf_op jit(solution)/shard_map/depth/pallas_call | solution.py:489
  78.2 6.5 %all-to-all-done.1.totals = f32[16,8,128]{2,1,0:T(8,128)S(1)} async-done(((f32[16,8,128]{2,1,0:T(8,128)}), f32[16,8,128]{2,1,0:T(8,128)S(1)}, u32[]{:S(2)}, u32[]{:S(2)}) %all-to-all-start.1) | async-done | bytes 65568 | tf_op jit(solution)/shard_map/all_to_all | solution.py:487
  84.7 0.0 copy-done.1
  84.7 0.0 copy-done.2
  84.7 3.1 %light.1 = f32[8,256,512]{2,1,0:T(8,128)} custom-call(f32[8]{0:T(128)S(1)} %copy-done.1, s32[8]{0:T(128)S(1)} %copy-done.2, f32[2,256,512]{2,1,0:T(8,128)S(1)} %get-tuple-element.18.depths, f32[16,8,128]{2,1,0:T(8,128)S(1)} %all-to-all-done.1.totals), custom_call_target="tpu_custom_call" | custom-call | tf_op jit(solution)/shard_map/light/pallas_call | solution.py:512
Async XLA Ops:
  7.1 42.9 %copy-start = (s32[256,512]{1,0:T(8,128)S(1)}, s32[256,512]{1,0:T(8,128)}, u32[]{:S(2)}) copy-start(s32[256,512]{1,0:T(8,128)} %gap_mask.1) | copy-start | bytes 1572868
  54.6 30.1 %copy-start.1 = (f32[8]{0:T(128)S(1)}, f32[8]{0:T(128)}, u32[]{:S(2)}) copy-start(f32[8]{0:T(128)} %extinction.1) | copy-start | bytes 100
  54.6 30.1 %copy-start.2 = (s32[8]{0:T(128)S(1)}, s32[8]{0:T(128)}, u32[]{:S(2)}) copy-start(s32[8]{0:T(128)} %side.1) | copy-start | bytes 100
  54.6 5.4 %collective-permute-start = (f32[24,512]{1,0:T(8,128)S(1)}, f32[24,512]{1,0:T(8,128)S(1)}, u32[]{:S(2)}, u32[]{:S(2)}) collective-permute-start(f32[24,512]{1,0:T(8,128)S(1)} %get-tuple-element.12), channel_id=1, source_target_pairs={{16,32},{48,64},{80,96},{32,16},{64,48},{96,80},{17,33},{49,65},{8... | collective-permute-start | bytes 147464 | tf_op jit(solution)/shard_map/ppermute | solution.py:392
  56.5 3.5 %collective-permute-start.1 = (f32[24,512]{1,0:T(8,128)S(1)}, f32[24,512]{1,0:T(8,128)S(1)}, u32[]{:S(2)}, u32[]{:S(2)}) collective-permute-start(f32[24,512]{1,0:T(8,128)S(1)} %get-tuple-element.13), channel_id=1, source_target_pairs={{0,16},{32,48},{64,80},{96,112},{16,0},{48,32},{80,64},{112,96},{1... | collective-permute-start | bytes 147464 | tf_op jit(solution)/shard_map/ppermute | solution.py:392
  60.2 3.1 %collective-permute-start.2 = (f32[3,24,128]{2,1,0:T(8,128)S(1)}, f32[3,24,128]{2,1,0:T(8,128)S(1)}, u32[]{:S(2)}, u32[]{:S(2)}) collective-permute-start(f32[3,24,128]{2,1,0:T(8,128)S(1)} %get-tuple-element.14), channel_id=1, source_target_pairs={{1,2},{3,4},{5,6},{7,8},{9,10},{11,12},{13,14},{2,1},{4,3},{6,5},{... | collective-permute-start | bytes 110600 | tf_op jit(solution)/shard_map/ppermute | solution.py:392
  60.9 4.2 %collective-permute-start.3 = (f32[3,24,128]{2,1,0:T(8,128)S(1)}, f32[3,24,128]{2,1,0:T(8,128)S(1)}, u32[]{:S(2)}, u32[]{:S(2)}) collective-permute-start(f32[3,24,128]{2,1,0:T(8,128)S(1)} %get-tuple-element.15), channel_id=1, source_target_pairs={{0,1},{2,3},{4,5},{6,7},{8,9},{10,11},{12,13},{14,15},{1,0},{3,2},... | collective-permute-start | bytes 110600 | tf_op jit(solution)/shard_map/ppermute | solution.py:392
  70.7 14.0 %all-to-all-start.1 = ((f32[16,8,128]{2,1,0:T(8,128)}), f32[16,8,128]{2,1,0:T(8,128)S(1)}, u32[]{:S(2)}, u32[]{:S(2)}) async-start(f32[16,8,128]{2,1,0:T(8,128)} %get-tuple-element.19), calls=%async_computation.1 | async-start | bytes 131072 | tf_op jit(solution)/shard_map/all_to_all | solution.py:487

commit v7 on v6

--- a/solution.py
+++ b/solution.py
@@ -14,7 +14,6 @@
 GROUP = 64
 TEAM = 8
 DELAY = 2
-PARTS = 4
 PIECES = 1
 
 F32 = jnp.float32
@@ -28,6 +27,10 @@
 
 def hbm():
     return pl.BlockSpec(memory_space=pltpu.HBM)
+
+
+def pinned(values):
+    return pltpu.with_memory_space_constraint(values, pltpu.HBM)
 
 
 def smem():
@@ -61,7 +64,6 @@
     segment,
     wide,
     dealt,
-    packed,
     slots,
     ids,
     slots_s,
@@ -150,19 +152,9 @@
         copy_slots(g).wait()
         place_team(g)
 
-    part = devices // PARTS
-    stores = []
-    for i in range(PARTS):
-
-        @pl.loop(i * part, (i + 1) * part, unroll=4)
-        def _(t):
-            packed[t] = dealt[pl.ds(pl.multiple_of(t * BLOCK, 8), BLOCK), :].astype(BF16)
-
-        at = pl.ds(i * part, part)
-        stores.append(pltpu.make_async_copy(packed.at[at], out.at[at], sems.at[3 + DELAY + i]))
-        stores[-1].start()
-    for store in stores:
-        store.wait()
+    @pl.loop(0, devices, unroll=4)
+    def _(t):
+        out[t] = dealt[pl.ds(pl.multiple_of(t * BLOCK, 8), BLOCK), :].astype(BF16)
 
 
 def bin_kernel(got, gap_mask, out, one, two, acc, codes, lines):
@@ -406,22 +398,21 @@
         deal_kernel,
         out_shape=jax.ShapeDtypeStruct((devices, BLOCK, 128), BF16),
         in_specs=[hbm()] * 3,
-        out_specs=hbm(),
+        out_specs=vmem(),
         scratch_shapes=[
             pltpu.VMEM((rows_here, 128), BF16),
             pltpu.VMEM((chunks, 128), I32),
             pltpu.VMEM((chunks, 128), I32),
             pltpu.VMEM((rows_here, 128), F32),
             pltpu.VMEM((devices * BLOCK, 128), F32),
-            pltpu.VMEM((devices, BLOCK, 128), BF16),
             pltpu.VMEM((chunks // TEAM, 8, 128), I32),
             pltpu.VMEM((devices, 128), F32),
             pltpu.SMEM((chunks // TEAM, 8, 128), I32),
-            pltpu.SemaphoreType.DMA((3 + DELAY + PARTS,)),
+            pltpu.SemaphoreType.DMA((3 + DELAY,)),
         ],
-        compiler_params=pltpu.CompilerParams(vmem_limit_bytes=60 * mib),
+        compiler_params=pltpu.CompilerParams(vmem_limit_bytes=24 * mib),
         name="deal",
-    )(heights, tile_owner.reshape(chunks, 128), segment_ids.reshape(chunks, 128))
+    )(*map(pinned, (heights, tile_owner.reshape(chunks, 128), segment_ids.reshape(chunks, 128))))
 
     got = lax.all_to_all(dealt, ("east", "north"), split_axis=0, concat_axis=0, tiled=True)
 

time: 88.1 us -> 86.7 us (0.984)
  Pallas kernels: 21.5 us -> 20.3 us
    pallas_call x1, Pallas kernels: 6.5 us -> 5.33 us  [body(): pl.pallas_call(deal_kernel, out_shape=jax.ShapeDtypeStruct((devices, BLOC...]
where the time goes in v7:
time: 86.7 us; the launch traced here: 86.4 us
  blocking collectives  42.7 us (49%)
  Pallas kernels  20.3 us (23%)
  starting transfers between devices  11.4 us (13%)
  waiting for transfers between devices  11.3 us (13%)
    all_to_all x1, blocking collectives, body(): lax.all_to_all(dealt, ('east', 'north'), split_axis=0, concat_axis=0, til...  42.7 us
    all_to_all x1, waiting for transfers between devices, body(): lax.all_to_all(totals, 'north', split_axis=0, concat_axis=0, tiled=True)  6.46 us
    all_to_all x1, starting transfers between devices, body(): lax.all_to_all(totals, 'north', split_axis=0, concat_axis=0, tiled=True)  6.28 us
    pallas_call x1, Pallas kernels, body(): pl.pallas_call(fill_kernel, out_shape=(shape, jax.ShapeDtypeStruct((n_nor...  5.64 us
    pallas_call x1, Pallas kernels, body(): pl.pallas_call(deal_kernel, out_shape=jax.ShapeDtypeStruct((devices, BLOC...  5.33 us
    ppermute x4, starting transfers between devices, swapped(): return lax.ppermute(values, axis, edges + [(j, i) for i, j in edges])  5.09 us
    ppermute x4, waiting for transfers between devices, swapped(): return lax.ppermute(values, axis, edges + [(j, i) for i, j in edges])  4.82 us
    pallas_call x1, Pallas kernels, body(): pl.pallas_call(bin_kernel, out_shape=(jax.ShapeDtypeStruct((tile_rows, ti...  4.53 us
  transfers between devices with their start and end apart: 5, of which 3 were waited for; matrix products, arithmetic and copies ran while one was open for 0% of the time, Pallas kernels for 2%

profile of v7, /device:TPU:2, one launch (start us, length us, event | category | flops | bytes accessed | tf_op | source)
XLA Modules:
  0.0 86.4 jit_solution(16652416169000436997)
XLA Ops:
  0.6 5.3 %deal.1 = bf16[128,72,128]{2,1,0:T(8,128)(2,1)S(1)} custom-call(bf16[4096,128]{1,0:T(8,128)(2,1)} %heights_in.1, s32[32,128]{1,0:T(8,128)} %bitcast.2, s32[32,128]{1,0:T(8,128)} %bitcast.3), custom_call_target="tpu_custom_call" | custom-call | tf_op jit(solution)/shard_map/deal/pallas_call | solution.py:397
  6.0 0.0 copy-start
  6.0 42.7 %all_to_all.10.got = bf16[128,72,128]{2,1,0:T(8,128)(2,1)S(1)} all-to-all(bf16[128,72,128]{2,1,0:T(8,128)(2,1)S(1)} %deal.1), channel_id=1, replica_groups=mesh['east'=8,'north'=16] {'east','north'}, dimensions={0} | all-to-all | bytes 4718592 | tf_op jit(solution)/shard_map/all_to_all | solution.py:417
  48.7 0.0 copy-done
  48.7 4.5 %bin.1 = (f32[256,512]{1,0:T(8,128)S(1)}, f32[24,512]{1,0:T(8,128)S(1)}, f32[24,512]{1,0:T(8,128)S(1)}) custom-call(bf16[128,72,128]{2,1,0:T(8,128)(2,1)S(1)} %all_to_all.10.got, s32[256,512]{1,0:T(8,128)S(1)} %copy-done), custom_call_target="tpu_custom_call" | custom-call | tf_op jit(solution)/shard_map/bin/pallas_call | solution.py:420
  53.2 0.0 copy-start.1
  53.2 0.0 copy-start.2
  53.2 1.9 %collective-permute-start = (f32[24,512]{1,0:T(8,128)S(1)}, f32[24,512]{1,0:T(8,128)S(1)}, u32[]{:S(2)}, u32[]{:S(2)}) collective-permute-start(f32[24,512]{1,0:T(8,128)S(1)} %get-tuple-element.12), channel_id=1, source_target_pairs={{16,32},{48,64},{80,96},{32,16},{64,48},{96,80},{17,33},{49,65},{8... | collective-permute-start | bytes 147464 | tf_op jit(solution)/shard_map/ppermute | solution.py:384
  55.2 0.4 collective-permute-start.1
  55.6 3.0 %collective-permute-done.east_one.got_one = f32[24,512]{1,0:T(8,128)S(1)} collective-permute-done((f32[24,512]{1,0:T(8,128)S(1)}, f32[24,512]{1,0:T(8,128)S(1)}, u32[]{:S(2)}, u32[]{:S(2)}) %collective-permute-start) | collective-permute-done | bytes 49184 | tf_op jit(solution)/shard_map/ppermute | solution.py:384
  58.6 0.0 collective-permute-done.1.east_two.got_two
  58.6 0.2 sides.1
  58.8 0.7 collective-permute-start.2
  59.5 2.1 %collective-permute-start.3 = (f32[3,24,128]{2,1,0:T(8,128)S(1)}, f32[3,24,128]{2,1,0:T(8,128)S(1)}, u32[]{:S(2)}, u32[]{:S(2)}) collective-permute-start(f32[3,24,128]{2,1,0:T(8,128)S(1)} %get-tuple-element.15), channel_id=1, source_target_pairs={{0,1},{2,3},{4,5},{6,7},{8,9},{10,11},{12,13},{14,15},{1,0},{3,2},... | collective-permute-start | bytes 110600 | tf_op jit(solution)/shard_map/ppermute | solution.py:384
  61.6 0.3 turn.1.coded
  61.9 0.0 collective-permute-done.2.north_one
  61.9 1.8 %collective-permute-done.3.north_two = f32[3,24,128]{2,1,0:T(8,128)S(1)} collective-permute-done((f32[3,24,128]{2,1,0:T(8,128)S(1)}, f32[3,24,128]{2,1,0:T(8,128)S(1)}, u32[]{:S(2)}, u32[]{:S(2)}) %collective-permute-start.3) | collective-permute-done | bytes 36896 | tf_op jit(solution)/shard_map/ppermute | solution.py:384
  63.7 5.6 %fill.1 = (f32[70,3,8,128]{3,2,1,0:T(8,128)S(1)}, f32[16,8,128]{2,1,0:T(8,128)}) custom-call(f32[70,3,8,128]{3,2,1,0:T(8,128)S(1)} %turn.1.coded, f32[3,24,128]{2,1,0:T(8,128)S(1)} %collective-permute-done.2.north_one, f32[3,24,128]{2,1,0:T(8,128)S(1)} %collective-permute-done.3.north_two), custom_call_target="tpu_custom_call" | custom-call | tf_op jit(solution)/shard_map/fill/pallas_call | solution.py:468
  69.3 6.3 %all-to-all-start.1 = ((f32[16,8,128]{2,1,0:T(8,128)}), f32[16,8,128]{2,1,0:T(8,128)S(1)}, u32[]{:S(2)}, u32[]{:S(2)}) async-start(f32[16,8,128]{2,1,0:T(8,128)} %get-tuple-element.19), calls=%async_computation.1 | async-start | bytes 131072 | tf_op jit(solution)/shard_map/all_to_all | solution.py:478
  75.6 1.2 %depth.1 = (f32[256,512]{1,0:T(8,128)}, f32[2,256,512]{2,1,0:T(8,128)S(1)}) custom-call(f32[70,3,8,128]{3,2,1,0:T(8,128)S(1)} %get-tuple-element.16.cells), custom_call_target="tpu_custom_call" | custom-call | flops 402653184 | bytes 2097152 | tf_op jit(solution)/shard_map/depth/pallas_call | solution.py:480
  76.8 6.5 %all-to-all-done.1.totals = f32[16,8,128]{2,1,0:T(8,128)S(1)} async-done(((f32[16,8,128]{2,1,0:T(8,128)}), f32[16,8,128]{2,1,0:T(8,128)S(1)}, u32[]{:S(2)}, u32[]{:S(2)}) %all-to-all-start.1) | async-done | bytes 65568 | tf_op jit(solution)/shard_map/all_to_all | solution.py:478
  83.3 0.0 copy-done.1
  83.3 0.0 copy-done.2
  83.3 3.1 %light.1 = f32[8,256,512]{2,1,0:T(8,128)} custom-call(f32[8]{0:T(128)S(1)} %copy-done.1, s32[8]{0:T(128)S(1)} %copy-done.2, f32[2,256,512]{2,1,0:T(8,128)S(1)} %get-tuple-element.18.depths, f32[16,8,128]{2,1,0:T(8,128)S(1)} %all-to-all-done.1.totals), custom_call_target="tpu_custom_call" | custom-call | tf_op jit(solution)/shard_map/light/pallas_call | solution.py:503
Async XLA Ops:
  6.0 42.7 %copy-start = (s32[256,512]{1,0:T(8,128)S(1)}, s32[256,512]{1,0:T(8,128)}, u32[]{:S(2)}) copy-start(s32[256,512]{1,0:T(8,128)} %gap_mask.1) | copy-start | bytes 1572868
  53.2 30.1 %copy-start.1 = (f32[8]{0:T(128)S(1)}, f32[8]{0:T(128)}, u32[]{:S(2)}) copy-start(f32[8]{0:T(128)} %extinction.1) | copy-start | bytes 100
  53.2 30.1 %copy-start.2 = (s32[8]{0:T(128)S(1)}, s32[8]{0:T(128)}, u32[]{:S(2)}) copy-start(s32[8]{0:T(128)} %side.1) | copy-start | bytes 100
  53.2 5.4 %collective-permute-start = (f32[24,512]{1,0:T(8,128)S(1)}, f32[24,512]{1,0:T(8,128)S(1)}, u32[]{:S(2)}, u32[]{:S(2)}) collective-permute-start(f32[24,512]{1,0:T(8,128)S(1)} %get-tuple-element.12), channel_id=1, source_target_pairs={{16,32},{48,64},{80,96},{32,16},{64,48},{96,80},{17,33},{49,65},{8... | collective-permute-start | bytes 147464 | tf_op jit(solution)/shard_map/ppermute | solution.py:384
  55.2 3.5 %collective-permute-start.1 = (f32[24,512]{1,0:T(8,128)S(1)}, f32[24,512]{1,0:T(8,128)S(1)}, u32[]{:S(2)}, u32[]{:S(2)}) collective-permute-start(f32[24,512]{1,0:T(8,128)S(1)} %get-tuple-element.13), channel_id=1, source_target_pairs={{0,16},{32,48},{64,80},{96,112},{16,0},{48,32},{80,64},{112,96},{1... | collective-permute-start | bytes 147464 | tf_op jit(solution)/shard_map/ppermute | solution.py:384
  58.8 3.1 %collective-permute-start.2 = (f32[3,24,128]{2,1,0:T(8,128)S(1)}, f32[3,24,128]{2,1,0:T(8,128)S(1)}, u32[]{:S(2)}, u32[]{:S(2)}) collective-permute-start(f32[3,24,128]{2,1,0:T(8,128)S(1)} %get-tuple-element.14), channel_id=1, source_target_pairs={{1,2},{3,4},{5,6},{7,8},{9,10},{11,12},{13,14},{2,1},{4,3},{6,5},{... | collective-permute-start | bytes 110600 | tf_op jit(solution)/shard_map/ppermute | solution.py:384
  59.5 4.2 %collective-permute-start.3 = (f32[3,24,128]{2,1,0:T(8,128)S(1)}, f32[3,24,128]{2,1,0:T(8,128)S(1)}, u32[]{:S(2)}, u32[]{:S(2)}) collective-permute-start(f32[3,24,128]{2,1,0:T(8,128)S(1)} %get-tuple-element.15), channel_id=1, source_target_pairs={{0,1},{2,3},{4,5},{6,7},{8,9},{10,11},{12,13},{14,15},{1,0},{3,2},... | collective-permute-start | bytes 110600 | tf_op jit(solution)/shard_map/ppermute | solution.py:384
  69.3 14.0 %all-to-all-start.1 = ((f32[16,8,128]{2,1,0:T(8,128)}), f32[16,8,128]{2,1,0:T(8,128)S(1)}, u32[]{:S(2)}, u32[]{:S(2)}) async-start(f32[16,8,128]{2,1,0:T(8,128)} %get-tuple-element.19), calls=%async_computation.1 | async-start | bytes 131072 | tf_op jit(solution)/shard_map/all_to_all | solution.py:478

commit v8 on v7

--- a/solution.py
+++ b/solution.py
@@ -83,7 +83,7 @@
         load.start()
     zeros = jnp.zeros((BLOCK, 128), F32)
 
-    @pl.loop(0, devices, unroll=4)
+    @pl.loop(0, devices, unroll=8)
     def _(t):
         dealt[pl.ds(pl.multiple_of(t * BLOCK, 8), BLOCK), :] = zeros
 
@@ -129,7 +129,7 @@
         copy_slots(g).start()
     loads[2].wait()
 
-    @pl.loop(0, rows // 64, unroll=4)
+    @pl.loop(0, rows // 64, unroll=8)
     def _(c):
         at = pl.ds(pl.multiple_of(c * 64, 64), 64)
         wide[at, :] = heights[at, :].astype(F32)
@@ -152,7 +152,7 @@
         copy_slots(g).wait()
         place_team(g)
 
-    @pl.loop(0, devices, unroll=4)
+    @pl.loop(0, devices, unroll=8)
     def _(t):
         out[t] = dealt[pl.ds(pl.multiple_of(t * BLOCK, 8), BLOCK), :].astype(BF16)
 
@@ -295,7 +295,7 @@
             before, here = here, after
         return carry
 
-    lax.fori_loop(0, STEPS, step, 0, unroll=2)
+    lax.fori_loop(0, STEPS, step, 0, unroll=4)
 
     sums = [jnp.zeros((8, 128), F32) for _ in range(lanes)]
     for v in range(deep):

time: 86.7 us -> 86.3 us (level)
  no operation moved by 1% of the time
where the time goes in v8:
time: 86.3 us; the launch traced here: 86 us
  blocking collectives  42.7 us (49%)
  Pallas kernels  19.9 us (23%)
  starting transfers between devices  11.4 us (13%)
  waiting for transfers between devices  11.3 us (13%)
    all_to_all x1, blocking collectives, body(): lax.all_to_all(dealt, ('east', 'north'), split_axis=0, concat_axis=0, til...  42.7 us
    all_to_all x1, waiting for transfers between devices, body(): lax.all_to_all(totals, 'north', split_axis=0, concat_axis=0, tiled=True)  6.46 us
    all_to_all x1, starting transfers between devices, body(): lax.all_to_all(totals, 'north', split_axis=0, concat_axis=0, tiled=True)  6.28 us
    pallas_call x1, Pallas kernels, body(): pl.pallas_call(fill_kernel, out_shape=(shape, jax.ShapeDtypeStruct((n_nor...  5.31 us
    pallas_call x1, Pallas kernels, body(): pl.pallas_call(deal_kernel, out_shape=jax.ShapeDtypeStruct((devices, BLOC...  5.24 us
    ppermute x4, starting transfers between devices, swapped(): return lax.ppermute(values, axis, edges + [(j, i) for i, j in edges])  5.09 us
    ppermute x4, waiting for transfers between devices, swapped(): return lax.ppermute(values, axis, edges + [(j, i) for i, j in edges])  4.82 us
    pallas_call x1, Pallas kernels, body(): pl.pallas_call(bin_kernel, out_shape=(jax.ShapeDtypeStruct((tile_rows, ti...  4.53 us
  transfers between devices with their start and end apart: 5, of which 3 were waited for; matrix products, arithmetic and copies ran while one was open for 0% of the time, Pallas kernels for 2%

profile of v8, /device:TPU:2, one launch (start us, length us, event | category | flops | bytes accessed | tf_op | source)
XLA Modules:
  0.0 86.0 jit_solution(14623986382299185672)
XLA Ops:
  0.6 5.2 %deal.1 = bf16[128,72,128]{2,1,0:T(8,128)(2,1)S(1)} custom-call(bf16[4096,128]{1,0:T(8,128)(2,1)} %heights_in.1, s32[32,128]{1,0:T(8,128)} %bitcast.2, s32[32,128]{1,0:T(8,128)} %bitcast.3), custom_call_target="tpu_custom_call" | custom-call | tf_op jit(solution)/shard_map/deal/pallas_call | solution.py:397
  5.9 0.0 copy-start
  5.9 42.7 %all_to_all.10.got = bf16[128,72,128]{2,1,0:T(8,128)(2,1)S(1)} all-to-all(bf16[128,72,128]{2,1,0:T(8,128)(2,1)S(1)} %deal.1), channel_id=1, replica_groups=mesh['east'=8,'north'=16] {'east','north'}, dimensions={0} | all-to-all | bytes 4718592 | tf_op jit(solution)/shard_map/all_to_all | solution.py:417
  48.6 0.0 copy-done
  48.6 4.5 %bin.1 = (f32[256,512]{1,0:T(8,128)S(1)}, f32[24,512]{1,0:T(8,128)S(1)}, f32[24,512]{1,0:T(8,128)S(1)}) custom-call(bf16[128,72,128]{2,1,0:T(8,128)(2,1)S(1)} %all_to_all.10.got, s32[256,512]{1,0:T(8,128)S(1)} %copy-done), custom_call_target="tpu_custom_call" | custom-call | tf_op jit(solution)/shard_map/bin/pallas_call | solution.py:420
  53.1 0.0 copy-start.1
  53.1 0.0 copy-start.2
  53.1 1.9 %collective-permute-start = (f32[24,512]{1,0:T(8,128)S(1)}, f32[24,512]{1,0:T(8,128)S(1)}, u32[]{:S(2)}, u32[]{:S(2)}) collective-permute-start(f32[24,512]{1,0:T(8,128)S(1)} %get-tuple-element.12), channel_id=1, source_target_pairs={{16,32},{48,64},{80,96},{32,16},{64,48},{96,80},{17,33},{49,65},{8... | collective-permute-start | bytes 147464 | tf_op jit(solution)/shard_map/ppermute | solution.py:384
  55.1 0.4 collective-permute-start.1
  55.5 3.0 %collective-permute-done.east_one.got_one = f32[24,512]{1,0:T(8,128)S(1)} collective-permute-done((f32[24,512]{1,0:T(8,128)S(1)}, f32[24,512]{1,0:T(8,128)S(1)}, u32[]{:S(2)}, u32[]{:S(2)}) %collective-permute-start) | collective-permute-done | bytes 49184 | tf_op jit(solution)/shard_map/ppermute | solution.py:384
  58.5 0.0 collective-permute-done.1.east_two.got_two
  58.6 0.2 sides.1
  58.7 0.7 collective-permute-start.2
  59.4 2.1 %collective-permute-start.3 = (f32[3,24,128]{2,1,0:T(8,128)S(1)}, f32[3,24,128]{2,1,0:T(8,128)S(1)}, u32[]{:S(2)}, u32[]{:S(2)}) collective-permute-start(f32[3,24,128]{2,1,0:T(8,128)S(1)} %get-tuple-element.15), channel_id=1, source_target_pairs={{0,1},{2,3},{4,5},{6,7},{8,9},{10,11},{12,13},{14,15},{1,0},{3,2},... | collective-permute-start | bytes 110600 | tf_op jit(solution)/shard_map/ppermute | solution.py:384
  61.5 0.3 turn.1.coded
  61.8 0.0 collective-permute-done.2.north_one
  61.8 1.8 %collective-permute-done.3.north_two = f32[3,24,128]{2,1,0:T(8,128)S(1)} collective-permute-done((f32[3,24,128]{2,1,0:T(8,128)S(1)}, f32[3,24,128]{2,1,0:T(8,128)S(1)}, u32[]{:S(2)}, u32[]{:S(2)}) %collective-permute-start.3) | collective-permute-done | bytes 36896 | tf_op jit(solution)/shard_map/ppermute | solution.py:384
  63.6 5.3 %fill.1 = (f32[70,3,8,128]{3,2,1,0:T(8,128)S(1)}, f32[16,8,128]{2,1,0:T(8,128)}) custom-call(f32[70,3,8,128]{3,2,1,0:T(8,128)S(1)} %turn.1.coded, f32[3,24,128]{2,1,0:T(8,128)S(1)} %collective-permute-done.2.north_one, f32[3,24,128]{2,1,0:T(8,128)S(1)} %collective-permute-done.3.north_two), custom_call_target="tpu_custom_call" | custom-call | tf_op jit(solution)/shard_map/fill/pallas_call | solution.py:468
  68.9 6.3 %all-to-all-start.1 = ((f32[16,8,128]{2,1,0:T(8,128)}), f32[16,8,128]{2,1,0:T(8,128)S(1)}, u32[]{:S(2)}, u32[]{:S(2)}) async-start(f32[16,8,128]{2,1,0:T(8,128)} %get-tuple-element.19), calls=%async_computation.1 | async-start | bytes 131072 | tf_op jit(solution)/shard_map/all_to_all | solution.py:478
  75.2 1.2 %depth.1 = (f32[256,512]{1,0:T(8,128)}, f32[2,256,512]{2,1,0:T(8,128)S(1)}) custom-call(f32[70,3,8,128]{3,2,1,0:T(8,128)S(1)} %get-tuple-element.16.cells), custom_call_target="tpu_custom_call" | custom-call | flops 402653184 | bytes 2097152 | tf_op jit(solution)/shard_map/depth/pallas_call | solution.py:480
  76.4 6.5 %all-to-all-done.1.totals = f32[16,8,128]{2,1,0:T(8,128)S(1)} async-done(((f32[16,8,128]{2,1,0:T(8,128)}), f32[16,8,128]{2,1,0:T(8,128)S(1)}, u32[]{:S(2)}, u32[]{:S(2)}) %all-to-all-start.1) | async-done | bytes 65568 | tf_op jit(solution)/shard_map/all_to_all | solution.py:478
  82.9 0.0 copy-done.1
  82.9 0.0 copy-done.2
  82.9 3.1 %light.1 = f32[8,256,512]{2,1,0:T(8,128)} custom-call(f32[8]{0:T(128)S(1)} %copy-done.1, s32[8]{0:T(128)S(1)} %copy-done.2, f32[2,256,512]{2,1,0:T(8,128)S(1)} %get-tuple-element.18.depths, f32[16,8,128]{2,1,0:T(8,128)S(1)} %all-to-all-done.1.totals), custom_call_target="tpu_custom_call" | custom-call | tf_op jit(solution)/shard_map/light/pallas_call | solution.py:503
Async XLA Ops:
  5.9 42.7 %copy-start = (s32[256,512]{1,0:T(8,128)S(1)}, s32[256,512]{1,0:T(8,128)}, u32[]{:S(2)}) copy-start(s32[256,512]{1,0:T(8,128)} %gap_mask.1) | copy-start | bytes 1572868
  53.1 29.7 %copy-start.1 = (f32[8]{0:T(128)S(1)}, f32[8]{0:T(128)}, u32[]{:S(2)}) copy-start(f32[8]{0:T(128)} %extinction.1) | copy-start | bytes 100
  53.1 29.7 %copy-start.2 = (s32[8]{0:T(128)S(1)}, s32[8]{0:T(128)}, u32[]{:S(2)}) copy-start(s32[8]{0:T(128)} %side.1) | copy-start | bytes 100
  53.1 5.4 %collective-permute-start = (f32[24,512]{1,0:T(8,128)S(1)}, f32[24,512]{1,0:T(8,128)S(1)}, u32[]{:S(2)}, u32[]{:S(2)}) collective-permute-start(f32[24,512]{1,0:T(8,128)S(1)} %get-tuple-element.12), channel_id=1, source_target_pairs={{16,32},{48,64},{80,96},{32,16},{64,48},{96,80},{17,33},{49,65},{8... | collective-permute-start | bytes 147464 | tf_op jit(solution)/shard_map/ppermute | solution.py:384
  55.1 3.5 %collective-permute-start.1 = (f32[24,512]{1,0:T(8,128)S(1)}, f32[24,512]{1,0:T(8,128)S(1)}, u32[]{:S(2)}, u32[]{:S(2)}) collective-permute-start(f32[24,512]{1,0:T(8,128)S(1)} %get-tuple-element.13), channel_id=1, source_target_pairs={{0,16},{32,48},{64,80},{96,112},{16,0},{48,32},{80,64},{112,96},{1... | collective-permute-start | bytes 147464 | tf_op jit(solution)/shard_map/ppermute | solution.py:384
  58.7 3.1 %collective-permute-start.2 = (f32[3,24,128]{2,1,0:T(8,128)S(1)}, f32[3,24,128]{2,1,0:T(8,128)S(1)}, u32[]{:S(2)}, u32[]{:S(2)}) collective-permute-start(f32[3,24,128]{2,1,0:T(8,128)S(1)} %get-tuple-element.14), channel_id=1, source_target_pairs={{1,2},{3,4},{5,6},{7,8},{9,10},{11,12},{13,14},{2,1},{4,3},{6,5},{... | collective-permute-start | bytes 110600 | tf_op jit(solution)/shard_map/ppermute | solution.py:384
  59.4 4.2 %collective-permute-start.3 = (f32[3,24,128]{2,1,0:T(8,128)S(1)}, f32[3,24,128]{2,1,0:T(8,128)S(1)}, u32[]{:S(2)}, u32[]{:S(2)}) collective-permute-start(f32[3,24,128]{2,1,0:T(8,128)S(1)} %get-tuple-element.15), channel_id=1, source_target_pairs={{0,1},{2,3},{4,5},{6,7},{8,9},{10,11},{12,13},{14,15},{1,0},{3,2},... | collective-permute-start | bytes 110600 | tf_op jit(solution)/shard_map/ppermute | solution.py:384
  68.9 14.0 %all-to-all-start.1 = ((f32[16,8,128]{2,1,0:T(8,128)}), f32[16,8,128]{2,1,0:T(8,128)S(1)}, u32[]{:S(2)}, u32[]{:S(2)}) async-start(f32[16,8,128]{2,1,0:T(8,128)} %get-tuple-element.19), calls=%async_computation.1 | async-start | bytes 131072 | tf_op jit(solution)/shard_map/all_to_all | solution.py:478
